TPU v7x, 256 devices: a whole 4x4x8 slice. The times are simulated.
256 devices in a mesh: gx: 4 (over x_hi, core), gy: 8 (over z), sa: 8 (over x_lo, y).
Axes of the slice: x: 4 (x_hi: 2, x_lo: 2; x = x_hi * 2 + x_lo), y: 4, z: 8, core: 2. Of those that a mesh axis runs over, the one named last changes fastest.
Arguments:
- green: bfloat16 [8, 16, 2, 2, 2048, 256], P('gx', 'gy', None, None, 'sa'), may hold values from -0.59765625 to 0.59765625
- offsets: int32 [4, 2], replicated, may hold values from -1 to 1, as said below
Outputs:
- hessian: float32 [8, 16, 4, 2, 256, 512], P('gx', 'gy', None, None, 'sa')
Inputs may be any that keep to these rules, and one draw needn't show every extreme that they name: `offsets`: each row is an offset (dx, dy) within 1 tiles with dx >= 0, and dy >= 0 where dx = 0; rows are distinct; (1, -1) and (1, 1) are always among them.
All inputs are finite; a program needn't handle non-finite values.
Results may differ from a plain program's by a relative error of at most 0.0003.
Values may be sent and summed in bfloat16 or wider, within the bound.
No kernel may reach another device: no remote copies, remote signals or barrier semaphores. Data moves between devices by JAX's collectives and lax.ppermute only.
A program may use at most 128 MiB of HBM per device.

v0:
```python
import jax
import jax.numpy as jnp
from jax import lax
from jax.sharding import PartitionSpec as P

NPAIR = 4


def from_behind(value, axis, steps):
    count = lax.axis_size(axis)
    initial, last = (max(0, -steps), min(count, count - steps))
    return lax.ppermute(value, axis, [(source, source + steps) for source in range(initial, last)])


def with_halo(shard, sides, width):
    for axis, dim in sides:
        size, length = (lax.axis_size(axis), shard.shape[dim])
        up = [(i, (i + 1) % size) for i in range(size - 1)]
        down = [(j, i) for i, j in up]
        last = lax.slice_in_dim(shard, length - width, length, axis=dim)
        initial = lax.slice_in_dim(shard, 0, width, axis=dim)
        before = lax.ppermute(last, axis, up)
        after = lax.ppermute(initial, axis, down)
        shard = jnp.concatenate([before, shard, after], axis=dim)
    return shard


def per_device(green, offsets):
    tiles_x = green.shape[0]
    tiles_y = green.shape[1]
    frequencies = green.shape[2]
    traces = green.shape[4]
    points = green.shape[5]
    following = from_behind(green[:1], "gx", -1)
    longer = jnp.concatenate([green, following], axis=0)
    widened = with_halo(longer, (("gy", 1),), 1)
    count = tiles_x * tiles_y * frequencies
    left = green.reshape(count, 2 * traces, points)
    zero = jnp.int32(0)

    def pair_term(index):
        start_x = offsets[index, 0]
        start_y = 1 + offsets[index, 1]
        beside = lax.dynamic_slice(widened, (start_x, start_y, zero, zero, zero, zero), green.shape)
        real_rows = beside.reshape(count, 2 * traces, points)
        imag_rows = jnp.concatenate([beside[:, :, :, 1], -beside[:, :, :, 0]], axis=3).reshape(
            count, 2 * traces, points
        )
        right = jnp.concatenate([real_rows, imag_rows], axis=2)
        block = jnp.einsum("nsp,nsq->npq", left, right, preferred_element_type=jnp.float32)
        return block.reshape(tiles_x, tiles_y, frequencies, points, 2 * points)

    terms = jnp.stack([pair_term(index) for index in range(NPAIR)], axis=2)
    return lax.psum_scatter(terms, "sa", scatter_dimension=4, tiled=True)


def solution(mesh):
    return jax.shard_map(
        per_device,
        mesh=mesh,
        in_specs=(P("gx", "gy", None, None, "sa", None), P()),
        out_specs=P("gx", "gy", None, None, "sa", None),
        check_vma=False,
    )
```

profile of v0, /device:TPU:100, one launch (start us, length us, event | category | flops | bytes accessed | tf_op | source)
XLA Modules:
  0.0 335.0 jit_solution(16009274254702204643)
XLA Ops:
  6.5 0.0 reduce-scatter.2.cloned.1.call-start
  6.5 1.3 slice.57
  7.8 1.9 collective-permute-start
  9.8 1.7 constant_dynamic-update-slice_fusion.1
  11.5 0.0 copy-start.4
  11.5 10.6 %collective-permute-done = bf16[1,2,2,2,256,256]{5,4,3,2,1,0:T(8,128)(2,1)S(1)} collective-permute-done((bf16[1,2,2,2,256,256]{5,4,3,2,1,0:T(8,128)(2,1)S(1)}, bf16[1,2,2,2,256,256]{5,4,3,2,1,0:T(8,128)(2,1)S(1)}, u32[]{:S(2)}, u32[]{:S(2)}) %collective-permute-start) | collective-permute-done | bytes 1048608 | tf_op jit(solution)/shard_map/ppermute | solution.py:12
  22.1 0.1 constant_dynamic-update-slice_fusion
  22.1 1.9 fusion.28
  24.0 5.0 %collective-permute-start.1 = (bf16[3,1,2,2,256,256]{5,4,3,2,1,0:T(8,128)(2,1)}, bf16[3,1,2,2,256,256]{5,4,3,2,1,0:T(8,128)(2,1)}, u32[]{:S(2)}, u32[]{:S(2)}) collective-permute-start(bf16[3,1,2,2,256,256]{5,4,3,2,1,0:T(8,128)(2,1)} %get-tuple-element.17), channel_id=1, source_target_pairs={{0,8},{8,16},{16,24},{24,32},{32,40},{40,48},{48,56},{1,9},{9,17},... | collective-permute-start | bytes 4718600 | tf_op jit(solution)/shard_map/ppermute | solution.py:22
  29.1 1.9 collective-permute-start.2
  31.0 0.0 copy-done.4
  31.0 0.7 fusion.29
  44.2 9.5 %collective-permute-done.1 = bf16[3,1,2,2,256,256]{5,4,3,2,1,0:T(8,128)(2,1)} collective-permute-done((bf16[3,1,2,2,256,256]{5,4,3,2,1,0:T(8,128)(2,1)}, bf16[3,1,2,2,256,256]{5,4,3,2,1,0:T(8,128)(2,1)}, u32[]{:S(2)}, u32[]{:S(2)}) %collective-permute-start.1) | collective-permute-done | bytes 1572896 | tf_op jit(solution)/shard_map/ppermute | solution.py:22
  53.6 5.3 %collective-permute-done.2 = bf16[3,1,2,2,256,256]{5,4,3,2,1,0:T(8,128)(2,1)} collective-permute-done((bf16[3,1,2,2,256,256]{5,4,3,2,1,0:T(8,128)(2,1)}, bf16[3,1,2,2,256,256]{5,4,3,2,1,0:T(8,128)(2,1)}, u32[]{:S(2)}, u32[]{:S(2)}) %collective-permute-start.2) | collective-permute-done | bytes 1572896 | tf_op jit(solution)/shard_map/ppermute | solution.py:23
  59.0 2.9 pad_maximum_fusion.1
  61.9 2.9 constant_dynamic-slice_fusion.7
  64.8 3.0 constant_dynamic-slice_fusion.3
  67.8 2.3 copy.4
  70.0 2.3 copy.14
  72.3 2.3 copy.13
  74.6 2.3 copy.11
  76.9 2.3 copy.10
  79.2 2.3 copy.8
  81.4 2.3 copy.7
  83.7 1.3 copy.5
  85.0 0.0 copy-start.3
  85.0 4.0 %copy.19 = bf16[8,512,256]{1,2,0:T(8,128)(2,1)} copy(bf16[8,512,256]{2,1,0:T(8,128)(2,1)} %bitcast.44) | data formatting | bytes 4194304 | tf_op jit(solution)/shard_map/reshape | solution.py:45
  89.0 0.0 copy-done.3
  89.0 5.8 %fusion = f32[8,512,256]{2,1,0:T(8,128)} fusion(bf16[8,512,256]{2,1,0:T(8,128)(2,1)} %bitcast.45, bf16[8,256,256]{1,2,0:T(8,128)(2,1)} %bitcast.60, bf16[8,256,256]{1,2,0:T(8,128)(2,1)S(1)} %bitcast.59, bf16[8,512,256]{1,2,0:T(8,128)(2,1)} %copy.19), kind=kOutput, calls=%fused_computation.2 | convolution fusion | flops 1086324736 | bytes 10485760 | tf_op jit(solution)/shard_map/nsp,nsq->npq/dot_general | solution.py:50
  94.8 5.3 %copy.15 = f32[2,2,1,2,256,512]{5,4,3,2,1,0:T(8,128)} copy(f32[2,2,1,2,256,512]{4,5,3,1,0,2:T(8,128)} %bitcast.49) | data formatting | bytes 8388608 | tf_op jit(solution)/shard_map/stack;reshape | solution.py:53
  100.0 0.0 copy-start.2
  100.0 4.0 %copy.22 = bf16[8,512,256]{1,2,0:T(8,128)(2,1)} copy(bf16[8,512,256]{2,1,0:T(8,128)(2,1)} %bitcast.43) | data formatting | bytes 4194304 | tf_op jit(solution)/shard_map/reshape | solution.py:45
  104.0 0.0 copy-done.2
  104.0 5.8 %fusion.18 = f32[8,512,256]{2,1,0:T(8,128)} fusion(bf16[8,512,256]{2,1,0:T(8,128)(2,1)} %bitcast.46, bf16[8,256,256]{1,2,0:T(8,128)(2,1)S(1)} %bitcast.57, bf16[8,256,256]{1,2,0:T(8,128)(2,1)} %bitcast.58, bf16[8,512,256]{1,2,0:T(8,128)(2,1)} %copy.22), kind=kOutput, calls=%fused_computation.20 | convolution fusion | flops 1086324736 | bytes 10485760 | tf_op jit(solution)/shard_map/nsp,nsq->npq/dot_general | solution.py:50
  109.8 5.3 %copy.18 = f32[2,2,1,2,256,512]{5,4,3,2,1,0:T(8,128)} copy(f32[2,2,1,2,256,512]{4,5,3,1,0,2:T(8,128)} %bitcast.50) | data formatting | bytes 8388608 | tf_op jit(solution)/shard_map/stack;reshape | solution.py:53
  115.0 0.0 copy-start.1
  115.0 4.0 %copy.21 = bf16[8,512,256]{1,2,0:T(8,128)(2,1)} copy(bf16[8,512,256]{2,1,0:T(8,128)(2,1)} %bitcast.42) | data formatting | bytes 4194304 | tf_op jit(solution)/shard_map/reshape | solution.py:45
  119.1 0.0 copy-done.1
  119.1 5.8 %fusion.12 = f32[8,512,256]{2,1,0:T(8,128)} fusion(bf16[8,512,256]{2,1,0:T(8,128)(2,1)} %bitcast.47, bf16[8,256,256]{1,2,0:T(8,128)(2,1)S(1)} %bitcast.55, bf16[8,256,256]{1,2,0:T(8,128)(2,1)} %bitcast.56, bf16[8,512,256]{1,2,0:T(8,128)(2,1)} %copy.21), kind=kOutput, calls=%fused_computation.14 | convolution fusion | flops 1086324736 | bytes 10485760 | tf_op jit(solution)/shard_map/nsp,nsq->npq/dot_general | solution.py:50
  124.8 5.3 %copy.17 = f32[2,2,1,2,256,512]{5,4,3,2,1,0:T(8,128)} copy(f32[2,2,1,2,256,512]{4,5,3,1,0,2:T(8,128)} %bitcast.51) | data formatting | bytes 8388608 | tf_op jit(solution)/shard_map/stack;reshape | solution.py:53
  130.1 0.0 copy-start
  130.1 2.4 copy.20
  132.5 0.0 copy-done
  132.5 5.8 %fusion.6 = f32[8,512,256]{2,1,0:T(8,128)} fusion(bf16[8,512,256]{2,1,0:T(8,128)(2,1)} %bitcast.48, bf16[8,256,256]{1,2,0:T(8,128)(2,1)S(1)} %bitcast.53, bf16[8,256,256]{1,2,0:T(8,128)(2,1)} %bitcast.54, bf16[8,512,256]{1,2,0:T(8,128)(2,1)} %copy.20), kind=kOutput, calls=%fused_computation.8 | convolution fusion | flops 1086324736 | bytes 10485760 | tf_op jit(solution)/shard_map/nsp,nsq->npq/dot_general | solution.py:50
  138.2 5.3 %copy.16 = f32[2,2,1,2,256,512]{5,4,3,2,1,0:T(8,128)} copy(f32[2,2,1,2,256,512]{4,5,3,1,0,2:T(8,128)} %bitcast.52) | data formatting | bytes 8388608 | tf_op jit(solution)/shard_map/stack;reshape | solution.py:53
  143.5 11.6 %pad_maximum_fusion = f32[2,2,4,2,256,512]{5,4,3,2,1,0:T(8,128)} fusion(f32[2,2,1,2,256,512]{5,4,3,2,1,0:T(8,128)} %copy.18, f32[2,2,1,2,256,512]{5,4,3,2,1,0:T(8,128)} %copy.17, f32[2,2,1,2,256,512]{5,4,3,2,1,0:T(8,128)} %copy.16, f32[2,2,1,2,256,512]{5,4,3,2,1,0:T(8,128)} %copy.15), kind=kLoop, calls=%fused_computation | loop fusion | flops 12582912 | bytes 33554432 | tf_op jit(solution)/shard_map/stack | solution.py:53
  155.1 0.0 reduce-scatter.2.cloned.1.call-update
  155.1 173.0 %reduce-scatter.2.cloned.1.call-done = f32[2,2,4,2,32,512]{5,4,3,2,1,0:T(8,128)} async-done(((f32[2,2,4,2,256,512]{5,4,3,2,1,0:T(8,128)}), f32[2,2,4,2,32,512]{5,4,3,2,1,0:T(8,128)}) %reduce-scatter.2.cloned.1.call-update) | async-done | bytes 2097168 | tf_op jit(solution)/shard_map/reduce_scatter | solution.py:54
Async XLA Ops:
  6.5 321.6 %reduce-scatter.2.cloned.1.call-start = ((), (), s32[]{:S(2)}) async-start(), calls=%async_computation.1 | async-start | bytes 18874368 | tf_op jit(solution)/shard_map/reduce_scatter | solution.py:54
  7.8 14.2 %collective-permute-start = (bf16[1,2,2,2,256,256]{5,4,3,2,1,0:T(8,128)(2,1)S(1)}, bf16[1,2,2,2,256,256]{5,4,3,2,1,0:T(8,128)(2,1)S(1)}, u32[]{:S(2)}, u32[]{:S(2)}) collective-permute-start(bf16[1,2,2,2,256,256]{5,4,3,2,1,0:T(8,128)(2,1)S(1)} %slice.57), channel_id=1, source_target_pairs={{64,0},{128,64},{192,128},{65,1},{129,65},{193,129},{66,2},{130,66... | collective-permute-start | bytes 3145736 | tf_op jit(solution)/shard_map/ppermute | solution.py:12
  11.5 19.5 %copy-start.4 = (s32[4,2]{0,1:T(2,128)S(1)}, s32[4,2]{0,1:T(2,128)}, u32[]{:S(2)}) copy-start(s32[4,2]{0,1:T(2,128)} %param.3) | copy-start | bytes 100
  24.0 29.6 %collective-permute-start.1 = (bf16[3,1,2,2,256,256]{5,4,3,2,1,0:T(8,128)(2,1)}, bf16[3,1,2,2,256,256]{5,4,3,2,1,0:T(8,128)(2,1)}, u32[]{:S(2)}, u32[]{:S(2)}) collective-permute-start(bf16[3,1,2,2,256,256]{5,4,3,2,1,0:T(8,128)(2,1)} %get-tuple-element.17), channel_id=1, source_target_pairs={{0,8},{8,16},{16,24},{24,32},{32,40},{40,48},{48,56},{1,9},{9,17},... | collective-permute-start | bytes 4718600 | tf_op jit(solution)/shard_map/ppermute | solution.py:22
  29.1 29.9 %collective-permute-start.2 = (bf16[3,1,2,2,256,256]{5,4,3,2,1,0:T(8,128)(2,1)}, bf16[3,1,2,2,256,256]{5,4,3,2,1,0:T(8,128)(2,1)}, u32[]{:S(2)}, u32[]{:S(2)}) collective-permute-start(bf16[3,1,2,2,256,256]{5,4,3,2,1,0:T(8,128)(2,1)} %get-tuple-element.18), channel_id=1, source_target_pairs={{8,0},{16,8},{24,16},{32,24},{40,32},{48,40},{56,48},{9,1},{17,9},... | collective-permute-start | bytes 4718600 | tf_op jit(solution)/shard_map/ppermute | solution.py:23
  85.0 4.0 %copy-start.3 = (bf16[2,2,2,1,256,256]{4,5,2,1,0,3:T(8,128)(2,1)S(1)}, bf16[2,2,2,1,256,256]{4,5,2,1,0,3:T(8,128)(2,1)}, u32[]{:S(2)}) copy-start(bf16[2,2,2,1,256,256]{4,5,2,1,0,3:T(8,128)(2,1)} %copy.4) | copy-start | bytes 3145732
  100.0 4.0 %copy-start.2 = (bf16[2,2,2,1,256,256]{4,5,2,1,0,3:T(8,128)(2,1)S(1)}, bf16[2,2,2,1,256,256]{4,5,2,1,0,3:T(8,128)(2,1)}, u32[]{:S(2)}) copy-start(bf16[2,2,2,1,256,256]{4,5,2,1,0,3:T(8,128)(2,1)} %copy.14) | copy-start | bytes 3145732
  115.0 4.0 %copy-start.1 = (bf16[2,2,2,1,256,256]{4,5,2,1,0,3:T(8,128)(2,1)S(1)}, bf16[2,2,2,1,256,256]{4,5,2,1,0,3:T(8,128)(2,1)}, u32[]{:S(2)}) copy-start(bf16[2,2,2,1,256,256]{4,5,2,1,0,3:T(8,128)(2,1)} %copy.11) | copy-start | bytes 3145732
  130.1 2.4 copy-start
Sparse Core Ops, SparseCore 0:
  155.3 172.8 reduce-scatter.1
where the time goes:
time: 338 us; the launch traced here: 335 us
  waiting for transfers between devices  198 us (59%)
  local copies, waits for them, and re-layouts  61.2 us (18%)
  between operations  26 us (8%)
  matrix products  23 us (7%)
  other arithmetic  17.6 us (5%)
  starting transfers between devices  8.87 us (3%)
    reduce_scatter x1, waiting for transfers between devices, per_device(): return lax.psum_scatter(terms, 'sa', scatter_dimension=4, tiled=True)  173 us
    dot_general x4, matrix products, pair_term(): jnp.einsum('nsp,nsq->npq', left, right, preferred_element_type=jnp.float32)  23 us
    another operation x4, local copies, waits for them, and re-layouts, per_device(): terms = jnp.stack([pair_term(index) for index in range(NPAIR)], axis=2)  21 us
    reshape x4, local copies, waits for them, and re-layouts, pair_term(): real_rows = beside.reshape(count, 2 * traces, points)  14.4 us
    another operation x1, other arithmetic, per_device(): terms = jnp.stack([pair_term(index) for index in range(NPAIR)], axis=2)  11.6 us
    ppermute x1, waiting for transfers between devices, from_behind(): lax.ppermute(value, axis, [(source, source + steps) for source in range(i...  10.6 us
    ppermute x1, waiting for transfers between devices, with_halo(): before = lax.ppermute(last, axis, up)  9.47 us
    slice x4, local copies, waits for them, and re-layouts, pair_term(): beside[:, :, :, 1]  9.06 us
  transfers between devices with their start and end apart: 4, of which 4 were waited for; matrix products, arithmetic and copies ran while one was open for 1% of the time, Pallas kernels for 0%

commit v1 on v0

v1 whole, which is shorter than its diff:
```python
import functools

import jax
import jax.numpy as jnp
from jax import lax
from jax.experimental import pallas as pl
from jax.experimental.pallas import tpu as pltpu
from jax.sharding import PartitionSpec as P

NPAIR = 4
RING = 4
LOOSE0, LOOSE1, DOWN, UP = range(4)
GROUPS = (
    ((0, 0, LOOSE0), (0, 0, LOOSE1), (0, 0, UP), (1, 0, LOOSE0), (0, 1, DOWN)),
    ((0, 0, DOWN), (1, 0, LOOSE1), (1, 0, DOWN), (1, 0, UP), (0, 1, LOOSE0), (0, 1, LOOSE1)),
    ((0, 1, UP), (1, 1, LOOSE0), (1, 1, LOOSE1), (1, 1, DOWN), (1, 1, UP)),
)


def slot_table(offsets):
    dx = [offsets[k, 0] for k in range(NPAIR)]
    dy = [offsets[k, 1] for k in range(NPAIR)]
    code = [
        jnp.where(dx[k] == 0, dy[k], jnp.where(dy[k] == 0, 2, jnp.where(dy[k] < 0, 3, 4)))
        for k in range(NPAIR)
    ]
    rank = [
        sum((code[j] < code[k]).astype(jnp.int32) for j in range(NPAIR) if j != k) for k in range(NPAIR)
    ]

    def pick(values, slot):
        return sum(jnp.where(rank[k] == slot, values[k], 0) for k in range(NPAIR))

    return [(pick(dx, s), pick(dy, s), pick(list(range(NPAIR)), s)) for s in range(NPAIR)]


def blocks_kernel(groups, halo, *refs):
    count = 4 + (6 if halo else 0)
    meta, offsets, mine, theirs = refs[:4]
    outs = refs[count : count + 8 * len(groups)]
    left, right, acc = refs[count + 8 * len(groups) :]
    points = mine.shape[-1]
    traces = mine.shape[-2]
    sources = {(tx, ty): (mine.at[tx, ty], theirs.at[tx, ty]) for tx in range(2) for ty in range(2)}
    if halo:
        x_m, x_t, up_m, up_t, down_m, down_t = refs[4:count]
        for ty in range(2):
            sources[2, ty] = (x_m.at[ty], x_t.at[ty])
        for tx in range(3):
            sources[tx, 2] = (up_m.at[tx], up_t.at[tx])
        for tx in range(1, 3):
            sources[tx, -1] = (down_m.at[tx - 1], down_t.at[tx - 1])
    for (tx, ty), parts in sources.items():
        tile = tx * 4 + ty + 1
        for i, part in enumerate(parts):
            re, im = part[0], part[1]
            low = slice(2 * i * traces, (2 * i + 1) * traces)
            high = slice((2 * i + 1) * traces, (2 * i + 2) * traces)
            right[tile, low, :points] = re
            right[tile, high, :points] = im
            right[tile, low, points:] = im
            right[tile, high, points:] = -re
            if tx < 2 and 0 <= ty < 2:
                left[tx * 2 + ty, :, low] = re.T
                left[tx * 2 + ty, :, high] = im.T
    x_lo, y = meta[0], meta[1]
    slots = slot_table(offsets)
    rows = points // (2 * RING)
    step = 0
    for g, group in enumerate(groups):
        for b, (tx, ty, slot) in enumerate(group):
            dx, dy, _ = slots[slot]
            tile = (tx + dx) * 4 + (ty + dy + 1)
            place = acc.at[step % 2]
            step += 1
            place[...] = jnp.dot(left[tx * 2 + ty], right[tile], preferred_element_type=jnp.float32)
            for d in range(RING):
                for h in range(2):
                    start = lax.rem(x_lo + h, 2) * (points // 2) + lax.rem(y + d, RING) * rows
                    outs[8 * g + 2 * d + h][b] = place[pl.ds(pl.multiple_of(start, rows), rows), :]


def blocks(groups, meta, offsets, tiles, halos):
    points, traces = tiles[0].shape[-1], tiles[0].shape[-2]
    smem = pl.BlockSpec(memory_space=pltpu.SMEM)
    vmem = pl.BlockSpec(memory_space=pltpu.VMEM)
    out_shape = []
    for group in groups:
        shape = (len(group), points // (2 * RING), 2 * points)
        out_shape += [jax.ShapeDtypeStruct(shape, jnp.float32)] * (2 * RING)
    number = sum(len(group) for group in groups)
    outs = pl.pallas_call(
        functools.partial(blocks_kernel, groups, bool(halos)),
        out_shape=out_shape,
        in_specs=[smem, smem] + [vmem] * (len(tiles) + len(halos)),
        out_specs=[vmem] * len(out_shape),
        scratch_shapes=[
            pltpu.VMEM((4, points, 4 * traces), jnp.bfloat16),
            pltpu.VMEM((12, 4 * traces, 2 * points), jnp.bfloat16),
            pltpu.VMEM((2, points, 2 * points), jnp.float32),
        ],
        compiler_params=pltpu.CompilerParams(vmem_limit_bytes=40 * 1024 * 1024),
        cost_estimate=pl.CostEstimate(
            flops=number * 2 * points * 2 * points * 4 * traces,
            bytes_accessed=number * points * 2 * points * 4 + 4 * 1024 * 1024,
            transcendentals=0,
        ),
        name="tile_blocks",
    )(meta, offsets, *tiles, *halos)
    return [outs[8 * g : 8 * g + 8] for g in range(len(groups))]


def final_kernel(meta, offsets, *refs):
    out = refs[-1]
    x_lo = meta[0]
    slots = slot_table(offsets)
    for g, group in enumerate(GROUPS):
        own, before, after, other = refs[4 * g : 4 * g + 4]
        for b, (tx, ty, slot) in enumerate(group):
            pair = slots[slot][2]
            out[tx, ty, pair, x_lo] = own[b] + before[b] + after[b]
            out[tx, ty, pair, 1 - x_lo] = other[b]


def final(meta, offsets, parts, shape):
    smem = pl.BlockSpec(memory_space=pltpu.SMEM)
    vmem = pl.BlockSpec(memory_space=pltpu.VMEM)
    flat = [part for group in parts for part in group]
    return pl.pallas_call(
        final_kernel,
        out_shape=jax.ShapeDtypeStruct(shape, jnp.float32),
        in_specs=[smem, smem] + [vmem] * len(flat),
        out_specs=vmem,
        compiler_params=pltpu.CompilerParams(vmem_limit_bytes=40 * 1024 * 1024),
        name="place_blocks",
    )(meta, offsets, *flat)


def shift(axis, size, steps):
    return functools.partial(
        lax.ppermute, axis_name=axis, perm=[(i, i + steps) for i in range(size) if 0 <= i + steps < size]
    )


def per_device(green, offsets):
    points = green.shape[5]
    gx, gy = lax.axis_size("gx"), lax.axis_size("gy")
    sa = lax.axis_index("sa")
    x_lo, y = sa // RING, sa % RING
    meta = jnp.stack([x_lo, y]).astype(jnp.int32)
    swap = functools.partial(lax.ppermute, axis_name="sa", perm=[(i, (i + RING) % (2 * RING)) for i in range(2 * RING)])

    def around(steps):
        perm = [(h * RING + i, h * RING + (i + steps) % RING) for h in range(2) for i in range(RING)]
        return functools.partial(lax.ppermute, axis_name="sa", perm=perm)

    def halo(tiles):
        beside = shift("gx", gx, -1)(tiles[0])
        up = shift("gy", gy, -1)(jnp.stack([tiles[0, 0], tiles[1, 0], beside[0]]))
        down = shift("gy", gy, 1)(jnp.stack([tiles[1, 1], beside[1]]))
        return beside, up, down

    theirs = swap(lax.dynamic_index_in_dim(green, 1 - x_lo, 2, keepdims=False))
    mine = lax.dynamic_index_in_dim(green, x_lo, 2, keepdims=False)
    halo_mine = halo(mine)
    halo_theirs = halo(theirs)
    tiles = [mine, theirs]
    halos = [value for pair in zip(halo_mine, halo_theirs) for value in pair]
    pieces = blocks(GROUPS[:1], meta, offsets, tiles, []) + blocks(GROUPS[1:], meta, offsets, tiles, halos)
    parts = []
    for own_a, own_b, next_a, next_b, far_a, far_b, prev_a, prev_b in pieces:
        far_b = around(-1)(far_b)
        far_a = around(1)(far_a)
        from_prev_b = around(1)(next_b)
        from_next_a = around(-1)(prev_a)
        from_next_b = around(-1)(prev_b + far_b)
        from_prev_a = around(1)(next_a + far_a)
        other = swap(own_b + from_prev_b + from_next_b)
        parts.append((own_a, from_prev_a, from_next_a, other))
    shape = green.shape[:2] + (NPAIR, green.shape[2], points // (2 * RING), 2 * points)
    return final(meta, offsets, parts, shape)


def solution(mesh):
    return jax.shard_map(
        per_device,
        mesh=mesh,
        in_specs=(P("gx", "gy", None, None, "sa", None), P()),
        out_specs=P("gx", "gy", None, None, "sa", None),
        check_vma=False,
    )
```

time: 338 us -> 152 us (0.45)
  waiting for transfers between devices: 198 us -> 89.4 us
  local copies, waits for them, and re-layouts: 61.2 us -> 2.17 us
  starting transfers between devices: 8.87 us -> 45.8 us
  between operations: 26 us -> 0.22 us
  matrix products: 23 us -> 0 us
  other arithmetic: 17.6 us -> 4.25 us
  Pallas kernels: 0 us -> 10.3 us
    reduce_scatter x1 -> x0, waiting for transfers between devices: 173 us -> none  [per_device(): return lax.psum_scatter(terms, 'sa', scatter_dimension=4, tiled=True)]
    ppermute x3 -> x28, waiting for transfers between devices: 25.4 us -> 89.4 us  [the longest x1 21.7 us: per_device(): theirs = swap(lax.dynamic_index_in_dim(green, 1 - x_lo, 2, keepdims=False))]
    ppermute x3 -> x28, starting transfers between devices: 8.87 us -> 45.8 us  [the longest x3 9.51 us: per_device(): from_next_b = around(-1)(prev_b + far_b)]
    dot_general x4 -> x0, matrix products: 23 us -> none  [pair_term(): jnp.einsum('nsp,nsq->npq', left, right, preferred_element_type=jnp.float32)]
    another operation x4 -> x2, local copies, waits for them, and re-layouts: 21 us -> 0.11 us  [halo(): down = shift('gy', gy, 1)(jnp.stack([tiles[1, 1], beside[1]]))]
    reshape x4 -> x0, local copies, waits for them, and re-layouts: 14.4 us -> none  [pair_term(): real_rows = beside.reshape(count, 2 * traces, points)]
    slice x7 -> x2, local copies, waits for them, and re-layouts: 12.9 us -> 0.07 us  [halo(): down = shift('gy', gy, 1)(jnp.stack([tiles[1, 1], beside[1]]))]
    pallas_call x0 -> x3, Pallas kernels: none -> 10.3 us  [the longest x2 8.14 us: blocks(): pl.pallas_call(functools.partial(blocks_kernel, groups, bool(halos)), out...]
  transfers between devices with their start and end apart: 4 -> 28, of which waited for: 4 -> 17; matrix products, arithmetic and copies ran while one was open for 1% -> 3% of each run, Pallas kernels for 0% -> 5%
where the time goes in v1:
time: 152 us
  waiting for transfers between devices  89.4 us (59%)
  starting transfers between devices  45.8 us (30%)
  Pallas kernels  10.3 us (7%)
  other arithmetic  4.25 us (3%)
  local copies, waits for them, and re-layouts  2.17 us (1%)
    ppermute x1, waiting for transfers between devices, per_device(): theirs = swap(lax.dynamic_index_in_dim(green, 1 - x_lo, 2, keepdims=False))  21.7 us
    ppermute x3, waiting for transfers between devices, per_device(): far_b = around(-1)(far_b)  15.3 us
    ppermute x3, waiting for transfers between devices, per_device(): from_next_a = around(-1)(prev_a)  10.4 us
    ppermute x3, waiting for transfers between devices, per_device(): from_prev_b = around(1)(next_b)  9.64 us
    ppermute x3, starting transfers between devices, per_device(): from_next_b = around(-1)(prev_b + far_b)  9.51 us
    ppermute x2, waiting for transfers between devices, halo(): down = shift('gy', gy, 1)(jnp.stack([tiles[1, 1], beside[1]]))  9.4 us
    ppermute x2, starting transfers between devices, halo(): down = shift('gy', gy, 1)(jnp.stack([tiles[1, 1], beside[1]]))  8.84 us
    ppermute x3, waiting for transfers between devices, per_device(): from_prev_a = around(1)(next_a + far_a)  8.17 us
  transfers between devices with their start and end apart: 28, of which 17 were waited for; matrix products, arithmetic and copies ran while one was open for 3% of the time, Pallas kernels for 5%

profile of v1, /device:TPU:100, one launch (start us, length us, event | category | flops | bytes accessed | tf_op | source)
XLA Modules:
  0.0 152.2 jit_solution(13377258117873255908)
XLA Ops:
  0.0 1.8 %dynamic-slice_bitcast_fusion.2 = (bf16[2,2,1,2,256,256]{5,4,3,1,2,0:T(8,128)(2,1)S(1)}, bf16[2,2,2,256,256]{4,3,2,1,0:T(8,128)(2,1)S(1)}, bf16[2,2,2,256,256]{4,3,2,1,0:T(8,128)(2,1)S(1)}) fusion(bf16[2,2,2,2,256,256]{5,4,3,2,1,0:T(8,128)(2,1)} %param.2, s32[]{:T(128)S(6)} %select_n.20, s32[]{:T(128)S(6)} %select_n.21), kind=kLoop, calls=%fused_computation.2 | loop fusion | bytes 5242888
  1.8 1.3 collective-permute-start
  3.2 1.9 %collective-permute-start.8 = (bf16[2,2,256,256]{3,2,1,0:T(8,128)(2,1)S(1)}, bf16[2,2,256,256]{3,2,1,0:T(8,128)(2,1)S(1)}, u32[]{:S(2)}, u32[]{:S(2)}) collective-permute-start(bf16[2,2,256,256]{3,2,1,0:T(8,128)(2,1)S(1)} %slice_bitcast_fusion.1), channel_id=1, source_target_pairs={{64,0},{128,64},{192,128},{65,1},{129,65},{193,129},{66,2},{130,66... | collective-permute-start | bytes 1572872 | tf_op jit(solution)/shard_map/ppermute | solution.py:158
  5.1 0.1 slice_bitcast_fusion.3
  5.1 21.7 %collective-permute-done.refs_3_ = bf16[2,2,2,256,256]{4,3,2,1,0:T(8,128)(2,1)S(1)} collective-permute-done((bf16[2,2,2,256,256]{4,3,2,1,0:T(8,128)(2,1)S(1)}, bf16[2,2,2,256,256]{4,3,2,1,0:T(8,128)(2,1)S(1)}, u32[]{:S(2)}, u32[]{:S(2)}) %collective-permute-start) | collective-permute-done | bytes 1048608 | tf_op jit(solution)/shard_map/ppermute | solution.py:163
  26.9 1.9 %collective-permute-start.9 = (bf16[2,2,256,256]{3,2,1,0:T(8,128)(2,1)S(1)}, bf16[2,2,256,256]{3,2,1,0:T(8,128)(2,1)S(1)}, u32[]{:S(2)}, u32[]{:S(2)}) collective-permute-start(bf16[2,2,256,256]{3,2,1,0:T(8,128)(2,1)S(1)} %slice_bitcast_fusion), channel_id=1, source_target_pairs={{64,0},{128,64},{192,128},{65,1},{129,65},{193,129},{66,2},{130,66... | collective-permute-start | bytes 1572872 | tf_op jit(solution)/shard_map/ppermute | solution.py:158
  28.8 2.4 %collective-permute-done.8.refs_4_ = bf16[2,2,256,256]{3,2,1,0:T(8,128)(2,1)S(1)} collective-permute-done((bf16[2,2,256,256]{3,2,1,0:T(8,128)(2,1)S(1)}, bf16[2,2,256,256]{3,2,1,0:T(8,128)(2,1)S(1)}, u32[]{:S(2)}, u32[]{:S(2)}) %collective-permute-start.8) | collective-permute-done | bytes 524320 | tf_op jit(solution)/shard_map/ppermute | solution.py:158
  31.2 1.0 pad_maximum_fusion
  32.2 2.0 %collective-permute-start.10 = (bf16[3,2,256,256]{3,2,1,0:T(8,128)(2,1)}, bf16[3,2,256,256]{3,2,1,0:T(8,128)(2,1)}, u32[]{:S(2)}, u32[]{:S(2)}) collective-permute-start(bf16[3,2,256,256]{3,2,1,0:T(8,128)(2,1)} %pad_maximum_fusion), channel_id=1, source_target_pairs={{8,0},{16,8},{24,16},{32,24},{40,32},{48,40},{56,48},{9,1},{17,9},... | collective-permute-start | bytes 2359304 | tf_op jit(solution)/shard_map/ppermute | solution.py:159
  34.2 0.1 slice_bitcast_fusion.2
  34.2 2.5 %collective-permute-done.9.refs_5_ = bf16[2,2,256,256]{3,2,1,0:T(8,128)(2,1)S(1)} collective-permute-done((bf16[2,2,256,256]{3,2,1,0:T(8,128)(2,1)S(1)}, bf16[2,2,256,256]{3,2,1,0:T(8,128)(2,1)S(1)}, u32[]{:S(2)}, u32[]{:S(2)}) %collective-permute-start.9) | collective-permute-done | bytes 524320 | tf_op jit(solution)/shard_map/ppermute | solution.py:158
  36.8 0.0 copy-start
  36.8 1.0 pad_maximum_fusion.1
  37.8 2.0 %collective-permute-start.11 = (bf16[3,2,256,256]{3,2,1,0:T(8,128)(2,1)}, bf16[3,2,256,256]{3,2,1,0:T(8,128)(2,1)}, u32[]{:S(2)}, u32[]{:S(2)}) collective-permute-start(bf16[3,2,256,256]{3,2,1,0:T(8,128)(2,1)} %pad_maximum_fusion.1), channel_id=1, source_target_pairs={{8,0},{16,8},{24,16},{32,24},{40,32},{48,40},{56,48},{9,1},{17,9},... | collective-permute-start | bytes 2359304 | tf_op jit(solution)/shard_map/ppermute | solution.py:159
  39.8 0.8 pad_maximum_fusion.2
  40.7 5.0 %collective-permute-start.12 = (bf16[2,2,256,256]{3,2,1,0:T(8,128)(2,1)}, bf16[2,2,256,256]{3,2,1,0:T(8,128)(2,1)}, u32[]{:S(2)}, u32[]{:S(2)}) collective-permute-start(bf16[2,2,256,256]{3,2,1,0:T(8,128)(2,1)} %pad_maximum_fusion.2), channel_id=1, source_target_pairs={{0,8},{8,16},{16,24},{24,32},{32,40},{40,48},{48,56},{1,9},{9,17},... | collective-permute-start | bytes 1572872 | tf_op jit(solution)/shard_map/ppermute | solution.py:160
  45.7 0.8 pad_maximum_fusion.3
  46.5 3.8 %collective-permute-start.13 = (bf16[2,2,256,256]{3,2,1,0:T(8,128)(2,1)}, bf16[2,2,256,256]{3,2,1,0:T(8,128)(2,1)}, u32[]{:S(2)}, u32[]{:S(2)}) collective-permute-start(bf16[2,2,256,256]{3,2,1,0:T(8,128)(2,1)} %pad_maximum_fusion.3), channel_id=1, source_target_pairs={{0,8},{8,16},{16,24},{24,32},{32,40},{40,48},{48,56},{1,9},{9,17},... | collective-permute-start | bytes 1572872 | tf_op jit(solution)/shard_map/ppermute | solution.py:160
  50.4 0.1 copy.6.refs_1_.offsets
  50.5 0.1 pad_add_fusion.refs_0_.meta
  50.5 2.4 %tile_blocks.2 = (f32[5,32,512]{2,1,0:T(8,128)S(1)}, f32[5,32,512]{2,1,0:T(8,128)S(1)}, f32[5,32,512]{2,1,0:T(8,128)S(1)}, f32[5,32,512]{2,1,0:T(8,128)S(1)}, f3...) custom-call(s32[2]{0:T(128)S(1)} %pad_add_fusion.refs_0_.meta, ...), custom_call_target="tpu_custom_call" | custom-call | flops 1342177280 | bytes 6815744 | tf_op jit(solution)/shard_map/tile_blocks/pallas_call | solution.py:92
  53.0 1.7 %collective-permute-start.1 = (f32[5,32,512]{2,1,0:T(8,128)S(1)}, f32[5,32,512]{2,1,0:T(8,128)S(1)}, u32[]{:S(2)}, u32[]{:S(2)}) collective-permute-start(f32[5,32,512]{2,1,0:T(8,128)S(1)} %get-tuple-element.31), channel_id=1, source_target_pairs={{0,1},{1,2},{2,3},{3,0},{4,5},{5,6},{6,7},{7,4},{8,9},{9,10},{10,1... | collective-permute-start | bytes 983048 | tf_op jit(solution)/shard_map/ppermute | solution.py:173
  54.6 3.7 %collective-permute-done.12.refs_8_ = bf16[2,2,256,256]{3,2,1,0:T(8,128)(2,1)} collective-permute-done((bf16[2,2,256,256]{3,2,1,0:T(8,128)(2,1)}, bf16[2,2,256,256]{3,2,1,0:T(8,128)(2,1)}, u32[]{:S(2)}, u32[]{:S(2)}) %collective-permute-start.12) | collective-permute-done | bytes 524320 | tf_op jit(solution)/shard_map/ppermute | solution.py:160
  58.4 0.0 collective-permute-done.10.refs_6_
  58.4 5.7 %collective-permute-done.13.refs_9_ = bf16[2,2,256,256]{3,2,1,0:T(8,128)(2,1)} collective-permute-done((bf16[2,2,256,256]{3,2,1,0:T(8,128)(2,1)}, bf16[2,2,256,256]{3,2,1,0:T(8,128)(2,1)}, u32[]{:S(2)}, u32[]{:S(2)}) %collective-permute-start.13) | collective-permute-done | bytes 524320 | tf_op jit(solution)/shard_map/ppermute | solution.py:160
  64.0 6.2 %collective-permute-done.11.refs_7_ = bf16[3,2,256,256]{3,2,1,0:T(8,128)(2,1)} collective-permute-done((bf16[3,2,256,256]{3,2,1,0:T(8,128)(2,1)}, bf16[3,2,256,256]{3,2,1,0:T(8,128)(2,1)}, u32[]{:S(2)}, u32[]{:S(2)}) %collective-permute-start.11) | collective-permute-done | bytes 786464 | tf_op jit(solution)/shard_map/ppermute | solution.py:159
  70.2 5.7 %tile_blocks.3 = (f32[6,32,512]{2,1,0:T(8,128)S(1)}, f32[6,32,512]{2,1,0:T(8,128)S(1)}, f32[6,32,512]{2,1,0:T(8,128)S(1)}, f32[6,32,512]{2,1,0:T(8,128)S(1)}, f3...) custom-call(s32[2]{0:T(128)S(1)} %pad_add_fusion.refs_0_.meta, ...), custom_call_target="tpu_custom_call" | custom-call | flops 2952790016 | bytes 9961472 | tf_op jit(solution)/shard_map/tile_blocks/pallas_call | solution.py:92
  75.9 3.1 %collective-permute-start.18 = (f32[6,32,512]{2,1,0:T(8,128)S(1)}, f32[6,32,512]{2,1,0:T(8,128)S(1)}, u32[]{:S(2)}, u32[]{:S(2)}) collective-permute-start(f32[6,32,512]{2,1,0:T(8,128)S(1)} %get-tuple-element.44), channel_id=1, source_target_pairs={{0,3},{1,0},{2,1},{3,2},{4,7},{5,4},{6,5},{7,6},{8,11},{9,8},{10,9... | collective-permute-start | bytes 1179656 | tf_op jit(solution)/shard_map/ppermute | solution.py:172
  79.0 0.7 collective-permute-start.5
  79.8 0.4 collective-permute-start.3
  80.2 1.6 %collective-permute-start.4 = (f32[5,32,512]{2,1,0:T(8,128)S(1)}, f32[5,32,512]{2,1,0:T(8,128)S(1)}, u32[]{:S(2)}, u32[]{:S(2)}) collective-permute-start(f32[5,32,512]{2,1,0:T(8,128)S(1)} %get-tuple-element.34), channel_id=1, source_target_pairs={{0,1},{1,2},{2,3},{3,0},{4,5},{5,6},{6,7},{7,4},{8,9},{9,10},{10,1... | collective-permute-start | bytes 983048 | tf_op jit(solution)/shard_map/ppermute | solution.py:174
  81.8 1.7 %collective-permute-start.25 = (f32[5,32,512]{2,1,0:T(8,128)S(1)}, f32[5,32,512]{2,1,0:T(8,128)S(1)}, u32[]{:S(2)}, u32[]{:S(2)}) collective-permute-start(f32[5,32,512]{2,1,0:T(8,128)S(1)} %get-tuple-element.52), channel_id=1, source_target_pairs={{0,3},{1,0},{2,1},{3,2},{4,7},{5,4},{6,5},{7,6},{8,11},{9,8},{10,9... | collective-permute-start | bytes 983048 | tf_op jit(solution)/shard_map/ppermute | solution.py:172
  83.5 12.2 %collective-permute-done.5 = f32[5,32,512]{2,1,0:T(8,128)S(1)} collective-permute-done((f32[5,32,512]{2,1,0:T(8,128)S(1)}, f32[5,32,512]{2,1,0:T(8,128)S(1)}, u32[]{:S(2)}, u32[]{:S(2)}) %collective-permute-start.5) | collective-permute-done | bytes 327712 | tf_op jit(solution)/shard_map/ppermute | solution.py:172
  95.6 1.0 collective-permute-start.14
  96.7 5.9 %collective-permute-done.3.refs_2_ = f32[5,32,512]{2,1,0:T(8,128)S(1)} collective-permute-done((f32[5,32,512]{2,1,0:T(8,128)S(1)}, f32[5,32,512]{2,1,0:T(8,128)S(1)}, u32[]{:S(2)}, u32[]{:S(2)}) %collective-permute-start.3) | collective-permute-done | bytes 327712 | tf_op jit(solution)/shard_map/ppermute | solution.py:175
  102.7 3.7 %collective-permute-start.6 = (f32[5,32,512]{2,1,0:T(8,128)S(1)}, f32[5,32,512]{2,1,0:T(8,128)S(1)}, u32[]{:S(2)}, u32[]{:S(2)}) collective-permute-start(f32[5,32,512]{2,1,0:T(8,128)S(1)} %add.54), channel_id=1, source_target_pairs={{0,3},{1,0},{2,1},{3,2},{4,7},{5,4},{6,5},{7,6},{8,11},{9,8},{10,9... | collective-permute-start | bytes 983048 | tf_op jit(solution)/shard_map/ppermute | solution.py:176
  106.3 0.0 collective-permute-done.18
  106.3 0.0 collective-permute-start.21
  106.4 0.1 add.58
  106.4 0.1 collective-permute-start.17
  106.5 3.2 %collective-permute-done.25 = f32[5,32,512]{2,1,0:T(8,128)S(1)} collective-permute-done((f32[5,32,512]{2,1,0:T(8,128)S(1)}, f32[5,32,512]{2,1,0:T(8,128)S(1)}, u32[]{:S(2)}, u32[]{:S(2)}) %collective-permute-start.25) | collective-permute-done | bytes 327712 | tf_op jit(solution)/shard_map/ppermute | solution.py:172
  109.7 3.7 %collective-permute-start.19 = (f32[6,32,512]{2,1,0:T(8,128)S(1)}, f32[6,32,512]{2,1,0:T(8,128)S(1)}, u32[]{:S(2)}, u32[]{:S(2)}) collective-permute-start(f32[6,32,512]{2,1,0:T(8,128)S(1)} %add.58), channel_id=1, source_target_pairs={{0,3},{1,0},{2,1},{3,2},{4,7},{5,4},{6,5},{7,6},{8,11},{9,8},{10,9... | collective-permute-start | bytes 1179656 | tf_op jit(solution)/shard_map/ppermute | solution.py:176
  113.5 3.2 %collective-permute-done.6 = f32[5,32,512]{2,1,0:T(8,128)S(1)} collective-permute-done((f32[5,32,512]{2,1,0:T(8,128)S(1)}, f32[5,32,512]{2,1,0:T(8,128)S(1)}, u32[]{:S(2)}, u32[]{:S(2)}) %collective-permute-start.6) | collective-permute-done | bytes 327712 | tf_op jit(solution)/shard_map/ppermute | solution.py:176
  116.7 1.0 collective-permute-start.2
  117.7 0.5 collective-permute-done.21
  118.2 1.1 collective-permute-start.24
  119.3 2.1 %collective-permute-start.26 = (f32[5,32,512]{2,1,0:T(8,128)S(1)}, f32[5,32,512]{2,1,0:T(8,128)S(1)}, u32[]{:S(2)}, u32[]{:S(2)}) collective-permute-start(f32[5,32,512]{2,1,0:T(8,128)S(1)} %add.62), channel_id=1, source_target_pairs={{0,3},{1,0},{2,1},{3,2},{4,7},{5,4},{6,5},{7,6},{8,11},{9,8},{10,9... | collective-permute-start | bytes 983048 | tf_op jit(solution)/shard_map/ppermute | solution.py:176
  121.5 0.1 add_add_fusion.2
  121.6 0.1 add.56
  121.6 5.0 %collective-permute-done.17 = f32[6,32,512]{2,1,0:T(8,128)S(1)} collective-permute-done((f32[6,32,512]{2,1,0:T(8,128)S(1)}, f32[6,32,512]{2,1,0:T(8,128)S(1)}, u32[]{:S(2)}, u32[]{:S(2)}) %collective-permute-start.17) | collective-permute-done | bytes 393248 | tf_op jit(solution)/shard_map/ppermute | solution.py:174
  126.6 0.6 collective-permute-start.7
  127.3 1.5 %collective-permute-start.23 = (f32[5,32,512]{2,1,0:T(8,128)S(1)}, f32[5,32,512]{2,1,0:T(8,128)S(1)}, u32[]{:S(2)}, u32[]{:S(2)}) collective-permute-start(f32[5,32,512]{2,1,0:T(8,128)S(1)} %get-tuple-element.48), channel_id=1, source_target_pairs={{0,3},{1,0},{2,1},{3,2},{4,7},{5,4},{6,5},{7,6},{8,11},{9,8},{10,9... | collective-permute-start | bytes 983048 | tf_op jit(solution)/shard_map/ppermute | solution.py:175
  128.8 0.1 add_add_fusion
  128.9 2.1 %collective-permute-done.2.refs_1_ = f32[5,32,512]{2,1,0:T(8,128)S(1)} collective-permute-done((f32[5,32,512]{2,1,0:T(8,128)S(1)}, f32[5,32,512]{2,1,0:T(8,128)S(1)}, u32[]{:S(2)}, u32[]{:S(2)}) %collective-permute-start.2) | collective-permute-done | bytes 327712 | tf_op jit(solution)/shard_map/ppermute | solution.py:177
  131.1 1.0 collective-permute-start.16
  132.1 4.6 %collective-permute-done.24 = f32[5,32,512]{2,1,0:T(8,128)S(1)} collective-permute-done((f32[5,32,512]{2,1,0:T(8,128)S(1)}, f32[5,32,512]{2,1,0:T(8,128)S(1)}, u32[]{:S(2)}, u32[]{:S(2)}) %collective-permute-start.24) | collective-permute-done | bytes 327712 | tf_op jit(solution)/shard_map/ppermute | solution.py:174
  136.7 0.6 collective-permute-start.20
  137.3 0.1 add_add_fusion.1
  137.4 0.9 collective-permute-start.22
  138.3 0.8 collective-permute-done.23.refs_10_
  139.2 1.2 collective-permute-start.27
  140.4 3.6 %collective-permute-done.16.refs_6_ = f32[6,32,512]{2,1,0:T(8,128)S(1)} collective-permute-done((f32[6,32,512]{2,1,0:T(8,128)S(1)}, f32[6,32,512]{2,1,0:T(8,128)S(1)}, u32[]{:S(2)}, u32[]{:S(2)}) %collective-permute-start.16) | collective-permute-done | bytes 393248 | tf_op jit(solution)/shard_map/ppermute | solution.py:175
  144.0 6.0 %collective-permute-done.22.refs_9_ = f32[5,32,512]{2,1,0:T(8,128)S(1)} collective-permute-done((f32[5,32,512]{2,1,0:T(8,128)S(1)}, f32[5,32,512]{2,1,0:T(8,128)S(1)}, u32[]{:S(2)}, u32[]{:S(2)}) %collective-permute-start.22) | collective-permute-done | bytes 327712 | tf_op jit(solution)/shard_map/ppermute | solution.py:177
  150.0 2.1 %place_blocks.1 = f32[2,2,4,2,32,512]{5,4,3,2,1,0:T(8,128)} custom-call(s32[2]{0:T(128)S(1)} %pad_add_fusion.refs_0_.meta, s32[4,2]{1,0:T(4,128)S(1)} %copy.6.refs_1_.offsets, f32[5,32,512]{2,1,0:T(8,128)S(1)} %get-tuple-element.29.refs_0_, f32[5,32,512]{2,1,0:T(8,128)S(1)} %collective-permute-done.2.refs_1_, ...), custom_call_target="tpu_custom_call" | custom-call | tf_op jit(solution)/shard_map/place_blocks/pallas_call | solution.py:129
  (19 shorter events, 0.3 us)
Async XLA Ops:
  1.8 25.0 %collective-permute-start = (bf16[2,2,2,256,256]{4,3,2,1,0:T(8,128)(2,1)S(1)}, bf16[2,2,2,256,256]{4,3,2,1,0:T(8,128)(2,1)S(1)}, u32[]{:S(2)}, u32[]{:S(2)}) collective-permute-start(bf16[2,2,2,256,256]{4,3,2,1,0:T(8,128)(2,1)S(1)} %get-tuple-element.55), channel_id=1, source_target_pairs={{0,4},{1,5},{2,6},{3,7},{4,0},{5,1},{6,2},{7,3},{8,12},{9,13},{10,... | collective-permute-start | bytes 3145736 | tf_op jit(solution)/shard_map/ppermute | solution.py:163
  3.2 28.0 %collective-permute-start.8 = (bf16[2,2,256,256]{3,2,1,0:T(8,128)(2,1)S(1)}, bf16[2,2,256,256]{3,2,1,0:T(8,128)(2,1)S(1)}, u32[]{:S(2)}, u32[]{:S(2)}) collective-permute-start(bf16[2,2,256,256]{3,2,1,0:T(8,128)(2,1)S(1)} %slice_bitcast_fusion.1), channel_id=1, source_target_pairs={{64,0},{128,64},{192,128},{65,1},{129,65},{193,129},{66,2},{130,66... | collective-permute-start | bytes 1572872 | tf_op jit(solution)/shard_map/ppermute | solution.py:158
  26.9 9.9 %collective-permute-start.9 = (bf16[2,2,256,256]{3,2,1,0:T(8,128)(2,1)S(1)}, bf16[2,2,256,256]{3,2,1,0:T(8,128)(2,1)S(1)}, u32[]{:S(2)}, u32[]{:S(2)}) collective-permute-start(bf16[2,2,256,256]{3,2,1,0:T(8,128)(2,1)S(1)} %slice_bitcast_fusion), channel_id=1, source_target_pairs={{64,0},{128,64},{192,128},{65,1},{129,65},{193,129},{66,2},{130,66... | collective-permute-start | bytes 1572872 | tf_op jit(solution)/shard_map/ppermute | solution.py:158
  32.2 26.2 %collective-permute-start.10 = (bf16[3,2,256,256]{3,2,1,0:T(8,128)(2,1)}, bf16[3,2,256,256]{3,2,1,0:T(8,128)(2,1)}, u32[]{:S(2)}, u32[]{:S(2)}) collective-permute-start(bf16[3,2,256,256]{3,2,1,0:T(8,128)(2,1)} %pad_maximum_fusion), channel_id=1, source_target_pairs={{8,0},{16,8},{24,16},{32,24},{40,32},{48,40},{56,48},{9,1},{17,9},... | collective-permute-start | bytes 2359304 | tf_op jit(solution)/shard_map/ppermute | solution.py:159
  36.8 13.6 %copy-start = (s32[4,2]{0,1:T(2,128)S(1)}, s32[4,2]{0,1:T(2,128)}, u32[]{:S(2)}) copy-start(s32[4,2]{0,1:T(2,128)} %param.3) | copy-start | bytes 100
  37.8 32.4 %collective-permute-start.11 = (bf16[3,2,256,256]{3,2,1,0:T(8,128)(2,1)}, bf16[3,2,256,256]{3,2,1,0:T(8,128)(2,1)}, u32[]{:S(2)}, u32[]{:S(2)}) collective-permute-start(bf16[3,2,256,256]{3,2,1,0:T(8,128)(2,1)} %pad_maximum_fusion.1), channel_id=1, source_target_pairs={{8,0},{16,8},{24,16},{32,24},{40,32},{48,40},{56,48},{9,1},{17,9},... | collective-permute-start | bytes 2359304 | tf_op jit(solution)/shard_map/ppermute | solution.py:159
  40.7 17.7 %collective-permute-start.12 = (bf16[2,2,256,256]{3,2,1,0:T(8,128)(2,1)}, bf16[2,2,256,256]{3,2,1,0:T(8,128)(2,1)}, u32[]{:S(2)}, u32[]{:S(2)}) collective-permute-start(bf16[2,2,256,256]{3,2,1,0:T(8,128)(2,1)} %pad_maximum_fusion.2), channel_id=1, source_target_pairs={{0,8},{8,16},{16,24},{24,32},{32,40},{40,48},{48,56},{1,9},{9,17},... | collective-permute-start | bytes 1572872 | tf_op jit(solution)/shard_map/ppermute | solution.py:160
  46.5 17.5 %collective-permute-start.13 = (bf16[2,2,256,256]{3,2,1,0:T(8,128)(2,1)}, bf16[2,2,256,256]{3,2,1,0:T(8,128)(2,1)}, u32[]{:S(2)}, u32[]{:S(2)}) collective-permute-start(bf16[2,2,256,256]{3,2,1,0:T(8,128)(2,1)} %pad_maximum_fusion.3), channel_id=1, source_target_pairs={{0,8},{8,16},{16,24},{24,32},{32,40},{40,48},{48,56},{1,9},{9,17},... | collective-permute-start | bytes 1572872 | tf_op jit(solution)/shard_map/ppermute | solution.py:160
  53.0 28.8 %collective-permute-start.1 = (f32[5,32,512]{2,1,0:T(8,128)S(1)}, f32[5,32,512]{2,1,0:T(8,128)S(1)}, u32[]{:S(2)}, u32[]{:S(2)}) collective-permute-start(f32[5,32,512]{2,1,0:T(8,128)S(1)} %get-tuple-element.31), channel_id=1, source_target_pairs={{0,1},{1,2},{2,3},{3,0},{4,5},{5,6},{6,7},{7,4},{8,9},{9,10},{10,1... | collective-permute-start | bytes 983048 | tf_op jit(solution)/shard_map/ppermute | solution.py:173
  75.9 30.4 %collective-permute-start.18 = (f32[6,32,512]{2,1,0:T(8,128)S(1)}, f32[6,32,512]{2,1,0:T(8,128)S(1)}, u32[]{:S(2)}, u32[]{:S(2)}) collective-permute-start(f32[6,32,512]{2,1,0:T(8,128)S(1)} %get-tuple-element.44), channel_id=1, source_target_pairs={{0,3},{1,0},{2,1},{3,2},{4,7},{5,4},{6,5},{7,6},{8,11},{9,8},{10,9... | collective-permute-start | bytes 1179656 | tf_op jit(solution)/shard_map/ppermute | solution.py:172
  79.0 16.6 %collective-permute-start.5 = (f32[5,32,512]{2,1,0:T(8,128)S(1)}, f32[5,32,512]{2,1,0:T(8,128)S(1)}, u32[]{:S(2)}, u32[]{:S(2)}) collective-permute-start(f32[5,32,512]{2,1,0:T(8,128)S(1)} %get-tuple-element.36), channel_id=1, source_target_pairs={{0,3},{1,0},{2,1},{3,2},{4,7},{5,4},{6,5},{7,6},{8,11},{9,8},{10,9... | collective-permute-start | bytes 983048 | tf_op jit(solution)/shard_map/ppermute | solution.py:172
  79.8 22.9 %collective-permute-start.3 = (f32[5,32,512]{2,1,0:T(8,128)S(1)}, f32[5,32,512]{2,1,0:T(8,128)S(1)}, u32[]{:S(2)}, u32[]{:S(2)}) collective-permute-start(f32[5,32,512]{2,1,0:T(8,128)S(1)} %get-tuple-element.32), channel_id=1, source_target_pairs={{0,3},{1,0},{2,1},{3,2},{4,7},{5,4},{6,5},{7,6},{8,11},{9,8},{10,9... | collective-permute-start | bytes 983048 | tf_op jit(solution)/shard_map/ppermute | solution.py:175
  80.2 26.2 %collective-permute-start.4 = (f32[5,32,512]{2,1,0:T(8,128)S(1)}, f32[5,32,512]{2,1,0:T(8,128)S(1)}, u32[]{:S(2)}, u32[]{:S(2)}) collective-permute-start(f32[5,32,512]{2,1,0:T(8,128)S(1)} %get-tuple-element.34), channel_id=1, source_target_pairs={{0,1},{1,2},{2,3},{3,0},{4,5},{5,6},{6,7},{7,4},{8,9},{9,10},{10,1... | collective-permute-start | bytes 983048 | tf_op jit(solution)/shard_map/ppermute | solution.py:174
  81.8 27.9 %collective-permute-start.25 = (f32[5,32,512]{2,1,0:T(8,128)S(1)}, f32[5,32,512]{2,1,0:T(8,128)S(1)}, u32[]{:S(2)}, u32[]{:S(2)}) collective-permute-start(f32[5,32,512]{2,1,0:T(8,128)S(1)} %get-tuple-element.52), channel_id=1, source_target_pairs={{0,3},{1,0},{2,1},{3,2},{4,7},{5,4},{6,5},{7,6},{8,11},{9,8},{10,9... | collective-permute-start | bytes 983048 | tf_op jit(solution)/shard_map/ppermute | solution.py:172
  95.6 23.7 %collective-permute-start.14 = (f32[6,32,512]{2,1,0:T(8,128)S(1)}, f32[6,32,512]{2,1,0:T(8,128)S(1)}, u32[]{:S(2)}, u32[]{:S(2)}) collective-permute-start(f32[6,32,512]{2,1,0:T(8,128)S(1)} %get-tuple-element.39), channel_id=1, source_target_pairs={{0,1},{1,2},{2,3},{3,0},{4,5},{5,6},{6,7},{7,4},{8,9},{9,10},{10,1... | collective-permute-start | bytes 1179656 | tf_op jit(solution)/shard_map/ppermute | solution.py:173
  102.7 14.0 %collective-permute-start.6 = (f32[5,32,512]{2,1,0:T(8,128)S(1)}, f32[5,32,512]{2,1,0:T(8,128)S(1)}, u32[]{:S(2)}, u32[]{:S(2)}) collective-permute-start(f32[5,32,512]{2,1,0:T(8,128)S(1)} %add.54), channel_id=1, source_target_pairs={{0,3},{1,0},{2,1},{3,2},{4,7},{5,4},{6,5},{7,6},{8,11},{9,8},{10,9... | collective-permute-start | bytes 983048 | tf_op jit(solution)/shard_map/ppermute | solution.py:176
  106.3 11.9 %collective-permute-start.21 = (f32[5,32,512]{2,1,0:T(8,128)S(1)}, f32[5,32,512]{2,1,0:T(8,128)S(1)}, u32[]{:S(2)}, u32[]{:S(2)}) collective-permute-start(f32[5,32,512]{2,1,0:T(8,128)S(1)} %get-tuple-element.47), channel_id=1, source_target_pairs={{0,1},{1,2},{2,3},{3,0},{4,5},{5,6},{6,7},{7,4},{8,9},{9,10},{10,1... | collective-permute-start | bytes 983048 | tf_op jit(solution)/shard_map/ppermute | solution.py:173
  106.4 20.2 %collective-permute-start.17 = (f32[6,32,512]{2,1,0:T(8,128)S(1)}, f32[6,32,512]{2,1,0:T(8,128)S(1)}, u32[]{:S(2)}, u32[]{:S(2)}) collective-permute-start(f32[6,32,512]{2,1,0:T(8,128)S(1)} %get-tuple-element.42), channel_id=1, source_target_pairs={{0,1},{1,2},{2,3},{3,0},{4,5},{5,6},{6,7},{7,4},{8,9},{9,10},{10,1... | collective-permute-start | bytes 1179656 | tf_op jit(solution)/shard_map/ppermute | solution.py:174
  109.7 17.6 %collective-permute-start.19 = (f32[6,32,512]{2,1,0:T(8,128)S(1)}, f32[6,32,512]{2,1,0:T(8,128)S(1)}, u32[]{:S(2)}, u32[]{:S(2)}) collective-permute-start(f32[6,32,512]{2,1,0:T(8,128)S(1)} %add.58), channel_id=1, source_target_pairs={{0,3},{1,0},{2,1},{3,2},{4,7},{5,4},{6,5},{7,6},{8,11},{9,8},{10,9... | collective-permute-start | bytes 1179656 | tf_op jit(solution)/shard_map/ppermute | solution.py:176
  116.7 14.4 %collective-permute-start.2 = (f32[5,32,512]{2,1,0:T(8,128)S(1)}, f32[5,32,512]{2,1,0:T(8,128)S(1)}, u32[]{:S(2)}, u32[]{:S(2)}) collective-permute-start(f32[5,32,512]{2,1,0:T(8,128)S(1)} %add.52), channel_id=1, source_target_pairs={{0,1},{1,2},{2,3},{3,0},{4,5},{5,6},{6,7},{7,4},{8,9},{9,10},{10,1... | collective-permute-start | bytes 983048 | tf_op jit(solution)/shard_map/ppermute | solution.py:177
  118.2 18.5 %collective-permute-start.24 = (f32[5,32,512]{2,1,0:T(8,128)S(1)}, f32[5,32,512]{2,1,0:T(8,128)S(1)}, u32[]{:S(2)}, u32[]{:S(2)}) collective-permute-start(f32[5,32,512]{2,1,0:T(8,128)S(1)} %get-tuple-element.50), channel_id=1, source_target_pairs={{0,1},{1,2},{2,3},{3,0},{4,5},{5,6},{6,7},{7,4},{8,9},{9,10},{10,1... | collective-permute-start | bytes 983048 | tf_op jit(solution)/shard_map/ppermute | solution.py:174
  119.3 17.4 %collective-permute-start.26 = (f32[5,32,512]{2,1,0:T(8,128)S(1)}, f32[5,32,512]{2,1,0:T(8,128)S(1)}, u32[]{:S(2)}, u32[]{:S(2)}) collective-permute-start(f32[5,32,512]{2,1,0:T(8,128)S(1)} %add.62), channel_id=1, source_target_pairs={{0,3},{1,0},{2,1},{3,2},{4,7},{5,4},{6,5},{7,6},{8,11},{9,8},{10,9... | collective-permute-start | bytes 983048 | tf_op jit(solution)/shard_map/ppermute | solution.py:176
  126.6 10.8 %collective-permute-start.7 = (f32[5,32,512]{2,1,0:T(8,128)S(1)}, f32[5,32,512]{2,1,0:T(8,128)S(1)}, u32[]{:S(2)}, u32[]{:S(2)}) collective-permute-start(f32[5,32,512]{2,1,0:T(8,128)S(1)} %add_add_fusion.2), channel_id=1, source_target_pairs={{0,4},{1,5},{2,6},{3,7},{4,0},{5,1},{6,2},{7,3},{8,12},{9,13},{10,... | collective-permute-start | bytes 983048 | tf_op jit(solution)/shard_map/ppermute | solution.py:178
  127.3 11.9 %collective-permute-start.23 = (f32[5,32,512]{2,1,0:T(8,128)S(1)}, f32[5,32,512]{2,1,0:T(8,128)S(1)}, u32[]{:S(2)}, u32[]{:S(2)}) collective-permute-start(f32[5,32,512]{2,1,0:T(8,128)S(1)} %get-tuple-element.48), channel_id=1, source_target_pairs={{0,3},{1,0},{2,1},{3,2},{4,7},{5,4},{6,5},{7,6},{8,11},{9,8},{10,9... | collective-permute-start | bytes 983048 | tf_op jit(solution)/shard_map/ppermute | solution.py:175
  131.1 12.9 %collective-permute-start.16 = (f32[6,32,512]{2,1,0:T(8,128)S(1)}, f32[6,32,512]{2,1,0:T(8,128)S(1)}, u32[]{:S(2)}, u32[]{:S(2)}) collective-permute-start(f32[6,32,512]{2,1,0:T(8,128)S(1)} %get-tuple-element.40), channel_id=1, source_target_pairs={{0,3},{1,0},{2,1},{3,2},{4,7},{5,4},{6,5},{7,6},{8,11},{9,8},{10,9... | collective-permute-start | bytes 1179656 | tf_op jit(solution)/shard_map/ppermute | solution.py:175
  136.7 13.3 %collective-permute-start.15 = (f32[6,32,512]{2,1,0:T(8,128)S(1)}, f32[6,32,512]{2,1,0:T(8,128)S(1)}, u32[]{:S(2)}, u32[]{:S(2)}) collective-permute-start(f32[6,32,512]{2,1,0:T(8,128)S(1)} %add.56), channel_id=1, source_target_pairs={{0,1},{1,2},{2,3},{3,0},{4,5},{5,6},{6,7},{7,4},{8,9},{9,10},{10,1... | collective-permute-start | bytes 1179656 | tf_op jit(solution)/shard_map/ppermute | solution.py:177
  136.7 13.3 %collective-permute-start.20 = (f32[6,32,512]{2,1,0:T(8,128)S(1)}, f32[6,32,512]{2,1,0:T(8,128)S(1)}, u32[]{:S(2)}, u32[]{:S(2)}) collective-permute-start(f32[6,32,512]{2,1,0:T(8,128)S(1)} %add_add_fusion), channel_id=1, source_target_pairs={{0,4},{1,5},{2,6},{3,7},{4,0},{5,1},{6,2},{7,3},{8,12},{9,13},{10,... | collective-permute-start | bytes 1179656 | tf_op jit(solution)/shard_map/ppermute | solution.py:178
  137.4 12.6 %collective-permute-start.22 = (f32[5,32,512]{2,1,0:T(8,128)S(1)}, f32[5,32,512]{2,1,0:T(8,128)S(1)}, u32[]{:S(2)}, u32[]{:S(2)}) collective-permute-start(f32[5,32,512]{2,1,0:T(8,128)S(1)} %add.60), channel_id=1, source_target_pairs={{0,1},{1,2},{2,3},{3,0},{4,5},{5,6},{6,7},{7,4},{8,9},{9,10},{10,1... | collective-permute-start | bytes 983048 | tf_op jit(solution)/shard_map/ppermute | solution.py:177
  139.2 10.9 %collective-permute-start.27 = (f32[5,32,512]{2,1,0:T(8,128)S(1)}, f32[5,32,512]{2,1,0:T(8,128)S(1)}, u32[]{:S(2)}, u32[]{:S(2)}) collective-permute-start(f32[5,32,512]{2,1,0:T(8,128)S(1)} %add_add_fusion.1), channel_id=1, source_target_pairs={{0,4},{1,5},{2,6},{3,7},{4,0},{5,1},{6,2},{7,3},{8,12},{9,13},{10,... | collective-permute-start | bytes 983048 | tf_op jit(solution)/shard_map/ppermute | solution.py:178

commit v2 on v0

v2 whole, which is shorter than its diff:
```python
import functools

import jax
import jax.numpy as jnp
from jax import lax
from jax.experimental import pallas as pl
from jax.experimental.pallas import tpu as pltpu
from jax.sharding import PartitionSpec as P

NPAIR = 4
RING = 4
LOOSE0, LOOSE1, DOWN, UP = range(4)
SHORT = pl.CostEstimate(flops=0, bytes_accessed=0, transcendentals=0)
EARLY = ((0, 0, UP), (0, 0, LOOSE0), (0, 0, LOOSE1), (0, 1, DOWN), (1, 0, LOOSE0))
SIDES = (
    (0, 0, DOWN),
    (1, 0, LOOSE1),
    (1, 0, UP),
    (0, 1, LOOSE0),
    (0, 1, LOOSE1),
    (0, 1, UP),
)
CORNERS = ((1, 1, LOOSE0), (1, 1, LOOSE1), (1, 1, DOWN), (1, 1, UP), (1, 0, DOWN))
BESIDE = ((2, 0), (2, 1))
ABOVE = ((0, 2), (1, 2))
BELOW = ((1, -1),)
CORNER_UP = ((2, 2),)
CORNER_DOWN = ((2, -1),)


def slot_table(offsets):
    dx = [offsets[k, 0] for k in range(NPAIR)]
    dy = [offsets[k, 1] for k in range(NPAIR)]
    code = [
        jnp.where(dx[k] == 0, dy[k], jnp.where(dy[k] == 0, 2, jnp.where(dy[k] < 0, 3, 4)))
        for k in range(NPAIR)
    ]
    rank = [
        sum((code[j] < code[k]).astype(jnp.int32) for j in range(NPAIR) if j != k) for k in range(NPAIR)
    ]

    def pick(values, slot):
        return sum(jnp.where(rank[k] == slot, values[k], 0) for k in range(NPAIR))

    return [(pick(dx, s), pick(dy, s), pick(list(range(NPAIR)), s)) for s in range(NPAIR)]


def store_pieces(outs, place, meta, index, count):
    own_a, own_b, up_first, down_first, up_second, down_second = outs
    x_lo, y = meta[0], meta[1]
    half = place.shape[0] // 2
    rows = half // RING
    target = {
        (0, 0): (own_a, 0),
        (0, 1): (own_b, 0),
        (2, 0): (up_first, 0),
        (1, 1): (up_first, count),
        (2, 1): (down_first, 0),
        (3, 0): (down_first, count),
        (1, 0): (up_second, 0),
        (3, 1): (down_second, 0),
    }
    for (d, h), (ref, base) in target.items():
        start = lax.rem(x_lo + h, 2) * half + lax.rem(y + d, RING) * rows
        ref[base + index] = place[pl.ds(pl.multiple_of(start, rows), rows), :]


def load_tile(left, right, tile, own, parts):
    traces, points = parts[0].shape[-2:]
    for i, part in enumerate(parts):
        re, im = part[0], part[1]
        low = slice(2 * i * traces, (2 * i + 1) * traces)
        high = slice((2 * i + 1) * traces, (2 * i + 2) * traces)
        right[tile, low, :points] = re
        right[tile, high, :points] = im
        right[tile, low, points:] = im
        right[tile, high, points:] = -re
        if own is not None:
            left[own, :, low] = re.T
            left[own, :, high] = im.T


def early_kernel(meta, offsets, token, green, *refs):
    outs, (left, right, acc) = refs[:6], refs[7:]
    refs[6][...] = token[...]
    slots = slot_table(offsets)
    count = 2 * len(EARLY)
    for freq in range(2):
        for tx in range(2):
            for ty in range(2):
                load_tile(left, right, freq * 8 + tx * 4 + ty + 1, freq * 4 + tx * 2 + ty, [green.at[tx, ty, freq]])
    for b, (tx, ty, slot) in enumerate(EARLY):
        dx, dy, _ = slots[slot]
        for freq in range(2):
            place = acc.at[freq]
            tile = freq * 8 + (tx + dx) * 4 + (ty + dy + 1)
            place[...] = jnp.dot(left[freq * 4 + tx * 2 + ty], right[tile], preferred_element_type=jnp.float32)
            store_pieces(outs, place, meta, 2 * b + freq, count)


def late_kernel(group, where, *refs):
    count = 3 + len(where)
    meta, offsets, token = refs[:3]
    outs, (left, right, acc) = refs[count : count + 6], refs[count + 7 :]
    refs[count + 6][...] = token[...]
    sources = {}
    for ref, tiles in zip(refs[3:count], where):
        for i, (tx, ty) in enumerate(tiles):
            sources.setdefault((tx, ty), []).append(ref.at[i])
    for (tx, ty), parts in sources.items():
        own = tx * 2 + ty if tx < 2 and 0 <= ty < 2 else None
        load_tile(left, right, tx * 4 + ty + 1, own, parts)
    slots = slot_table(offsets)
    for b, (tx, ty, slot) in enumerate(group):
        dx, dy, _ = slots[slot]
        tile = (tx + dx) * 4 + (ty + dy + 1)
        place = acc.at[b % 2]
        place[...] = jnp.dot(left[tx * 2 + ty], right[tile], preferred_element_type=jnp.float32)
        store_pieces(outs, place, meta, b, len(group))


def call_blocks(kernel, count, depth, tiles, lefts, points, arrays, token, name):
    meta, offsets, *values = arrays
    smem = pl.BlockSpec(memory_space=pltpu.SMEM)
    vmem = pl.BlockSpec(memory_space=pltpu.VMEM)
    *pieces, token = pl.pallas_call(
        kernel,
        out_shape=[
            jax.ShapeDtypeStruct((pieces * count, points // (2 * RING), 2 * points), jnp.float32)
            for pieces in (1, 1, 2, 2, 1, 1)
        ]
        + [jax.ShapeDtypeStruct(token.shape, token.dtype)],
        in_specs=[smem, smem] + [vmem] * (1 + len(values)),
        out_specs=[vmem] * 7,
        scratch_shapes=[
            pltpu.VMEM((lefts, points, depth), jnp.bfloat16),
            pltpu.VMEM((tiles, depth, 2 * points), jnp.bfloat16),
            pltpu.VMEM((2, points, 2 * points), jnp.float32),
        ],
        compiler_params=pltpu.CompilerParams(vmem_limit_bytes=40 * 1024 * 1024),
        cost_estimate=SHORT,
        name=name,
    )(meta, offsets, token, *values)
    return pieces, token


def call_step(kernel, out_shape, token, arrays, name):
    vmem = pl.BlockSpec(memory_space=pltpu.VMEM)
    *outs, token = pl.pallas_call(
        kernel,
        out_shape=list(out_shape) + [jax.ShapeDtypeStruct(token.shape, token.dtype)],
        in_specs=[vmem] * (1 + len(arrays)),
        out_specs=[vmem] * (1 + len(out_shape)),
        cost_estimate=SHORT,
        name=name,
    )(token, *arrays)
    return outs, token


def swapped_kernel(token, mine, theirs, above_mine, beside, below, above_theirs, out_token):
    for i, part in enumerate((mine, theirs)):
        beside[i] = part[0]
        below[i] = part[1, 1]
    for tx in range(2):
        above_theirs[tx] = theirs[tx, 0]
    out_token[...] = token[...]


def second_kernel(token, up_received, down_received, up_own, down_own, *refs):
    up, down, out_token = refs[-3:]
    count = up_own.shape[0]
    up[...] = up_own[...] + up_received[:count]
    down[...] = down_own[...] + down_received[:count]
    out_token[...] = token[...]


def back_kernel(token, down_arrived, own, up_received, *refs):
    out, out_token = refs[-2:]
    count = own.shape[0]
    out[...] = own[...] + up_received[count:] + down_arrived[...]
    out_token[...] = token[...]


def final_kernel(meta, offsets, *refs):
    out = refs[-1]
    x_lo = meta[0]
    slots = slot_table(offsets)
    for g, group in enumerate((EARLY, SIDES, CORNERS)):
        own, before, after, other = refs[4 * g : 4 * g + 4]
        for b, (tx, ty, slot) in enumerate(group):
            pair = slots[slot][2]
            if g == 0:
                for freq in range(2):
                    i = 2 * b + freq
                    out[tx, ty, pair, freq] = (own[i] + before[i] + after[len(group) * 2 + i]) + other[i]
            else:
                out[tx, ty, pair, x_lo] = own[b] + before[b] + after[len(group) + b]
                out[tx, ty, pair, 1 - x_lo] = other[b]


def final(meta, offsets, parts, token, shape):
    smem = pl.BlockSpec(memory_space=pltpu.SMEM)
    vmem = pl.BlockSpec(memory_space=pltpu.VMEM)
    flat = [part for group in parts for part in group]
    return pl.pallas_call(
        final_kernel,
        out_shape=jax.ShapeDtypeStruct(shape, jnp.float32),
        in_specs=[smem, smem] + [vmem] * (len(flat) + 1),
        out_specs=vmem,
        compiler_params=pltpu.CompilerParams(vmem_limit_bytes=40 * 1024 * 1024),
        name="place_blocks",
    )(meta, offsets, *flat, token)


def per_device(green, offsets):
    points, traces = green.shape[5], green.shape[4]
    gx, gy = lax.axis_size("gx"), lax.axis_size("gy")
    sa = lax.axis_index("sa")
    x_lo, y = sa // RING, sa % RING
    meta = jnp.stack([x_lo, y]).astype(jnp.int32)

    def swap(value):
        return lax.ppermute(value, "sa", [(i, (i + RING) % (2 * RING)) for i in range(2 * RING)])

    def around(value, steps):
        return lax.ppermute(value, "sa", [(h * RING + i, h * RING + (i + steps) % RING) for h in range(2) for i in range(RING)])

    def tiles_from(value, dx, dy):
        perm = [
            ((ix + dx) * gy + iy + dy, ix * gy + iy)
            for ix in range(gx - dx)
            for iy in range(max(0, -dy), min(gy, gy - dy))
        ]
        return lax.ppermute(value, ("gx", "gy"), perm)

    def first(pieces):
        return around(pieces[2], 1), around(pieces[3], -1)

    def second(pieces, received, token, also=()):
        up, down = pieces[4], pieces[5]
        (up, down), token = call_step(second_kernel, [up, down], token, [*received, up, down, *also], "second")
        return (around(up, 1), around(down, -1)), token

    def back(pieces, received, arrived, token):
        own = pieces[1]
        (out,), token = call_step(back_kernel, [own], token, [arrived[1], own, received[0], arrived[0]], "back")
        return swap(out), token

    def blocks(group, inputs, token, name):
        kernel = functools.partial(late_kernel, group, [where for where, _ in inputs])
        arrays = [meta, offsets] + [value for _, value in inputs]
        return call_blocks(kernel, len(group), 4 * traces, 12, 4, points, arrays, token, name)

    token = jnp.zeros((8, 128), jnp.float32)
    theirs = swap(lax.dynamic_index_in_dim(green, 1 - x_lo, 2, keepdims=False))
    mine = lax.dynamic_index_in_dim(green, x_lo, 2, keepdims=False)
    above_mine = tiles_from(mine[:, 0], 0, 1)
    early, token = call_blocks(
        early_kernel, 2 * len(EARLY), 2 * traces, 16, 8, points, [meta, offsets, green], token, "early_blocks"
    )
    early_first = first(early)
    dtype, shape = green.dtype, mine.shape[2:]
    sent = [jax.ShapeDtypeStruct(lead + shape, dtype) for lead in ((2, 2), (2,), (2,))]
    sent, token = call_step(swapped_kernel, sent, token, [mine, theirs, above_mine], "swapped")
    above_theirs = tiles_from(sent[2], 0, 1)
    beside = tiles_from(sent[0], 1, 0)
    below = tiles_from(sent[1], 0, -1)
    corner_up = tiles_from(beside[:, 0], 0, 1)
    corner_down = tiles_from(beside[:, 1], 0, -1)
    own = ((0, 0), (0, 1), (1, 0), (1, 1))
    tiles = [(own, mine.reshape(4, *shape)), (own, theirs.reshape(4, *shape))]
    early_second, token = second(early, early_first, token)
    tiles += [(BESIDE, beside[0]), (BESIDE, beside[1]), (BELOW, below[:1]), (BELOW, below[1:])]
    tiles += [(ABOVE, above_mine), (ABOVE, above_theirs)]
    sides, token = blocks(SIDES, tiles, token, "side_blocks")
    sides_first = first(sides)
    early_back, token = back(early, early_first, early_second, token)
    tiles += [(CORNER_UP, corner_up[:1]), (CORNER_UP, corner_up[1:])]
    tiles += [(CORNER_DOWN, corner_down[:1]), (CORNER_DOWN, corner_down[1:])]
    corners, token = blocks(CORNERS, tiles, token, "corner_blocks")
    corners_first = first(corners)
    sides_second, token = second(sides, sides_first, token, [early_back])
    corners_second, token = second(corners, corners_first, token)
    sides_back, token = back(sides, sides_first, sides_second, token)
    corners_back, token = back(corners, corners_first, corners_second, token)
    parts = [
        (early[0], early_second[0], early_first[1], early_back),
        (sides[0], sides_second[0], sides_first[1], sides_back),
        (corners[0], corners_second[0], corners_first[1], corners_back),
    ]
    shape = green.shape[:2] + (NPAIR, green.shape[2], points // (2 * RING), 2 * points)
    return final(meta, offsets, parts, token, shape)


def solution(mesh):
    return jax.shard_map(
        per_device,
        mesh=mesh,
        in_specs=(P("gx", "gy", None, None, "sa", None), P()),
        out_specs=P("gx", "gy", None, None, "sa", None),
        check_vma=False,
    )
```

time: 338 us -> 150 us (0.44)
  waiting for transfers between devices: 198 us -> 37.7 us
  Pallas kernels: 0 us -> 34.6 us
  starting transfers between devices: 8.87 us -> 41.4 us
  local copies, waits for them, and re-layouts: 61.2 us -> 34.1 us
  between operations: 26 us -> 0.26 us
  matrix products: 23 us -> 0 us
  other arithmetic: 17.6 us -> 0.07 us
    reduce_scatter x1 -> x0, waiting for transfers between devices: 173 us -> none  [per_device(): return lax.psum_scatter(terms, 'sa', scatter_dimension=4, tiled=True)]
    pallas_call x0 -> x11, Pallas kernels: none -> 34.6 us  [the longest x7 18.9 us: call_step(): pl.pallas_call(kernel, out_shape=list(out_shape) + [jax.ShapeDtypeStruct(...]
    ppermute x3 -> x22, starting transfers between devices: 8.87 us -> 41.4 us  [the longest x12 19.4 us: around(): lax.ppermute(value, 'sa', [(h * RING + i, h * RING + (i + steps) % RING)...]
    unnamed x11 -> x87, local copies, waits for them, and re-layouts: 1.75 us -> 25.7 us
    dot_general x4 -> x0, matrix products: 23 us -> none  [pair_term(): jnp.einsum('nsp,nsq->npq', left, right, preferred_element_type=jnp.float32)]
    another operation x4 -> x0, local copies, waits for them, and re-layouts: 21 us -> none  [per_device(): terms = jnp.stack([pair_term(index) for index in range(NPAIR)], axis=2)]
    reshape x4 -> x0, local copies, waits for them, and re-layouts: 14.4 us -> none  [pair_term(): real_rows = beside.reshape(count, 2 * traces, points)]
    ppermute x3 -> x22, waiting for transfers between devices: 25.4 us -> 37.7 us  [the longest x12 21.2 us: around(): lax.ppermute(value, 'sa', [(h * RING + i, h * RING + (i + steps) % RING)...]
  transfers between devices with their start and end apart: 4 -> 22, of which waited for: 4 -> 8; matrix products, arithmetic and copies ran while one was open for 1% -> 5% of each run, Pallas kernels for 0% -> 21%
where the time goes in v2:
time: 150 us; the launch traced here: 148 us
  starting transfers between devices  41.4 us (28%)
  waiting for transfers between devices  37.7 us (25%)
  Pallas kernels  34.6 us (23%)
  local copies, waits for them, and re-layouts  34.1 us (23%)
    unnamed x87, local copies, waits for them, and re-layouts  25.7 us
    ppermute x12, waiting for transfers between devices, around(): lax.ppermute(value, 'sa', [(h * RING + i, h * RING + (i + steps) % RING)...  21.2 us
    ppermute x12, starting transfers between devices, around(): lax.ppermute(value, 'sa', [(h * RING + i, h * RING + (i + steps) % RING)...  19.4 us
    pallas_call x7, Pallas kernels, call_step(): pl.pallas_call(kernel, out_shape=list(out_shape) + [jax.ShapeDtypeStruct(...  18.9 us
    ppermute x6, starting transfers between devices, tiles_from(): return lax.ppermute(value, ('gx', 'gy'), perm)  17.8 us
    ppermute x4, waiting for transfers between devices, swap(): lax.ppermute(value, 'sa', [(i, (i + RING) % (2 * RING)) for i in range(2...  14.6 us
    pallas_call x3, Pallas kernels, call_blocks(): pl.pallas_call(kernel, out_shape=[jax.ShapeDtypeStruct((pieces * count, p...  12.4 us
    ppermute x4, starting transfers between devices, swap(): lax.ppermute(value, 'sa', [(i, (i + RING) % (2 * RING)) for i in range(2...  4.14 us
  transfers between devices with their start and end apart: 22, of which 8 were waited for; matrix products, arithmetic and copies ran while one was open for 5% of the time, Pallas kernels for 21%

profile of v2, /device:TPU:100, one launch (start us, length us, event | category | flops | bytes accessed | tf_op | source)
XLA Modules:
  0.0 148.2 jit_solution(12292761640223468729)
XLA Ops:
  0.0 1.7 %dynamic-slice_bitcast_fusion = (bf16[2,2,2,256,256]{4,3,2,1,0:T(8,128)(2,1)S(1)}, bf16[2,2,1,2,256,256]{5,4,3,2,1,0:T(8,128)(2,1)S(1)}) fusion(bf16[2,2,2,2,256,256]{5,4,3,2,1,0:T(8,128)(2,1)} %green.1, s32[]{:T(128)S(6)} %select_n.21, s32[]{:T(128)S(6)} %select_n.20), kind=kLoop, calls=%fused_computation.1 | loop fusion | bytes 4194312 | tf_op jit(solution)/shard_map/jit(dynamic_index_in_dim)/squeeze | solution.py:255
  1.7 1.3 collective-permute-start
  3.0 0.9 slice_bitcast_fusion.4
  3.9 2.0 %collective-permute-start.1 = (bf16[2,2,256,256]{3,2,1,0:T(8,128)(2,1)}, bf16[2,2,256,256]{3,2,1,0:T(8,128)(2,1)}, u32[]{:S(2)}, u32[]{:S(2)}) collective-permute-start(bf16[2,2,256,256]{3,2,1,0:T(8,128)(2,1)} %slice_bitcast_fusion.4), channel_id=1, source_target_pairs={{8,0},{16,8},{24,16},{32,24},{40,32},{48,40},{56,48},{72,64},{80,7... | collective-permute-start | bytes 1572872 | tf_op jit(solution)/shard_map/ppermute | solution.py:234
  6.1 1.6 %copy-done.4 = bf16[2,2,2,2,256,256]{5,4,3,2,1,0:T(8,128)(2,1)S(1)} copy-done((bf16[2,2,2,2,256,256]{5,4,3,2,1,0:T(8,128)(2,1)S(1)}, bf16[2,2,2,2,256,256]{5,4,3,2,1,0:T(8,128)(2,1)}, u32[]{:S(2)}) %copy-start.4) | copy-done | bytes 2097176
  7.7 4.0 %early_blocks.1 = (f32[10,32,512]{2,1,0:T(8,128)S(1)}, f32[10,32,512]{2,1,0:T(8,128)S(1)}, f32[20,32,512]{2,1,0:T(8,128)}, f32[20,32,512]{2,1,0:T(8,128)}, f32[1...) custom-call(s32[2]{0:T(128)S(1)} %pad_add_fusion.meta.refs_0_, ...), custom_call_target="tpu_custom_call" | custom-call | tf_op jit(solution)/shard_map/early_blocks/pallas_call | solution.py:126
  11.7 0.8 copy-done.15
  12.5 0.9 copy-done.17
  13.4 0.8 copy-done.18
  14.2 0.9 copy-done.19
  15.7 1.6 %collective-permute-start.2 = (f32[20,32,512]{2,1,0:T(8,128)}, f32[20,32,512]{2,1,0:T(8,128)}, u32[]{:S(2)}, u32[]{:S(2)}) collective-permute-start(f32[20,32,512]{2,1,0:T(8,128)} %get-tuple-element.48), channel_id=1, source_target_pairs={{0,1},{1,2},{2,3},{3,0},{4,5},{5,6},{6,7},{7,4},{8,9},{9,10},{10,1... | collective-permute-start | bytes 3932168 | tf_op jit(solution)/shard_map/ppermute | solution.py:226
  17.3 1.7 %collective-permute-start.3 = (f32[20,32,512]{2,1,0:T(8,128)}, f32[20,32,512]{2,1,0:T(8,128)S(1)}, u32[]{:S(2)}, u32[]{:S(2)}) collective-permute-start(f32[20,32,512]{2,1,0:T(8,128)} %get-tuple-element.49), channel_id=1, source_target_pairs={{0,3},{1,0},{2,1},{3,2},{4,7},{5,4},{6,5},{7,6},{8,11},{9,8},{10,9... | collective-permute-start | bytes 3932168 | tf_op jit(solution)/shard_map/ppermute | solution.py:226
  18.9 2.0 %collective-permute-done.1.above_mine.refs_9_ = bf16[2,2,256,256]{3,2,1,0:T(8,128)(2,1)} collective-permute-done((bf16[2,2,256,256]{3,2,1,0:T(8,128)(2,1)}, bf16[2,2,256,256]{3,2,1,0:T(8,128)(2,1)}, u32[]{:S(2)}, u32[]{:S(2)}) %collective-permute-start.1) | collective-permute-done | bytes 524320 | tf_op jit(solution)/shard_map/ppermute | solution.py:234
  20.9 5.8 %collective-permute-done.theirs = bf16[2,2,2,256,256]{4,3,2,1,0:T(8,128)(2,1)S(1)} collective-permute-done((bf16[2,2,2,256,256]{4,3,2,1,0:T(8,128)(2,1)S(1)}, bf16[2,2,2,256,256]{4,3,2,1,0:T(8,128)(2,1)S(1)}, u32[]{:S(2)}, u32[]{:S(2)}) %collective-permute-start) | collective-permute-done | bytes 1048608 | tf_op jit(solution)/shard_map/ppermute | solution.py:223
  26.7 1.0 copy-done.2
  27.7 3.1 %swapped.1 = (bf16[2,2,2,256,256]{4,3,2,1,0:T(8,128)(2,1)}, bf16[2,2,256,256]{3,2,1,0:T(8,128)(2,1)}, bf16[2,2,256,256]{3,2,1,0:T(8,128)(2,1)}, f32[8,128]{1,0:T(8,128)}) custom-call(f32[8,128]{1,0:T(8,128)} %copy-done.33, bf16[2,2,2,256,256]{4,3,2,1,0:T(8,128)(2,1)} %bitcast.20, bf16[2,2,2,256,256]{4,3,2,1,0:T(8,128)(2,1)} %copy-done.2, ...), custom_call_target="tpu_custom_call" | custom-call | tf_op jit(solution)/shard_map/swapped/pallas_call | solution.py:149
  30.8 1.3 copy.6
  32.1 1.9 %collective-permute-start.5 = (bf16[2,2,2,256,256]{4,3,2,0,1:T(8,128)(2,1)S(1)}, bf16[2,2,2,256,256]{4,3,2,0,1:T(8,128)(2,1)S(1)}, u32[]{:S(2)}, u32[]{:S(2)}) collective-permute-start(bf16[2,2,2,256,256]{4,3,2,0,1:T(8,128)(2,1)S(1)} %copy.6), channel_id=1, source_target_pairs={{64,0},{72,8},{80,16},{88,24},{96,32},{104,40},{112,48},{120,56},{... | collective-permute-start | bytes 3145736 | tf_op jit(solution)/shard_map/ppermute | solution.py:234
  34.0 5.0 %collective-permute-start.6 = (bf16[2,2,256,256]{3,2,1,0:T(8,128)(2,1)}, bf16[2,2,256,256]{3,2,1,0:T(8,128)(2,1)}, u32[]{:S(2)}, u32[]{:S(2)}) collective-permute-start(bf16[2,2,256,256]{3,2,1,0:T(8,128)(2,1)} %get-tuple-element.55), channel_id=1, source_target_pairs={{0,8},{8,16},{16,24},{24,32},{32,40},{40,48},{48,56},{64,72},{72,8... | collective-permute-start | bytes 1572872 | tf_op jit(solution)/shard_map/ppermute | solution.py:234
  39.0 1.9 %collective-permute-start.7 = (bf16[2,2,256,256]{3,2,1,0:T(8,128)(2,1)}, bf16[2,2,256,256]{3,2,1,0:T(8,128)(2,1)}, u32[]{:S(2)}, u32[]{:S(2)}) collective-permute-start(bf16[2,2,256,256]{3,2,1,0:T(8,128)(2,1)} %get-tuple-element.56), channel_id=1, source_target_pairs={{8,0},{16,8},{24,16},{32,24},{40,32},{48,40},{56,48},{72,64},{80,7... | collective-permute-start | bytes 1572872 | tf_op jit(solution)/shard_map/ppermute | solution.py:234
  41.0 6.5 %collective-permute-done.2.up_received = f32[20,32,512]{2,1,0:T(8,128)} collective-permute-done((f32[20,32,512]{2,1,0:T(8,128)}, f32[20,32,512]{2,1,0:T(8,128)}, u32[]{:S(2)}, u32[]{:S(2)}) %collective-permute-start.2) | collective-permute-done | bytes 1310752 | tf_op jit(solution)/shard_map/ppermute | solution.py:226
  47.4 1.1 copy-done.5
  48.5 3.3 %second.3 = (f32[10,32,512]{2,1,0:T(8,128)}, f32[10,32,512]{2,1,0:T(8,128)}, f32[8,128]{1,0:T(8,128)}) custom-call(f32[8,128]{1,0:T(8,128)} %get-tuple-element.47.token, f32[20,32,512]{2,1,0:T(8,128)} %collective-permute-done.2.up_received, f32[20,32,512]{2,1,0:T(8,128)} %copy-done.5, f32[10,32,512]{2,1,0:T(8,128)} %copy-done.18, f32[10,32,512]{2,1,0:T(8,128)} %copy-done.19), custom_call_target="tpu_custom_call" | custom-call | tf_op jit(solution)/shard_map/second/pallas_call | solution.py:149
  51.8 1.5 %collective-permute-start.4 = (f32[10,32,512]{2,1,0:T(8,128)}, f32[10,32,512]{2,1,0:T(8,128)}, u32[]{:S(2)}, u32[]{:S(2)}) collective-permute-start(f32[10,32,512]{2,1,0:T(8,128)} %get-tuple-element.52), channel_id=1, source_target_pairs={{0,1},{1,2},{2,3},{3,0},{4,5},{5,6},{6,7},{7,4},{8,9},{9,10},{10,1... | collective-permute-start | bytes 1966088 | tf_op jit(solution)/shard_map/ppermute | solution.py:226
  53.3 1.7 %collective-permute-start.8 = (f32[10,32,512]{2,1,0:T(8,128)}, f32[10,32,512]{2,1,0:T(8,128)}, u32[]{:S(2)}, u32[]{:S(2)}) collective-permute-start(f32[10,32,512]{2,1,0:T(8,128)} %get-tuple-element.58), channel_id=1, source_target_pairs={{0,3},{1,0},{2,1},{3,2},{4,7},{5,4},{6,5},{7,6},{8,11},{9,8},{10,9... | collective-permute-start | bytes 1966088 | tf_op jit(solution)/shard_map/ppermute | solution.py:226
  55.0 1.1 slice_bitcast_fusion
  56.2 5.0 %collective-permute-start.11 = (bf16[2,2,256,256]{3,2,1,0:T(8,128)(2,1)}, bf16[2,2,256,256]{3,2,1,0:T(8,128)(2,1)}, u32[]{:S(2)}, u32[]{:S(2)}) collective-permute-start(bf16[2,2,256,256]{3,2,1,0:T(8,128)(2,1)} %get-tuple-element.87), channel_id=1, source_target_pairs={{0,8},{8,16},{16,24},{24,32},{32,40},{40,48},{48,56},{64,72},{72,8... | collective-permute-start | bytes 1572872 | tf_op jit(solution)/shard_map/ppermute | solution.py:234
  61.2 1.9 %collective-permute-start.10 = (bf16[2,2,256,256]{3,2,1,0:T(8,128)(2,1)}, bf16[2,2,256,256]{3,2,1,0:T(8,128)(2,1)}, u32[]{:S(2)}, u32[]{:S(2)}) collective-permute-start(bf16[2,2,256,256]{3,2,1,0:T(8,128)(2,1)} %get-tuple-element.88), channel_id=1, source_target_pairs={{8,0},{16,8},{24,16},{32,24},{40,32},{48,40},{56,48},{72,64},{80,7... | collective-permute-start | bytes 1572872 | tf_op jit(solution)/shard_map/ppermute | solution.py:234
  63.2 1.2 fusion.2
  64.6 1.2 copy-done.1
  66.2 3.7 %side_blocks.1 = (f32[6,32,512]{2,1,0:T(8,128)S(1)}, f32[6,32,512]{2,1,0:T(8,128)S(1)}, f32[12,32,512]{2,1,0:T(8,128)S(1)}, f32[12,32,512]{2,1,0:T(8,128)S(1)}, ...) custom-call(s32[2]{0:T(128)S(1)} %pad_add_fusion.meta.refs_0_, ...), custom_call_target="tpu_custom_call" | custom-call | tf_op jit(solution)/shard_map/side_blocks/pallas_call | solution.py:126
  69.9 0.8 copy-done.20
  70.6 0.7 copy-done.22
  71.4 0.7 copy-done.23
  73.5 0.9 copy-done.36
  74.3 0.9 copy-done.37
  75.2 2.8 %back.3 = (f32[10,32,512]{2,1,0:T(8,128)}, f32[8,128]{1,0:T(8,128)}) custom-call(f32[8,128]{1,0:T(8,128)} %copy-done.34, f32[10,32,512]{2,1,0:T(8,128)} %collective-permute-done.8.down_arrived, f32[10,32,512]{2,1,0:T(8,128)} %copy-done.17, f32[20,32,512]{2,1,0:T(8,128)} %collective-permute-done.2.up_received, ...), custom_call_target="tpu_custom_call" | custom-call | tf_op jit(solution)/shard_map/back/pallas_call | solution.py:149
  78.1 0.8 collective-permute-start.9
  79.2 3.0 %collective-permute-start.13 = (f32[12,32,512]{2,1,0:T(8,128)}, f32[12,32,512]{2,1,0:T(8,128)}, u32[]{:S(2)}, u32[]{:S(2)}) collective-permute-start(f32[12,32,512]{2,1,0:T(8,128)} %copy-done.36), channel_id=1, source_target_pairs={{0,3},{1,0},{2,1},{3,2},{4,7},{5,4},{6,5},{7,6},{8,11},{9,8},{10,9... | collective-permute-start | bytes 2359304 | tf_op jit(solution)/shard_map/ppermute | solution.py:226
  82.2 1.1 fusion
  83.2 1.1 fusion.1
  84.3 4.7 %corner_blocks.1 = (f32[5,32,512]{2,1,0:T(8,128)S(1)}, f32[5,32,512]{2,1,0:T(8,128)S(1)}, f32[10,32,512]{2,1,0:T(8,128)}, f32[10,32,512]{2,1,0:T(8,128)}, f32[5,...) custom-call(s32[2]{0:T(128)S(1)} %pad_add_fusion.meta.refs_0_, ...), custom_call_target="tpu_custom_call" | custom-call | tf_op jit(solution)/shard_map/corner_blocks/pallas_call | solution.py:126
  89.1 0.8 copy-done.25
  89.8 0.7 copy-done.27
  92.6 3.2 %collective-permute-start.16 = (f32[10,32,512]{2,1,0:T(8,128)}, f32[10,32,512]{2,1,0:T(8,128)S(1)}, u32[]{:S(2)}, u32[]{:S(2)}) collective-permute-start(f32[10,32,512]{2,1,0:T(8,128)} %get-tuple-element.71), channel_id=1, source_target_pairs={{0,3},{1,0},{2,1},{3,2},{4,7},{5,4},{6,5},{7,6},{8,11},{9,8},{10,9... | collective-permute-start | bytes 1966088 | tf_op jit(solution)/shard_map/ppermute | solution.py:226
  95.8 5.1 %collective-permute-done.12.up_received = f32[12,32,512]{2,1,0:T(8,128)} collective-permute-done((f32[12,32,512]{2,1,0:T(8,128)}, f32[12,32,512]{2,1,0:T(8,128)}, u32[]{:S(2)}, u32[]{:S(2)}) %collective-permute-start.12) | collective-permute-done | bytes 786464 | tf_op jit(solution)/shard_map/ppermute | solution.py:226
  100.9 2.7 %second.4 = (f32[6,32,512]{2,1,0:T(8,128)}, f32[6,32,512]{2,1,0:T(8,128)}, f32[8,128]{1,0:T(8,128)}) custom-call(f32[8,128]{1,0:T(8,128)} %copy-done.31, f32[12,32,512]{2,1,0:T(8,128)} %collective-permute-done.12.up_received, f32[12,32,512]{2,1,0:T(8,128)} %collective-permute-done.13.down_received.refs_6_, f32[6,32,512]{2,1,0:T(8,128)} %copy-done.23, ...), custom_call_target="tpu_custom_call" | custom-call | tf_op jit(solution)/shard_map/second/pallas_call | solution.py:149
  104.0 2.9 %collective-permute-start.17 = (f32[6,32,512]{2,1,0:T(8,128)}, f32[6,32,512]{2,1,0:T(8,128)S(1)}, u32[]{:S(2)}, u32[]{:S(2)}) collective-permute-start(f32[6,32,512]{2,1,0:T(8,128)} %get-tuple-element.75), channel_id=1, source_target_pairs={{0,3},{1,0},{2,1},{3,2},{4,7},{5,4},{6,5},{7,6},{8,11},{9,8},{10,9... | collective-permute-start | bytes 1179656 | tf_op jit(solution)/shard_map/ppermute | solution.py:226
  106.9 7.9 %collective-permute-done.15.up_received = f32[10,32,512]{2,1,0:T(8,128)S(1)} collective-permute-done((f32[10,32,512]{2,1,0:T(8,128)}, f32[10,32,512]{2,1,0:T(8,128)S(1)}, u32[]{:S(2)}, u32[]{:S(2)}) %collective-permute-start.15) | collective-permute-done | bytes 655392 | tf_op jit(solution)/shard_map/ppermute | solution.py:226
  114.9 0.8 copy-done.40
  116.0 2.4 %second.5 = (f32[5,32,512]{2,1,0:T(8,128)}, f32[5,32,512]{2,1,0:T(8,128)}, f32[8,128]{1,0:T(8,128)}) custom-call(f32[8,128]{1,0:T(8,128)} %get-tuple-element.69.token, f32[10,32,512]{2,1,0:T(8,128)} %copy-done.40, f32[10,32,512]{2,1,0:T(8,128)} %copy-done.7, f32[5,32,512]{2,1,0:T(8,128)} %copy-done.28, f32[5,32,512]{2,1,0:T(8,128)} %copy-done.29), custom_call_target="tpu_custom_call" | custom-call | tf_op jit(solution)/shard_map/second/pallas_call | solution.py:149
  118.5 3.1 %collective-permute-start.20 = (f32[5,32,512]{2,1,0:T(8,128)}, f32[5,32,512]{2,1,0:T(8,128)}, u32[]{:S(2)}, u32[]{:S(2)}) collective-permute-start(f32[5,32,512]{2,1,0:T(8,128)} %get-tuple-element.81), channel_id=1, source_target_pairs={{0,3},{1,0},{2,1},{3,2},{4,7},{5,4},{6,5},{7,6},{8,11},{9,8},{10,9... | collective-permute-start | bytes 983048 | tf_op jit(solution)/shard_map/ppermute | solution.py:226
  121.6 1.7 %collective-permute-done.14.refs_0_.refs_5_ = f32[6,32,512]{2,1,0:T(8,128)S(1)} collective-permute-done((f32[6,32,512]{2,1,0:T(8,128)}, f32[6,32,512]{2,1,0:T(8,128)S(1)}, u32[]{:S(2)}, u32[]{:S(2)}) %collective-permute-start.14) | collective-permute-done | bytes 393248 | tf_op jit(solution)/shard_map/ppermute | solution.py:226
  124.1 2.4 %back.4 = (f32[6,32,512]{2,1,0:T(8,128)}, f32[8,128]{1,0:T(8,128)}) custom-call(f32[8,128]{1,0:T(8,128)} %get-tuple-element.74.token, f32[6,32,512]{2,1,0:T(8,128)} %copy-done.41, f32[6,32,512]{2,1,0:T(8,128)} %copy-done.22, f32[12,32,512]{2,1,0:T(8,128)} %collective-permute-done.12.up_received, f32[6,32,512]{2,1,0:T(8,128)} %copy-done.11), custom_call_target="tpu_custom_call" | custom-call | tf_op jit(solution)/shard_map/back/pallas_call | solution.py:149
  126.5 1.2 collective-permute-start.18
  128.4 2.2 %back.5 = (f32[5,32,512]{2,1,0:T(8,128)}, f32[8,128]{1,0:T(8,128)}) custom-call(f32[8,128]{1,0:T(8,128)} %get-tuple-element.80.token, f32[5,32,512]{2,1,0:T(8,128)} %collective-permute-done.20.down_arrived, f32[5,32,512]{2,1,0:T(8,128)} %copy-done.27, f32[10,32,512]{2,1,0:T(8,128)} %copy-done.40, f32[5,32,512]{2,1,0:T(8,128)} %copy-done.13), custom_call_target="tpu_custom_call" | custom-call | tf_op jit(solution)/shard_map/back/pallas_call | solution.py:149
  130.6 0.8 collective-permute-start.21
  131.5 5.3 %collective-permute-done.18.refs_7_ = f32[6,32,512]{2,1,0:T(8,128)S(1)} collective-permute-done((f32[6,32,512]{2,1,0:T(8,128)}, f32[6,32,512]{2,1,0:T(8,128)S(1)}, u32[]{:S(2)}, u32[]{:S(2)}) %collective-permute-start.18) | collective-permute-done | bytes 393248 | tf_op jit(solution)/shard_map/ppermute | solution.py:223
  136.8 3.5 %collective-permute-done.21.refs_11_ = f32[5,32,512]{2,1,0:T(8,128)S(1)} collective-permute-done((f32[5,32,512]{2,1,0:T(8,128)}, f32[5,32,512]{2,1,0:T(8,128)S(1)}, u32[]{:S(2)}, u32[]{:S(2)}) %collective-permute-start.21) | collective-permute-done | bytes 327712 | tf_op jit(solution)/shard_map/ppermute | solution.py:223
  140.3 1.0 copy-done.12
  141.3 1.0 copy-done.14
  142.3 1.0 copy-done.21
  143.3 1.0 copy-done.26
  144.9 3.3 %place_blocks.1 = f32[2,2,4,2,32,512]{5,4,3,2,1,0:T(8,128)} custom-call(s32[2]{0:T(128)S(1)} %pad_add_fusion.meta.refs_0_, s32[4,2]{1,0:T(4,128)S(1)} %copy.9.offsets.refs_1_, f32[10,32,512]{2,1,0:T(8,128)S(1)} %copy-done.16, f32[10,32,512]{2,1,0:T(8,128)} %collective-permute-done.4.refs_0_.refs_1_, f32[20,32,512]{2,1,0:T(8,128)S(1)} %copy-done.6, ...), custom_call_target="tpu_custom_call" | custom-call | tf_op jit(solution)/shard_map/place_blocks/pallas_call | solution.py:205
  (89 shorter events, 8.2 us)
Async XLA Ops:
  1.7 2.2 %copy-start = (bf16[2,2,1,2,256,256]{5,4,3,2,1,0:T(8,128)(2,1)}, bf16[2,2,1,2,256,256]{5,4,3,2,1,0:T(8,128)(2,1)S(1)}, u32[]{:S(2)}) copy-start(bf16[2,2,1,2,256,256]{5,4,3,2,1,0:T(8,128)(2,1)S(1)} %get-tuple-element.86) | copy-start | bytes 3145732
  1.7 25.0 %collective-permute-start = (bf16[2,2,2,256,256]{4,3,2,1,0:T(8,128)(2,1)S(1)}, bf16[2,2,2,256,256]{4,3,2,1,0:T(8,128)(2,1)S(1)}, u32[]{:S(2)}, u32[]{:S(2)}) collective-permute-start(bf16[2,2,2,256,256]{4,3,2,1,0:T(8,128)(2,1)S(1)} %get-tuple-element.85), channel_id=1, source_target_pairs={{0,4},{1,5},{2,6},{3,7},{4,0},{5,1},{6,2},{7,3},{8,12},{9,13},{10,... | collective-permute-start | bytes 3145736 | tf_op jit(solution)/shard_map/ppermute | solution.py:223
  3.0 3.0 %copy-start.42 = (s32[4,2]{0,1:T(2,128)S(1)}, s32[4,2]{0,1:T(2,128)}, u32[]{:S(2)}) copy-start(s32[4,2]{0,1:T(2,128)} %param.3) | copy-start | bytes 100
  3.9 17.0 %collective-permute-start.1 = (bf16[2,2,256,256]{3,2,1,0:T(8,128)(2,1)}, bf16[2,2,256,256]{3,2,1,0:T(8,128)(2,1)}, u32[]{:S(2)}, u32[]{:S(2)}) collective-permute-start(bf16[2,2,256,256]{3,2,1,0:T(8,128)(2,1)} %slice_bitcast_fusion.4), channel_id=1, source_target_pairs={{8,0},{16,8},{24,16},{32,24},{40,32},{48,40},{56,48},{72,64},{80,7... | collective-permute-start | bytes 1572872 | tf_op jit(solution)/shard_map/ppermute | solution.py:234
  6.1 1.6 %copy-start.4 = (bf16[2,2,2,2,256,256]{5,4,3,2,1,0:T(8,128)(2,1)S(1)}, bf16[2,2,2,2,256,256]{5,4,3,2,1,0:T(8,128)(2,1)}, u32[]{:S(2)}) copy-start(bf16[2,2,2,2,256,256]{5,4,3,2,1,0:T(8,128)(2,1)} %green.1) | copy-start | bytes 6291460
  11.7 0.8 copy-start.15
  12.5 0.9 copy-start.17
  13.4 0.8 copy-start.18
  14.2 0.9 copy-start.19
  15.1 0.6 copy-start.33
  15.7 31.7 %collective-permute-start.2 = (f32[20,32,512]{2,1,0:T(8,128)}, f32[20,32,512]{2,1,0:T(8,128)}, u32[]{:S(2)}, u32[]{:S(2)}) collective-permute-start(f32[20,32,512]{2,1,0:T(8,128)} %get-tuple-element.48), channel_id=1, source_target_pairs={{0,1},{1,2},{2,3},{3,0},{4,5},{5,6},{6,7},{7,4},{8,9},{9,10},{10,1... | collective-permute-start | bytes 3932168 | tf_op jit(solution)/shard_map/ppermute | solution.py:226
  17.3 30.2 %collective-permute-start.3 = (f32[20,32,512]{2,1,0:T(8,128)}, f32[20,32,512]{2,1,0:T(8,128)S(1)}, u32[]{:S(2)}, u32[]{:S(2)}) collective-permute-start(f32[20,32,512]{2,1,0:T(8,128)} %get-tuple-element.49), channel_id=1, source_target_pairs={{0,3},{1,0},{2,1},{3,2},{4,7},{5,4},{6,5},{7,6},{8,11},{9,8},{10,9... | collective-permute-start | bytes 3932168 | tf_op jit(solution)/shard_map/ppermute | solution.py:226
  26.7 1.0 copy-start.2
  32.1 23.0 %collective-permute-start.5 = (bf16[2,2,2,256,256]{4,3,2,0,1:T(8,128)(2,1)S(1)}, bf16[2,2,2,256,256]{4,3,2,0,1:T(8,128)(2,1)S(1)}, u32[]{:S(2)}, u32[]{:S(2)}) collective-permute-start(bf16[2,2,2,256,256]{4,3,2,0,1:T(8,128)(2,1)S(1)} %copy.6), channel_id=1, source_target_pairs={{64,0},{72,8},{80,16},{88,24},{96,32},{104,40},{112,48},{120,56},{... | collective-permute-start | bytes 3145736 | tf_op jit(solution)/shard_map/ppermute | solution.py:234
  34.0 27.2 %collective-permute-start.6 = (bf16[2,2,256,256]{3,2,1,0:T(8,128)(2,1)}, bf16[2,2,256,256]{3,2,1,0:T(8,128)(2,1)}, u32[]{:S(2)}, u32[]{:S(2)}) collective-permute-start(bf16[2,2,256,256]{3,2,1,0:T(8,128)(2,1)} %get-tuple-element.55), channel_id=1, source_target_pairs={{0,8},{8,16},{16,24},{24,32},{32,40},{40,48},{48,56},{64,72},{72,8... | collective-permute-start | bytes 1572872 | tf_op jit(solution)/shard_map/ppermute | solution.py:234
  39.0 25.6 %collective-permute-start.7 = (bf16[2,2,256,256]{3,2,1,0:T(8,128)(2,1)}, bf16[2,2,256,256]{3,2,1,0:T(8,128)(2,1)}, u32[]{:S(2)}, u32[]{:S(2)}) collective-permute-start(bf16[2,2,256,256]{3,2,1,0:T(8,128)(2,1)} %get-tuple-element.56), channel_id=1, source_target_pairs={{8,0},{16,8},{24,16},{32,24},{40,32},{48,40},{56,48},{72,64},{80,7... | collective-permute-start | bytes 1572872 | tf_op jit(solution)/shard_map/ppermute | solution.py:234
  47.4 1.1 copy-start.5
  51.8 23.5 %collective-permute-start.4 = (f32[10,32,512]{2,1,0:T(8,128)}, f32[10,32,512]{2,1,0:T(8,128)}, u32[]{:S(2)}, u32[]{:S(2)}) collective-permute-start(f32[10,32,512]{2,1,0:T(8,128)} %get-tuple-element.52), channel_id=1, source_target_pairs={{0,1},{1,2},{2,3},{3,0},{4,5},{5,6},{6,7},{7,4},{8,9},{9,10},{10,1... | collective-permute-start | bytes 1966088 | tf_op jit(solution)/shard_map/ppermute | solution.py:226
  53.3 22.0 %collective-permute-start.8 = (f32[10,32,512]{2,1,0:T(8,128)}, f32[10,32,512]{2,1,0:T(8,128)}, u32[]{:S(2)}, u32[]{:S(2)}) collective-permute-start(f32[10,32,512]{2,1,0:T(8,128)} %get-tuple-element.58), channel_id=1, source_target_pairs={{0,3},{1,0},{2,1},{3,2},{4,7},{5,4},{6,5},{7,6},{8,11},{9,8},{10,9... | collective-permute-start | bytes 1966088 | tf_op jit(solution)/shard_map/ppermute | solution.py:226
  55.0 6.2 %copy-start.38 = (bf16[2,2,2,256,256]{4,3,2,0,1:T(8,128)(2,1)}, bf16[2,2,2,256,256]{4,3,2,0,1:T(8,128)(2,1)S(1)}, u32[]{:S(2)}) copy-start(bf16[2,2,2,256,256]{4,3,2,0,1:T(8,128)(2,1)S(1)} %collective-permute-done.5) | copy-start | bytes 3145732
  56.2 26.0 %collective-permute-start.11 = (bf16[2,2,256,256]{3,2,1,0:T(8,128)(2,1)}, bf16[2,2,256,256]{3,2,1,0:T(8,128)(2,1)}, u32[]{:S(2)}, u32[]{:S(2)}) collective-permute-start(bf16[2,2,256,256]{3,2,1,0:T(8,128)(2,1)} %get-tuple-element.87), channel_id=1, source_target_pairs={{0,8},{8,16},{16,24},{24,32},{32,40},{40,48},{48,56},{64,72},{72,8... | collective-permute-start | bytes 1572872 | tf_op jit(solution)/shard_map/ppermute | solution.py:234
  61.2 22.0 %collective-permute-start.10 = (bf16[2,2,256,256]{3,2,1,0:T(8,128)(2,1)}, bf16[2,2,256,256]{3,2,1,0:T(8,128)(2,1)}, u32[]{:S(2)}, u32[]{:S(2)}) collective-permute-start(bf16[2,2,256,256]{3,2,1,0:T(8,128)(2,1)} %get-tuple-element.88), channel_id=1, source_target_pairs={{8,0},{16,8},{24,16},{32,24},{40,32},{48,40},{56,48},{72,64},{80,7... | collective-permute-start | bytes 1572872 | tf_op jit(solution)/shard_map/ppermute | solution.py:234
  63.2 1.4 copy-start.39
  64.5 5.3 %copy-start.9 = (bf16[1,2,256,256]{3,2,1,0:T(8,128)(2,1)}, bf16[1,2,256,256]{3,2,1,0:T(8,128)(2,1)S(1)}, u32[]{:S(2)}) copy-start(bf16[1,2,256,256]{3,2,1,0:T(8,128)(2,1)S(1)} %get-tuple-element.96.refs_7_) | copy-start | bytes 786436
  64.5 1.3 copy-start.1
  64.5 1.6 %copy-start.3 = (bf16[2,2,2,256,256]{4,3,2,1,0:T(8,128)(2,1)S(1)}, bf16[2,2,2,256,256]{4,3,2,1,0:T(8,128)(2,1)}, u32[]{:S(2)}) copy-start(bf16[2,2,2,256,256]{4,3,2,1,0:T(8,128)(2,1)} %copy-done.2) | copy-start | bytes 3145732
  64.5 1.6 %copy-start.35 = (f32[8,128]{1,0:T(8,128)S(1)}, f32[8,128]{1,0:T(8,128)}, u32[]{:S(2)}) copy-start(f32[8,128]{1,0:T(8,128)} %get-tuple-element.53.refs_2_) | copy-start | bytes 12292
  69.9 0.8 copy-start.20
  70.6 0.7 copy-start.22
  71.4 0.8 copy-start.23
  72.1 0.7 copy-start.24
  72.9 0.6 copy-start.34
  73.5 0.9 copy-start.36
  74.3 0.9 copy-start.37
  78.1 6.2 %copy-start.10 = (bf16[1,2,256,256]{3,2,1,0:T(8,128)(2,1)S(1)}, bf16[1,2,256,256]{3,2,1,0:T(8,128)(2,1)}, u32[]{:S(2)}) copy-start(bf16[1,2,256,256]{3,2,1,0:T(8,128)(2,1)} %copy-done.9) | copy-start | bytes 786436
  78.1 6.2 %copy-start.30 = (f32[8,128]{1,0:T(8,128)S(1)}, f32[8,128]{1,0:T(8,128)}, u32[]{:S(2)}) copy-start(f32[8,128]{1,0:T(8,128)} %get-tuple-element.62.refs_2_) | copy-start | bytes 12292
  78.1 17.8 %collective-permute-start.9 = (f32[10,32,512]{2,1,0:T(8,128)}, f32[10,32,512]{2,1,0:T(8,128)}, u32[]{:S(2)}, u32[]{:S(2)}) collective-permute-start(f32[10,32,512]{2,1,0:T(8,128)} %get-tuple-element.60), channel_id=1, source_target_pairs={{0,4},{1,5},{2,6},{3,7},{4,0},{5,1},{6,2},{7,3},{8,12},{9,13},{10,... | collective-permute-start | bytes 1966088 | tf_op jit(solution)/shard_map/ppermute | solution.py:223
  78.9 22.0 %collective-permute-start.12 = (f32[12,32,512]{2,1,0:T(8,128)}, f32[12,32,512]{2,1,0:T(8,128)}, u32[]{:S(2)}, u32[]{:S(2)}) collective-permute-start(f32[12,32,512]{2,1,0:T(8,128)} %copy-done.37), channel_id=1, source_target_pairs={{0,1},{1,2},{2,3},{3,0},{4,5},{5,6},{6,7},{7,4},{8,9},{9,10},{10,1... | collective-permute-start | bytes 2359304 | tf_op jit(solution)/shard_map/ppermute | solution.py:226
  79.2 21.7 %collective-permute-start.13 = (f32[12,32,512]{2,1,0:T(8,128)}, f32[12,32,512]{2,1,0:T(8,128)}, u32[]{:S(2)}, u32[]{:S(2)}) collective-permute-start(f32[12,32,512]{2,1,0:T(8,128)} %copy-done.36), channel_id=1, source_target_pairs={{0,3},{1,0},{2,1},{3,2},{4,7},{5,4},{6,5},{7,6},{8,11},{9,8},{10,9... | collective-permute-start | bytes 2359304 | tf_op jit(solution)/shard_map/ppermute | solution.py:226
  89.1 0.8 copy-start.25
  89.8 0.7 copy-start.27
  90.6 0.7 copy-start.28
  91.3 0.7 copy-start.29
  92.6 22.3 %collective-permute-start.15 = (f32[10,32,512]{2,1,0:T(8,128)}, f32[10,32,512]{2,1,0:T(8,128)S(1)}, u32[]{:S(2)}, u32[]{:S(2)}) collective-permute-start(f32[10,32,512]{2,1,0:T(8,128)} %get-tuple-element.70), channel_id=1, source_target_pairs={{0,1},{1,2},{2,3},{3,0},{4,5},{5,6},{6,7},{7,4},{8,9},{9,10},{10,1... | collective-permute-start | bytes 1966088 | tf_op jit(solution)/shard_map/ppermute | solution.py:226
  92.6 22.3 %collective-permute-start.16 = (f32[10,32,512]{2,1,0:T(8,128)}, f32[10,32,512]{2,1,0:T(8,128)S(1)}, u32[]{:S(2)}, u32[]{:S(2)}) collective-permute-start(f32[10,32,512]{2,1,0:T(8,128)} %get-tuple-element.71), channel_id=1, source_target_pairs={{0,3},{1,0},{2,1},{3,2},{4,7},{5,4},{6,5},{7,6},{8,11},{9,8},{10,9... | collective-permute-start | bytes 1966088 | tf_op jit(solution)/shard_map/ppermute | solution.py:226
  103.7 19.6 %collective-permute-start.14 = (f32[6,32,512]{2,1,0:T(8,128)}, f32[6,32,512]{2,1,0:T(8,128)S(1)}, u32[]{:S(2)}, u32[]{:S(2)}) collective-permute-start(f32[6,32,512]{2,1,0:T(8,128)} %get-tuple-element.68), channel_id=1, source_target_pairs={{0,1},{1,2},{2,3},{3,0},{4,5},{5,6},{6,7},{7,4},{8,9},{9,10},{10,1... | collective-permute-start | bytes 1179656 | tf_op jit(solution)/shard_map/ppermute | solution.py:226
  104.0 19.2 %collective-permute-start.17 = (f32[6,32,512]{2,1,0:T(8,128)}, f32[6,32,512]{2,1,0:T(8,128)S(1)}, u32[]{:S(2)}, u32[]{:S(2)}) collective-permute-start(f32[6,32,512]{2,1,0:T(8,128)} %get-tuple-element.75), channel_id=1, source_target_pairs={{0,3},{1,0},{2,1},{3,2},{4,7},{5,4},{6,5},{7,6},{8,11},{9,8},{10,9... | collective-permute-start | bytes 1179656 | tf_op jit(solution)/shard_map/ppermute | solution.py:226
  114.9 0.8 copy-start.40
  114.9 1.1 copy-start.7
  118.3 9.4 %collective-permute-start.19 = (f32[5,32,512]{2,1,0:T(8,128)}, f32[5,32,512]{2,1,0:T(8,128)S(1)}, u32[]{:S(2)}, u32[]{:S(2)}) collective-permute-start(f32[5,32,512]{2,1,0:T(8,128)} %get-tuple-element.79), channel_id=1, source_target_pairs={{0,1},{1,2},{2,3},{3,0},{4,5},{5,6},{6,7},{7,4},{8,9},{9,10},{10,1... | collective-permute-start | bytes 983048 | tf_op jit(solution)/shard_map/ppermute | solution.py:226
  118.5 9.3 %collective-permute-start.20 = (f32[5,32,512]{2,1,0:T(8,128)}, f32[5,32,512]{2,1,0:T(8,128)}, u32[]{:S(2)}, u32[]{:S(2)}) collective-permute-start(f32[5,32,512]{2,1,0:T(8,128)} %get-tuple-element.81), channel_id=1, source_target_pairs={{0,3},{1,0},{2,1},{3,2},{4,7},{5,4},{6,5},{7,6},{8,11},{9,8},{10,9... | collective-permute-start | bytes 983048 | tf_op jit(solution)/shard_map/ppermute | solution.py:226
  123.3 0.7 copy-start.11
  123.3 0.9 copy-start.41
  124.1 16.1 %copy-start.8 = (f32[10,32,512]{2,1,0:T(8,128)S(1)}, f32[10,32,512]{2,1,0:T(8,128)}, u32[]{:S(2)}) copy-start(f32[10,32,512]{2,1,0:T(8,128)} %copy-done.7) | copy-start | bytes 1966084
  124.1 16.1 %copy-start.16 = (f32[10,32,512]{2,1,0:T(8,128)S(1)}, f32[10,32,512]{2,1,0:T(8,128)}, u32[]{:S(2)}) copy-start(f32[10,32,512]{2,1,0:T(8,128)} %copy-done.15) | copy-start | bytes 1966084
  126.5 13.8 %copy-start.6 = (f32[20,32,512]{2,1,0:T(8,128)S(1)}, f32[20,32,512]{2,1,0:T(8,128)}, u32[]{:S(2)}) copy-start(f32[20,32,512]{2,1,0:T(8,128)} %copy-done.5) | copy-start | bytes 3932164
  126.5 10.2 %collective-permute-start.18 = (f32[6,32,512]{2,1,0:T(8,128)}, f32[6,32,512]{2,1,0:T(8,128)S(1)}, u32[]{:S(2)}, u32[]{:S(2)}) collective-permute-start(f32[6,32,512]{2,1,0:T(8,128)} %get-tuple-element.77), channel_id=1, source_target_pairs={{0,4},{1,5},{2,6},{3,7},{4,0},{5,1},{6,2},{7,3},{8,12},{9,13},{10,... | collective-permute-start | bytes 1179656 | tf_op jit(solution)/shard_map/ppermute | solution.py:223
  127.7 0.7 copy-start.13
  130.6 9.7 %collective-permute-start.21 = (f32[5,32,512]{2,1,0:T(8,128)}, f32[5,32,512]{2,1,0:T(8,128)S(1)}, u32[]{:S(2)}, u32[]{:S(2)}) collective-permute-start(f32[5,32,512]{2,1,0:T(8,128)} %get-tuple-element.83), channel_id=1, source_target_pairs={{0,4},{1,5},{2,6},{3,7},{4,0},{5,1},{6,2},{7,3},{8,12},{9,13},{10,... | collective-permute-start | bytes 983048 | tf_op jit(solution)/shard_map/ppermute | solution.py:223
  140.3 1.0 copy-start.12
  141.3 1.0 copy-start.14
  142.3 1.0 copy-start.21
  143.2 1.0 copy-start.26
  144.2 0.7 copy-start.32
  (1 other events, 0.6 us)

commit v3 on v2

--- a/solution.py
+++ b/solution.py
@@ -10,7 +10,7 @@
 NPAIR = 4
 RING = 4
 LOOSE0, LOOSE1, DOWN, UP = range(4)
-SHORT = pl.CostEstimate(flops=0, bytes_accessed=0, transcendentals=0)
+MIB = 1024 * 1024
 EARLY = ((0, 0, UP), (0, 0, LOOSE0), (0, 0, LOOSE1), (0, 1, DOWN), (1, 0, LOOSE0))
 SIDES = (
     (0, 0, DOWN),
@@ -137,8 +137,8 @@
             pltpu.VMEM((tiles, depth, 2 * points), jnp.bfloat16),
             pltpu.VMEM((2, points, 2 * points), jnp.float32),
         ],
-        compiler_params=pltpu.CompilerParams(vmem_limit_bytes=40 * 1024 * 1024),
-        cost_estimate=SHORT,
+        compiler_params=pltpu.CompilerParams(vmem_limit_bytes=(24 if len(values) > 1 else 18) * MIB),
+        cost_estimate=pl.CostEstimate(flops=0, bytes_accessed=8 * MIB, transcendentals=0),
         name=name,
     )(meta, offsets, token, *values)
     return pieces, token
@@ -151,7 +151,8 @@
         out_shape=list(out_shape) + [jax.ShapeDtypeStruct(token.shape, token.dtype)],
         in_specs=[vmem] * (1 + len(arrays)),
         out_specs=[vmem] * (1 + len(out_shape)),
-        cost_estimate=SHORT,
+        compiler_params=pltpu.CompilerParams(vmem_limit_bytes=6 * MIB),
+        cost_estimate=pl.CostEstimate(flops=0, bytes_accessed=4 * MIB, transcendentals=0),
         name=name,
     )(token, *arrays)
     return outs, token
@@ -207,7 +208,8 @@
         out_shape=jax.ShapeDtypeStruct(shape, jnp.float32),
         in_specs=[smem, smem] + [vmem] * (len(flat) + 1),
         out_specs=vmem,
-        compiler_params=pltpu.CompilerParams(vmem_limit_bytes=40 * 1024 * 1024),
+        compiler_params=pltpu.CompilerParams(vmem_limit_bytes=10 * MIB),
+        cost_estimate=pl.CostEstimate(flops=0, bytes_accessed=8 * MIB, transcendentals=0),
         name="place_blocks",
     )(meta, offsets, *flat, token)
 

time: 150 us -> 120 us (0.80)
  local copies, waits for them, and re-layouts: 34.1 us -> 4.79 us
  Pallas kernels: 34.6 us -> 11.3 us
  waiting for transfers between devices: 37.7 us -> 60.8 us
    unnamed x87 -> x5, local copies, waits for them, and re-layouts: 25.7 us -> 1.69 us
    pallas_call x7, Pallas kernels: 18.9 us -> 0.69 us  [call_step(): pl.pallas_call(kernel, out_shape=list(out_shape) + [jax.ShapeDtypeStruct(...]
    ppermute x12, waiting for transfers between devices: 21.2 us -> 33.6 us  [around(): lax.ppermute(value, 'sa', [(h * RING + i, h * RING + (i + steps) % RING)...]
    ppermute x6, waiting for transfers between devices: 1.99 us -> 9.39 us  [tiles_from(): return lax.ppermute(value, ('gx', 'gy'), perm)]
    pallas_call x3, Pallas kernels: 12.4 us -> 8.44 us  [call_blocks(): pl.pallas_call(kernel, out_shape=[jax.ShapeDtypeStruct((pieces * count, p...]
    ppermute x4, waiting for transfers between devices: 14.6 us -> 17.8 us  [swap(): lax.ppermute(value, 'sa', [(i, (i + RING) % (2 * RING)) for i in range(2...]
  transfers between devices with their start and end apart: 22 -> 22, of which waited for: 8 -> 12; matrix products, arithmetic and copies ran while one was open for 5% -> 0% of each run, Pallas kernels for 21% -> 8%
where the time goes in v3:
time: 120 us
  waiting for transfers between devices  60.8 us (51%)
  starting transfers between devices  42.5 us (35%)
  Pallas kernels  11.3 us (9%)
  local copies, waits for them, and re-layouts  4.79 us (4%)
    ppermute x12, waiting for transfers between devices, around(): lax.ppermute(value, 'sa', [(h * RING + i, h * RING + (i + steps) % RING)...  33.6 us
    ppermute x12, starting transfers between devices, around(): lax.ppermute(value, 'sa', [(h * RING + i, h * RING + (i + steps) % RING)...  20 us
    ppermute x6, starting transfers between devices, tiles_from(): return lax.ppermute(value, ('gx', 'gy'), perm)  17.9 us
    ppermute x4, waiting for transfers between devices, swap(): lax.ppermute(value, 'sa', [(i, (i + RING) % (2 * RING)) for i in range(2...  17.8 us
    ppermute x6, waiting for transfers between devices, tiles_from(): return lax.ppermute(value, ('gx', 'gy'), perm)  9.39 us
    pallas_call x3, Pallas kernels, call_blocks(): pl.pallas_call(kernel, out_shape=[jax.ShapeDtypeStruct((pieces * count, p...  8.44 us
    ppermute x4, starting transfers between devices, swap(): lax.ppermute(value, 'sa', [(i, (i + RING) % (2 * RING)) for i in range(2...  4.66 us
    squeeze x1, local copies, waits for them, and re-layouts, per_device(): theirs = swap(lax.dynamic_index_in_dim(green, 1 - x_lo, 2, keepdims=False))  2.68 us
  transfers between devices with their start and end apart: 22, of which 12 were waited for; matrix products, arithmetic and copies ran while one was open for 0% of the time, Pallas kernels for 8%

profile of v3, /device:TPU:100, one launch (start us, length us, event | category | flops | bytes accessed | tf_op | source)
XLA Modules:
  0.0 119.7 jit_solution(7856161172255370248)
XLA Ops:
  0.0 2.7 %dynamic-slice_bitcast_fusion = (bf16[2,2,2,256,256]{4,3,2,1,0:T(8,128)(2,1)}, bf16[2,2,1,2,256,256]{5,4,3,2,1,0:T(8,128)(2,1)S(1)}) fusion(bf16[2,2,2,2,256,256]{5,4,3,2,1,0:T(8,128)(2,1)} %green.1, s32[]{:T(128)S(6)} %select_n.21, s32[]{:T(128)S(6)} %select_n.20), kind=kLoop, calls=%fused_computation.1 | loop fusion | bytes 4194312 | tf_op jit(solution)/shard_map/jit(dynamic_index_in_dim)/squeeze | solution.py:257
  2.7 1.2 %collective-permute-start = (bf16[2,2,2,256,256]{4,3,2,1,0:T(8,128)(2,1)}, bf16[2,2,2,256,256]{4,3,2,1,0:T(8,128)(2,1)S(1)}, u32[]{:S(2)}, u32[]{:S(2)}) collective-permute-start(bf16[2,2,2,256,256]{4,3,2,1,0:T(8,128)(2,1)} %get-tuple-element.85), channel_id=1, source_target_pairs={{0,4},{1,5},{2,6},{3,7},{4,0},{5,1},{6,2},{7,3},{8,12},{9,13},{10,... | collective-permute-start | bytes 3145736 | tf_op jit(solution)/shard_map/ppermute | solution.py:225
  3.9 0.1 copy.12
  4.0 2.0 %collective-permute-start.1 = (bf16[2,2,256,256]{3,2,1,0:T(8,128)(2,1)S(1)}, bf16[2,2,256,256]{3,2,1,0:T(8,128)(2,1)S(1)}, u32[]{:S(2)}, u32[]{:S(2)}) collective-permute-start(bf16[2,2,256,256]{3,2,1,0:T(8,128)(2,1)S(1)} %slice_bitcast_fusion.4), channel_id=1, source_target_pairs={{8,0},{16,8},{24,16},{32,24},{40,32},{48,40},{56,48},{72,64},{80,7... | collective-permute-start | bytes 1572872 | tf_op jit(solution)/shard_map/ppermute | solution.py:236
  6.0 0.0 copy-done.1
  6.0 0.1 copy.9.offsets.refs_1_
  6.1 0.1 pad_add_fusion.meta.refs_0_
  6.2 1.6 %copy-done = bf16[2,2,2,2,256,256]{5,4,3,2,1,0:T(8,128)(2,1)S(1)} copy-done((bf16[2,2,2,2,256,256]{5,4,3,2,1,0:T(8,128)(2,1)S(1)}, bf16[2,2,2,2,256,256]{5,4,3,2,1,0:T(8,128)(2,1)}, u32[]{:S(2)}) %copy-start) | copy-done | bytes 2097176
  7.8 2.5 %early_blocks.1 = (f32[10,32,512]{2,1,0:T(8,128)S(1)}, f32[10,32,512]{2,1,0:T(8,128)S(1)}, f32[20,32,512]{2,1,0:T(8,128)S(1)}, f32[20,32,512]{2,1,0:T(8,128)S(1)...) custom-call(s32[2]{0:T(128)S(1)} %pad_add_fusion.meta.refs_0_, ...), custom_call_target="tpu_custom_call" | custom-call | bytes 8388608 | tf_op jit(solution)/shard_map/early_blocks/pallas_call | solution.py:126
  10.3 1.7 %collective-permute-start.2 = (f32[20,32,512]{2,1,0:T(8,128)S(1)}, f32[20,32,512]{2,1,0:T(8,128)S(1)}, u32[]{:S(2)}, u32[]{:S(2)}) collective-permute-start(f32[20,32,512]{2,1,0:T(8,128)S(1)} %get-tuple-element.48), channel_id=1, source_target_pairs={{0,1},{1,2},{2,3},{3,0},{4,5},{5,6},{6,7},{7,4},{8,9},{9,10},{10,1... | collective-permute-start | bytes 3932168 | tf_op jit(solution)/shard_map/ppermute | solution.py:228
  11.9 1.7 %collective-permute-start.3 = (f32[20,32,512]{2,1,0:T(8,128)S(1)}, f32[20,32,512]{2,1,0:T(8,128)S(1)}, u32[]{:S(2)}, u32[]{:S(2)}) collective-permute-start(f32[20,32,512]{2,1,0:T(8,128)S(1)} %get-tuple-element.49), channel_id=1, source_target_pairs={{0,3},{1,0},{2,1},{3,2},{4,7},{5,4},{6,5},{7,6},{8,11},{9,8},{10,9... | collective-permute-start | bytes 3932168 | tf_op jit(solution)/shard_map/ppermute | solution.py:228
  13.6 7.1 %collective-permute-done.1.above_mine.refs_9_ = bf16[2,2,256,256]{3,2,1,0:T(8,128)(2,1)S(1)} collective-permute-done((bf16[2,2,256,256]{3,2,1,0:T(8,128)(2,1)S(1)}, bf16[2,2,256,256]{3,2,1,0:T(8,128)(2,1)S(1)}, u32[]{:S(2)}, u32[]{:S(2)}) %collective-permute-start.1) | collective-permute-done | bytes 524320 | tf_op jit(solution)/shard_map/ppermute | solution.py:236
  20.7 7.1 %collective-permute-done.theirs = bf16[2,2,2,256,256]{4,3,2,1,0:T(8,128)(2,1)S(1)} collective-permute-done((bf16[2,2,2,256,256]{4,3,2,1,0:T(8,128)(2,1)}, bf16[2,2,2,256,256]{4,3,2,1,0:T(8,128)(2,1)S(1)}, u32[]{:S(2)}, u32[]{:S(2)}) %collective-permute-start) | collective-permute-done | bytes 1048608 | tf_op jit(solution)/shard_map/ppermute | solution.py:225
  27.8 0.1 swapped.1
  27.9 0.1 copy.6
  28.0 1.9 %collective-permute-start.5 = (bf16[2,2,2,256,256]{4,3,2,0,1:T(8,128)(2,1)S(1)}, bf16[2,2,2,256,256]{4,3,2,0,1:T(8,128)(2,1)S(1)}, u32[]{:S(2)}, u32[]{:S(2)}) collective-permute-start(bf16[2,2,2,256,256]{4,3,2,0,1:T(8,128)(2,1)S(1)} %copy.6), channel_id=1, source_target_pairs={{64,0},{72,8},{80,16},{88,24},{96,32},{104,40},{112,48},{120,56},{... | collective-permute-start | bytes 3145736 | tf_op jit(solution)/shard_map/ppermute | solution.py:236
  29.9 5.0 %collective-permute-start.6 = (bf16[2,2,256,256]{3,2,1,0:T(8,128)(2,1)S(1)}, bf16[2,2,256,256]{3,2,1,0:T(8,128)(2,1)S(1)}, u32[]{:S(2)}, u32[]{:S(2)}) collective-permute-start(bf16[2,2,256,256]{3,2,1,0:T(8,128)(2,1)S(1)} %get-tuple-element.55), channel_id=1, source_target_pairs={{0,8},{8,16},{16,24},{24,32},{32,40},{40,48},{48,56},{64,72},{72,8... | collective-permute-start | bytes 1572872 | tf_op jit(solution)/shard_map/ppermute | solution.py:236
  35.0 1.9 %collective-permute-start.7 = (bf16[2,2,256,256]{3,2,1,0:T(8,128)(2,1)S(1)}, bf16[2,2,256,256]{3,2,1,0:T(8,128)(2,1)S(1)}, u32[]{:S(2)}, u32[]{:S(2)}) collective-permute-start(bf16[2,2,256,256]{3,2,1,0:T(8,128)(2,1)S(1)} %get-tuple-element.56), channel_id=1, source_target_pairs={{8,0},{16,8},{24,16},{32,24},{40,32},{48,40},{56,48},{72,64},{80,7... | collective-permute-start | bytes 1572872 | tf_op jit(solution)/shard_map/ppermute | solution.py:236
  36.9 4.9 %collective-permute-done.2.up_received = f32[20,32,512]{2,1,0:T(8,128)S(1)} collective-permute-done((f32[20,32,512]{2,1,0:T(8,128)S(1)}, f32[20,32,512]{2,1,0:T(8,128)S(1)}, u32[]{:S(2)}, u32[]{:S(2)}) %collective-permute-start.2) | collective-permute-done | bytes 1310752 | tf_op jit(solution)/shard_map/ppermute | solution.py:228
  41.8 0.0 collective-permute-done.3.down_received.refs_2_
  41.8 0.1 second.3
  41.9 1.7 %collective-permute-start.4 = (f32[10,32,512]{2,1,0:T(8,128)S(1)}, f32[10,32,512]{2,1,0:T(8,128)S(1)}, u32[]{:S(2)}, u32[]{:S(2)}) collective-permute-start(f32[10,32,512]{2,1,0:T(8,128)S(1)} %get-tuple-element.52), channel_id=1, source_target_pairs={{0,1},{1,2},{2,3},{3,0},{4,5},{5,6},{6,7},{7,4},{8,9},{9,10},{10,1... | collective-permute-start | bytes 1966088 | tf_op jit(solution)/shard_map/ppermute | solution.py:228
  43.6 1.7 %collective-permute-start.8 = (f32[10,32,512]{2,1,0:T(8,128)S(1)}, f32[10,32,512]{2,1,0:T(8,128)S(1)}, u32[]{:S(2)}, u32[]{:S(2)}) collective-permute-start(f32[10,32,512]{2,1,0:T(8,128)S(1)} %get-tuple-element.58), channel_id=1, source_target_pairs={{0,3},{1,0},{2,1},{3,2},{4,7},{5,4},{6,5},{7,6},{8,11},{9,8},{10,9... | collective-permute-start | bytes 1966088 | tf_op jit(solution)/shard_map/ppermute | solution.py:228
  45.2 0.0 collective-permute-done.5
  45.2 0.1 slice_bitcast_fusion
  45.3 5.0 %collective-permute-start.11 = (bf16[2,2,256,256]{3,2,1,0:T(8,128)(2,1)S(1)}, bf16[2,2,256,256]{3,2,1,0:T(8,128)(2,1)S(1)}, u32[]{:S(2)}, u32[]{:S(2)}) collective-permute-start(bf16[2,2,256,256]{3,2,1,0:T(8,128)(2,1)S(1)} %get-tuple-element.87), channel_id=1, source_target_pairs={{0,8},{8,16},{16,24},{24,32},{32,40},{40,48},{48,56},{64,72},{72,8... | collective-permute-start | bytes 1572872 | tf_op jit(solution)/shard_map/ppermute | solution.py:236
  50.4 0.0 collective-permute-done.6
  50.4 1.9 %collective-permute-start.10 = (bf16[2,2,256,256]{3,2,1,0:T(8,128)(2,1)S(1)}, bf16[2,2,256,256]{3,2,1,0:T(8,128)(2,1)S(1)}, u32[]{:S(2)}, u32[]{:S(2)}) collective-permute-start(bf16[2,2,256,256]{3,2,1,0:T(8,128)(2,1)S(1)} %get-tuple-element.88), channel_id=1, source_target_pairs={{8,0},{16,8},{24,16},{32,24},{40,32},{48,40},{56,48},{72,64},{80,7... | collective-permute-start | bytes 1572872 | tf_op jit(solution)/shard_map/ppermute | solution.py:236
  52.3 0.1 slice_bitcast_fusion.2
  52.4 0.0 collective-permute-done.7.refs_10_
  52.4 3.0 %side_blocks.1 = (f32[6,32,512]{2,1,0:T(8,128)S(1)}, f32[6,32,512]{2,1,0:T(8,128)S(1)}, f32[12,32,512]{2,1,0:T(8,128)S(1)}, f32[12,32,512]{2,1,0:T(8,128)S(1)}, ...) custom-call(s32[2]{0:T(128)S(1)} %pad_add_fusion.meta.refs_0_, ...), custom_call_target="tpu_custom_call" | custom-call | bytes 8388608 | tf_op jit(solution)/shard_map/side_blocks/pallas_call | solution.py:126
  55.5 2.9 %collective-permute-done.4.refs_0_.refs_1_ = f32[10,32,512]{2,1,0:T(8,128)S(1)} collective-permute-done((f32[10,32,512]{2,1,0:T(8,128)S(1)}, f32[10,32,512]{2,1,0:T(8,128)S(1)}, u32[]{:S(2)}, u32[]{:S(2)}) %collective-permute-start.4) | collective-permute-done | bytes 655392 | tf_op jit(solution)/shard_map/ppermute | solution.py:228
  58.4 0.0 collective-permute-done.8.down_arrived
  58.4 0.1 back.3
  58.6 0.9 collective-permute-start.9
  59.5 1.0 collective-permute-start.12
  60.5 2.2 %collective-permute-start.13 = (f32[12,32,512]{2,1,0:T(8,128)S(1)}, f32[12,32,512]{2,1,0:T(8,128)S(1)}, u32[]{:S(2)}, u32[]{:S(2)}) collective-permute-start(f32[12,32,512]{2,1,0:T(8,128)S(1)} %get-tuple-element.65), channel_id=1, source_target_pairs={{0,3},{1,0},{2,1},{3,2},{4,7},{5,4},{6,5},{7,6},{8,11},{9,8},{10,9... | collective-permute-start | bytes 2359304 | tf_op jit(solution)/shard_map/ppermute | solution.py:228
  62.7 0.0 collective-permute-done.11
  62.8 2.3 %collective-permute-done.10 = bf16[2,2,256,256]{3,2,1,0:T(8,128)(2,1)S(1)} collective-permute-done((bf16[2,2,256,256]{3,2,1,0:T(8,128)(2,1)S(1)}, bf16[2,2,256,256]{3,2,1,0:T(8,128)(2,1)S(1)}, u32[]{:S(2)}, u32[]{:S(2)}) %collective-permute-start.10) | collective-permute-done | bytes 524320 | tf_op jit(solution)/shard_map/ppermute | solution.py:236
  65.1 2.9 %corner_blocks.1 = (f32[5,32,512]{2,1,0:T(8,128)S(1)}, f32[5,32,512]{2,1,0:T(8,128)S(1)}, f32[10,32,512]{2,1,0:T(8,128)S(1)}, f32[10,32,512]{2,1,0:T(8,128)S(1)}...) custom-call(s32[2]{0:T(128)S(1)} %pad_add_fusion.meta.refs_0_, ...), custom_call_target="tpu_custom_call" | custom-call | bytes 8388608 | tf_op jit(solution)/shard_map/corner_blocks/pallas_call | solution.py:126
  68.0 0.9 collective-permute-start.15
  69.0 2.4 %collective-permute-start.16 = (f32[10,32,512]{2,1,0:T(8,128)S(1)}, f32[10,32,512]{2,1,0:T(8,128)S(1)}, u32[]{:S(2)}, u32[]{:S(2)}) collective-permute-start(f32[10,32,512]{2,1,0:T(8,128)S(1)} %get-tuple-element.71), channel_id=1, source_target_pairs={{0,3},{1,0},{2,1},{3,2},{4,7},{5,4},{6,5},{7,6},{8,11},{9,8},{10,9... | collective-permute-start | bytes 1966088 | tf_op jit(solution)/shard_map/ppermute | solution.py:228
  71.4 1.6 %collective-permute-done.9.refs_0_.refs_3_ = f32[10,32,512]{2,1,0:T(8,128)S(1)} collective-permute-done((f32[10,32,512]{2,1,0:T(8,128)S(1)}, f32[10,32,512]{2,1,0:T(8,128)S(1)}, u32[]{:S(2)}, u32[]{:S(2)}) %collective-permute-start.9) | collective-permute-done | bytes 655392 | tf_op jit(solution)/shard_map/ppermute | solution.py:225
  72.9 8.2 %collective-permute-done.12.up_received = f32[12,32,512]{2,1,0:T(8,128)S(1)} collective-permute-done((f32[12,32,512]{2,1,0:T(8,128)S(1)}, f32[12,32,512]{2,1,0:T(8,128)S(1)}, u32[]{:S(2)}, u32[]{:S(2)}) %collective-permute-start.12) | collective-permute-done | bytes 786464 | tf_op jit(solution)/shard_map/ppermute | solution.py:228
  81.2 0.0 collective-permute-done.13.down_received.refs_6_
  81.2 0.1 second.4
  81.3 1.6 %collective-permute-start.14 = (f32[6,32,512]{2,1,0:T(8,128)S(1)}, f32[6,32,512]{2,1,0:T(8,128)S(1)}, u32[]{:S(2)}, u32[]{:S(2)}) collective-permute-start(f32[6,32,512]{2,1,0:T(8,128)S(1)} %get-tuple-element.68), channel_id=1, source_target_pairs={{0,1},{1,2},{2,3},{3,0},{4,5},{5,6},{6,7},{7,4},{8,9},{9,10},{10,1... | collective-permute-start | bytes 1179656 | tf_op jit(solution)/shard_map/ppermute | solution.py:228
  82.9 1.8 %collective-permute-start.17 = (f32[6,32,512]{2,1,0:T(8,128)S(1)}, f32[6,32,512]{2,1,0:T(8,128)S(1)}, u32[]{:S(2)}, u32[]{:S(2)}) collective-permute-start(f32[6,32,512]{2,1,0:T(8,128)S(1)} %get-tuple-element.75), channel_id=1, source_target_pairs={{0,3},{1,0},{2,1},{3,2},{4,7},{5,4},{6,5},{7,6},{8,11},{9,8},{10,9... | collective-permute-start | bytes 1179656 | tf_op jit(solution)/shard_map/ppermute | solution.py:228
  84.7 10.5 %collective-permute-done.15.up_received = f32[10,32,512]{2,1,0:T(8,128)S(1)} collective-permute-done((f32[10,32,512]{2,1,0:T(8,128)S(1)}, f32[10,32,512]{2,1,0:T(8,128)S(1)}, u32[]{:S(2)}, u32[]{:S(2)}) %collective-permute-start.15) | collective-permute-done | bytes 655392 | tf_op jit(solution)/shard_map/ppermute | solution.py:228
  95.2 0.0 collective-permute-done.16.down_received.refs_10_
  95.2 0.1 second.5
  95.3 1.6 %collective-permute-start.19 = (f32[5,32,512]{2,1,0:T(8,128)S(1)}, f32[5,32,512]{2,1,0:T(8,128)S(1)}, u32[]{:S(2)}, u32[]{:S(2)}) collective-permute-start(f32[5,32,512]{2,1,0:T(8,128)S(1)} %get-tuple-element.79), channel_id=1, source_target_pairs={{0,1},{1,2},{2,3},{3,0},{4,5},{5,6},{6,7},{7,4},{8,9},{9,10},{10,1... | collective-permute-start | bytes 983048 | tf_op jit(solution)/shard_map/ppermute | solution.py:228
  96.9 1.8 %collective-permute-start.20 = (f32[5,32,512]{2,1,0:T(8,128)S(1)}, f32[5,32,512]{2,1,0:T(8,128)S(1)}, u32[]{:S(2)}, u32[]{:S(2)}) collective-permute-start(f32[5,32,512]{2,1,0:T(8,128)S(1)} %get-tuple-element.81), channel_id=1, source_target_pairs={{0,3},{1,0},{2,1},{3,2},{4,7},{5,4},{6,5},{7,6},{8,11},{9,8},{10,9... | collective-permute-start | bytes 983048 | tf_op jit(solution)/shard_map/ppermute | solution.py:228
  98.7 4.8 %collective-permute-done.14.refs_0_.refs_5_ = f32[6,32,512]{2,1,0:T(8,128)S(1)} collective-permute-done((f32[6,32,512]{2,1,0:T(8,128)S(1)}, f32[6,32,512]{2,1,0:T(8,128)S(1)}, u32[]{:S(2)}, u32[]{:S(2)}) %collective-permute-start.14) | collective-permute-done | bytes 393248 | tf_op jit(solution)/shard_map/ppermute | solution.py:228
  103.5 0.0 collective-permute-done.17.down_arrived
  103.5 0.1 back.4
  103.6 1.3 %collective-permute-start.18 = (f32[6,32,512]{2,1,0:T(8,128)S(1)}, f32[6,32,512]{2,1,0:T(8,128)S(1)}, u32[]{:S(2)}, u32[]{:S(2)}) collective-permute-start(f32[6,32,512]{2,1,0:T(8,128)S(1)} %get-tuple-element.77), channel_id=1, source_target_pairs={{0,4},{1,5},{2,6},{3,7},{4,0},{5,1},{6,2},{7,3},{8,12},{9,13},{10,... | collective-permute-start | bytes 1179656 | tf_op jit(solution)/shard_map/ppermute | solution.py:225
  104.9 2.2 %collective-permute-done.19.refs_0_.refs_9_ = f32[5,32,512]{2,1,0:T(8,128)S(1)} collective-permute-done((f32[5,32,512]{2,1,0:T(8,128)S(1)}, f32[5,32,512]{2,1,0:T(8,128)S(1)}, u32[]{:S(2)}, u32[]{:S(2)}) %collective-permute-start.19) | collective-permute-done | bytes 327712 | tf_op jit(solution)/shard_map/ppermute | solution.py:228
  107.0 0.0 collective-permute-done.20.down_arrived
  107.0 0.1 back.5
  107.1 1.3 %collective-permute-start.21 = (f32[5,32,512]{2,1,0:T(8,128)S(1)}, f32[5,32,512]{2,1,0:T(8,128)S(1)}, u32[]{:S(2)}, u32[]{:S(2)}) collective-permute-start(f32[5,32,512]{2,1,0:T(8,128)S(1)} %get-tuple-element.83), channel_id=1, source_target_pairs={{0,4},{1,5},{2,6},{3,7},{4,0},{5,1},{6,2},{7,3},{8,12},{9,13},{10,... | collective-permute-start | bytes 983048 | tf_op jit(solution)/shard_map/ppermute | solution.py:225
  108.3 5.6 %collective-permute-done.18.refs_7_ = f32[6,32,512]{2,1,0:T(8,128)S(1)} collective-permute-done((f32[6,32,512]{2,1,0:T(8,128)S(1)}, f32[6,32,512]{2,1,0:T(8,128)S(1)}, u32[]{:S(2)}, u32[]{:S(2)}) %collective-permute-start.18) | collective-permute-done | bytes 393248 | tf_op jit(solution)/shard_map/ppermute | solution.py:225
  113.9 3.5 %collective-permute-done.21.refs_11_ = f32[5,32,512]{2,1,0:T(8,128)S(1)} collective-permute-done((f32[5,32,512]{2,1,0:T(8,128)S(1)}, f32[5,32,512]{2,1,0:T(8,128)S(1)}, u32[]{:S(2)}, u32[]{:S(2)}) %collective-permute-start.21) | collective-permute-done | bytes 327712 | tf_op jit(solution)/shard_map/ppermute | solution.py:225
  117.5 2.2 %place_blocks.1 = f32[2,2,4,2,32,512]{5,4,3,2,1,0:T(8,128)} custom-call(s32[2]{0:T(128)S(1)} %pad_add_fusion.meta.refs_0_, s32[4,2]{1,0:T(4,128)S(1)} %copy.9.offsets.refs_1_, f32[10,32,512]{2,1,0:T(8,128)S(1)} %get-tuple-element.45.refs_0_, f32[10,32,512]{2,1,0:T(8,128)S(1)} %collective-permute-done.4.refs_0_.refs_1_, ...), custom_call_target="tpu_custom_call" | custom-call | bytes 8388608 | tf_op jit(solution)/shard_map/place_blocks/pallas_call | solution.py:206
  (7 shorter events, 0.1 us)
Async XLA Ops:
  2.7 25.1 %collective-permute-start = (bf16[2,2,2,256,256]{4,3,2,1,0:T(8,128)(2,1)}, bf16[2,2,2,256,256]{4,3,2,1,0:T(8,128)(2,1)S(1)}, u32[]{:S(2)}, u32[]{:S(2)}) collective-permute-start(bf16[2,2,2,256,256]{4,3,2,1,0:T(8,128)(2,1)} %get-tuple-element.85), channel_id=1, source_target_pairs={{0,4},{1,5},{2,6},{3,7},{4,0},{5,1},{6,2},{7,3},{8,12},{9,13},{10,... | collective-permute-start | bytes 3145736 | tf_op jit(solution)/shard_map/ppermute | solution.py:225
  3.9 2.2 %copy-start.1 = (s32[4,2]{0,1:T(2,128)S(1)}, s32[4,2]{0,1:T(2,128)}, u32[]{:S(2)}) copy-start(s32[4,2]{0,1:T(2,128)} %param.3) | copy-start | bytes 100
  4.0 16.7 %collective-permute-start.1 = (bf16[2,2,256,256]{3,2,1,0:T(8,128)(2,1)S(1)}, bf16[2,2,256,256]{3,2,1,0:T(8,128)(2,1)S(1)}, u32[]{:S(2)}, u32[]{:S(2)}) collective-permute-start(bf16[2,2,256,256]{3,2,1,0:T(8,128)(2,1)S(1)} %slice_bitcast_fusion.4), channel_id=1, source_target_pairs={{8,0},{16,8},{24,16},{32,24},{40,32},{48,40},{56,48},{72,64},{80,7... | collective-permute-start | bytes 1572872 | tf_op jit(solution)/shard_map/ppermute | solution.py:236
  6.2 1.6 %copy-start = (bf16[2,2,2,2,256,256]{5,4,3,2,1,0:T(8,128)(2,1)S(1)}, bf16[2,2,2,2,256,256]{5,4,3,2,1,0:T(8,128)(2,1)}, u32[]{:S(2)}) copy-start(bf16[2,2,2,2,256,256]{5,4,3,2,1,0:T(8,128)(2,1)} %green.1) | copy-start | bytes 6291460
  10.3 31.5 %collective-permute-start.2 = (f32[20,32,512]{2,1,0:T(8,128)S(1)}, f32[20,32,512]{2,1,0:T(8,128)S(1)}, u32[]{:S(2)}, u32[]{:S(2)}) collective-permute-start(f32[20,32,512]{2,1,0:T(8,128)S(1)} %get-tuple-element.48), channel_id=1, source_target_pairs={{0,1},{1,2},{2,3},{3,0},{4,5},{5,6},{6,7},{7,4},{8,9},{9,10},{10,1... | collective-permute-start | bytes 3932168 | tf_op jit(solution)/shard_map/ppermute | solution.py:228
  11.9 29.9 %collective-permute-start.3 = (f32[20,32,512]{2,1,0:T(8,128)S(1)}, f32[20,32,512]{2,1,0:T(8,128)S(1)}, u32[]{:S(2)}, u32[]{:S(2)}) collective-permute-start(f32[20,32,512]{2,1,0:T(8,128)S(1)} %get-tuple-element.49), channel_id=1, source_target_pairs={{0,3},{1,0},{2,1},{3,2},{4,7},{5,4},{6,5},{7,6},{8,11},{9,8},{10,9... | collective-permute-start | bytes 3932168 | tf_op jit(solution)/shard_map/ppermute | solution.py:228
  28.0 17.2 %collective-permute-start.5 = (bf16[2,2,2,256,256]{4,3,2,0,1:T(8,128)(2,1)S(1)}, bf16[2,2,2,256,256]{4,3,2,0,1:T(8,128)(2,1)S(1)}, u32[]{:S(2)}, u32[]{:S(2)}) collective-permute-start(bf16[2,2,2,256,256]{4,3,2,0,1:T(8,128)(2,1)S(1)} %copy.6), channel_id=1, source_target_pairs={{64,0},{72,8},{80,16},{88,24},{96,32},{104,40},{112,48},{120,56},{... | collective-permute-start | bytes 3145736 | tf_op jit(solution)/shard_map/ppermute | solution.py:236
  29.9 20.4 %collective-permute-start.6 = (bf16[2,2,256,256]{3,2,1,0:T(8,128)(2,1)S(1)}, bf16[2,2,256,256]{3,2,1,0:T(8,128)(2,1)S(1)}, u32[]{:S(2)}, u32[]{:S(2)}) collective-permute-start(bf16[2,2,256,256]{3,2,1,0:T(8,128)(2,1)S(1)} %get-tuple-element.55), channel_id=1, source_target_pairs={{0,8},{8,16},{16,24},{24,32},{32,40},{40,48},{48,56},{64,72},{72,8... | collective-permute-start | bytes 1572872 | tf_op jit(solution)/shard_map/ppermute | solution.py:236
  35.0 17.4 %collective-permute-start.7 = (bf16[2,2,256,256]{3,2,1,0:T(8,128)(2,1)S(1)}, bf16[2,2,256,256]{3,2,1,0:T(8,128)(2,1)S(1)}, u32[]{:S(2)}, u32[]{:S(2)}) collective-permute-start(bf16[2,2,256,256]{3,2,1,0:T(8,128)(2,1)S(1)} %get-tuple-element.56), channel_id=1, source_target_pairs={{8,0},{16,8},{24,16},{32,24},{40,32},{48,40},{56,48},{72,64},{80,7... | collective-permute-start | bytes 1572872 | tf_op jit(solution)/shard_map/ppermute | solution.py:236
  41.9 16.5 %collective-permute-start.4 = (f32[10,32,512]{2,1,0:T(8,128)S(1)}, f32[10,32,512]{2,1,0:T(8,128)S(1)}, u32[]{:S(2)}, u32[]{:S(2)}) collective-permute-start(f32[10,32,512]{2,1,0:T(8,128)S(1)} %get-tuple-element.52), channel_id=1, source_target_pairs={{0,1},{1,2},{2,3},{3,0},{4,5},{5,6},{6,7},{7,4},{8,9},{9,10},{10,1... | collective-permute-start | bytes 1966088 | tf_op jit(solution)/shard_map/ppermute | solution.py:228
  43.6 14.9 %collective-permute-start.8 = (f32[10,32,512]{2,1,0:T(8,128)S(1)}, f32[10,32,512]{2,1,0:T(8,128)S(1)}, u32[]{:S(2)}, u32[]{:S(2)}) collective-permute-start(f32[10,32,512]{2,1,0:T(8,128)S(1)} %get-tuple-element.58), channel_id=1, source_target_pairs={{0,3},{1,0},{2,1},{3,2},{4,7},{5,4},{6,5},{7,6},{8,11},{9,8},{10,9... | collective-permute-start | bytes 1966088 | tf_op jit(solution)/shard_map/ppermute | solution.py:228
  45.3 17.4 %collective-permute-start.11 = (bf16[2,2,256,256]{3,2,1,0:T(8,128)(2,1)S(1)}, bf16[2,2,256,256]{3,2,1,0:T(8,128)(2,1)S(1)}, u32[]{:S(2)}, u32[]{:S(2)}) collective-permute-start(bf16[2,2,256,256]{3,2,1,0:T(8,128)(2,1)S(1)} %get-tuple-element.87), channel_id=1, source_target_pairs={{0,8},{8,16},{16,24},{24,32},{32,40},{40,48},{48,56},{64,72},{72,8... | collective-permute-start | bytes 1572872 | tf_op jit(solution)/shard_map/ppermute | solution.py:236
  50.4 14.7 %collective-permute-start.10 = (bf16[2,2,256,256]{3,2,1,0:T(8,128)(2,1)S(1)}, bf16[2,2,256,256]{3,2,1,0:T(8,128)(2,1)S(1)}, u32[]{:S(2)}, u32[]{:S(2)}) collective-permute-start(bf16[2,2,256,256]{3,2,1,0:T(8,128)(2,1)S(1)} %get-tuple-element.88), channel_id=1, source_target_pairs={{8,0},{16,8},{24,16},{32,24},{40,32},{48,40},{56,48},{72,64},{80,7... | collective-permute-start | bytes 1572872 | tf_op jit(solution)/shard_map/ppermute | solution.py:236
  58.6 14.4 %collective-permute-start.9 = (f32[10,32,512]{2,1,0:T(8,128)S(1)}, f32[10,32,512]{2,1,0:T(8,128)S(1)}, u32[]{:S(2)}, u32[]{:S(2)}) collective-permute-start(f32[10,32,512]{2,1,0:T(8,128)S(1)} %get-tuple-element.60), channel_id=1, source_target_pairs={{0,4},{1,5},{2,6},{3,7},{4,0},{5,1},{6,2},{7,3},{8,12},{9,13},{10,... | collective-permute-start | bytes 1966088 | tf_op jit(solution)/shard_map/ppermute | solution.py:225
  59.5 21.7 %collective-permute-start.12 = (f32[12,32,512]{2,1,0:T(8,128)S(1)}, f32[12,32,512]{2,1,0:T(8,128)S(1)}, u32[]{:S(2)}, u32[]{:S(2)}) collective-permute-start(f32[12,32,512]{2,1,0:T(8,128)S(1)} %get-tuple-element.64), channel_id=1, source_target_pairs={{0,1},{1,2},{2,3},{3,0},{4,5},{5,6},{6,7},{7,4},{8,9},{9,10},{10,1... | collective-permute-start | bytes 2359304 | tf_op jit(solution)/shard_map/ppermute | solution.py:228
  60.5 20.7 %collective-permute-start.13 = (f32[12,32,512]{2,1,0:T(8,128)S(1)}, f32[12,32,512]{2,1,0:T(8,128)S(1)}, u32[]{:S(2)}, u32[]{:S(2)}) collective-permute-start(f32[12,32,512]{2,1,0:T(8,128)S(1)} %get-tuple-element.65), channel_id=1, source_target_pairs={{0,3},{1,0},{2,1},{3,2},{4,7},{5,4},{6,5},{7,6},{8,11},{9,8},{10,9... | collective-permute-start | bytes 2359304 | tf_op jit(solution)/shard_map/ppermute | solution.py:228
  68.0 27.2 %collective-permute-start.15 = (f32[10,32,512]{2,1,0:T(8,128)S(1)}, f32[10,32,512]{2,1,0:T(8,128)S(1)}, u32[]{:S(2)}, u32[]{:S(2)}) collective-permute-start(f32[10,32,512]{2,1,0:T(8,128)S(1)} %get-tuple-element.70), channel_id=1, source_target_pairs={{0,1},{1,2},{2,3},{3,0},{4,5},{5,6},{6,7},{7,4},{8,9},{9,10},{10,1... | collective-permute-start | bytes 1966088 | tf_op jit(solution)/shard_map/ppermute | solution.py:228
  69.0 26.3 %collective-permute-start.16 = (f32[10,32,512]{2,1,0:T(8,128)S(1)}, f32[10,32,512]{2,1,0:T(8,128)S(1)}, u32[]{:S(2)}, u32[]{:S(2)}) collective-permute-start(f32[10,32,512]{2,1,0:T(8,128)S(1)} %get-tuple-element.71), channel_id=1, source_target_pairs={{0,3},{1,0},{2,1},{3,2},{4,7},{5,4},{6,5},{7,6},{8,11},{9,8},{10,9... | collective-permute-start | bytes 1966088 | tf_op jit(solution)/shard_map/ppermute | solution.py:228
  81.3 22.2 %collective-permute-start.14 = (f32[6,32,512]{2,1,0:T(8,128)S(1)}, f32[6,32,512]{2,1,0:T(8,128)S(1)}, u32[]{:S(2)}, u32[]{:S(2)}) collective-permute-start(f32[6,32,512]{2,1,0:T(8,128)S(1)} %get-tuple-element.68), channel_id=1, source_target_pairs={{0,1},{1,2},{2,3},{3,0},{4,5},{5,6},{6,7},{7,4},{8,9},{9,10},{10,1... | collective-permute-start | bytes 1179656 | tf_op jit(solution)/shard_map/ppermute | solution.py:228
  82.9 20.6 %collective-permute-start.17 = (f32[6,32,512]{2,1,0:T(8,128)S(1)}, f32[6,32,512]{2,1,0:T(8,128)S(1)}, u32[]{:S(2)}, u32[]{:S(2)}) collective-permute-start(f32[6,32,512]{2,1,0:T(8,128)S(1)} %get-tuple-element.75), channel_id=1, source_target_pairs={{0,3},{1,0},{2,1},{3,2},{4,7},{5,4},{6,5},{7,6},{8,11},{9,8},{10,9... | collective-permute-start | bytes 1179656 | tf_op jit(solution)/shard_map/ppermute | solution.py:228
  95.3 11.7 %collective-permute-start.19 = (f32[5,32,512]{2,1,0:T(8,128)S(1)}, f32[5,32,512]{2,1,0:T(8,128)S(1)}, u32[]{:S(2)}, u32[]{:S(2)}) collective-permute-start(f32[5,32,512]{2,1,0:T(8,128)S(1)} %get-tuple-element.79), channel_id=1, source_target_pairs={{0,1},{1,2},{2,3},{3,0},{4,5},{5,6},{6,7},{7,4},{8,9},{9,10},{10,1... | collective-permute-start | bytes 983048 | tf_op jit(solution)/shard_map/ppermute | solution.py:228
  96.9 10.1 %collective-permute-start.20 = (f32[5,32,512]{2,1,0:T(8,128)S(1)}, f32[5,32,512]{2,1,0:T(8,128)S(1)}, u32[]{:S(2)}, u32[]{:S(2)}) collective-permute-start(f32[5,32,512]{2,1,0:T(8,128)S(1)} %get-tuple-element.81), channel_id=1, source_target_pairs={{0,3},{1,0},{2,1},{3,2},{4,7},{5,4},{6,5},{7,6},{8,11},{9,8},{10,9... | collective-permute-start | bytes 983048 | tf_op jit(solution)/shard_map/ppermute | solution.py:228
  103.6 10.4 %collective-permute-start.18 = (f32[6,32,512]{2,1,0:T(8,128)S(1)}, f32[6,32,512]{2,1,0:T(8,128)S(1)}, u32[]{:S(2)}, u32[]{:S(2)}) collective-permute-start(f32[6,32,512]{2,1,0:T(8,128)S(1)} %get-tuple-element.77), channel_id=1, source_target_pairs={{0,4},{1,5},{2,6},{3,7},{4,0},{5,1},{6,2},{7,3},{8,12},{9,13},{10,... | collective-permute-start | bytes 1179656 | tf_op jit(solution)/shard_map/ppermute | solution.py:225
  107.1 10.4 %collective-permute-start.21 = (f32[5,32,512]{2,1,0:T(8,128)S(1)}, f32[5,32,512]{2,1,0:T(8,128)S(1)}, u32[]{:S(2)}, u32[]{:S(2)}) collective-permute-start(f32[5,32,512]{2,1,0:T(8,128)S(1)} %get-tuple-element.83), channel_id=1, source_target_pairs={{0,4},{1,5},{2,6},{3,7},{4,0},{5,1},{6,2},{7,3},{8,12},{9,13},{10,... | collective-permute-start | bytes 983048 | tf_op jit(solution)/shard_map/ppermute | solution.py:225

commit v4 on v3

v4 whole, which is shorter than its diff:
```python
import functools

import jax
import jax.numpy as jnp
from jax import lax
from jax.experimental import pallas as pl
from jax.experimental.pallas import tpu as pltpu
from jax.sharding import PartitionSpec as P

NPAIR = 4
RING = 4
LOOSE0, LOOSE1, DOWN, UP = range(4)
MIB = 1024 * 1024
EARLY = ((0, 0, UP), (0, 0, LOOSE0), (0, 0, LOOSE1), (0, 1, DOWN), (1, 0, LOOSE0))
FIRST = ((0, 2, DOWN), (0, 1, LOOSE0), (0, 1, LOOSE1), (0, 1, UP), (1, 1, LOOSE0))
LAST = ((1, 0, LOOSE1), (1, 0, DOWN), (1, 0, UP), (1, 1, LOOSE1), (1, 1, DOWN), (1, 1, UP))
OWN = ((0, 0), (0, 1), (1, 0), (1, 1))
BESIDE = ((2, 0), (2, 1))
ABOVE = ((0, 2), (1, 2))
CORNER_UP = ((2, 2),)
CORNER_DOWN = ((2, -1),)


def slot_table(offsets):
    dx = [offsets[k, 0] for k in range(NPAIR)]
    dy = [offsets[k, 1] for k in range(NPAIR)]
    code = [
        jnp.where(dx[k] == 0, dy[k], jnp.where(dy[k] == 0, 2, jnp.where(dy[k] < 0, 3, 4)))
        for k in range(NPAIR)
    ]
    rank = [
        sum((code[j] < code[k]).astype(jnp.int32) for j in range(NPAIR) if j != k) for k in range(NPAIR)
    ]

    def pick(values, slot):
        return sum(jnp.where(rank[k] == slot, values[k], 0) for k in range(NPAIR))

    return [(pick(dx, s), pick(dy, s), pick(list(range(NPAIR)), s)) for s in range(NPAIR)]


REMAINDER = 2.0**-8
REAL_STEPS = 128
IMAG_STEPS = 32
LADDER = (32, 16, 8, 4, 2, 1)


def encode(ref, index, value):
    points = value.shape[1] // 2
    high = value.astype(jnp.bfloat16)
    ref[index, :, : 2 * points] = high
    high = high.astype(jnp.float32)
    size = jnp.abs(high)
    inverse = jnp.where(size > 1e-37, 1.0 / jnp.maximum(size, 1e-37), 0.0)
    share = (value - high) * inverse
    real = jnp.floor(share[:, :points] * (REAL_STEPS / REMAINDER))
    real = jnp.clip(real, -REAL_STEPS, REAL_STEPS - 1)
    code = jnp.where(real >= 0, real + REAL_STEPS, real - (REAL_STEPS - 1))
    rest = jnp.floor(share[:, points:] * (IMAG_STEPS / REMAINDER)) + IMAG_STEPS
    rest = jnp.clip(rest, 0, 2 * IMAG_STEPS - 1)
    for k in LADDER:
        over = rest >= k
        code = jnp.where(over, code * 2.0**k, code)
        rest = jnp.where(over, rest - k, rest)
    ref[index, :, 2 * points :] = code.astype(jnp.bfloat16)


def decode(ref, index):
    points = ref.shape[2] // 3
    high = ref[index, :, : 2 * points].astype(jnp.float32)
    code = ref[index, :, 2 * points :].astype(jnp.float32)
    size = jnp.abs(code) * (1.0 / REAL_STEPS)
    imag = jnp.full_like(size, 0.5 - IMAG_STEPS)
    for k in LADDER:
        over = size >= 2.0**k
        size = jnp.where(over, size * 2.0**-k, size)
        imag = jnp.where(over, imag + k, imag)
    real = (size - 1.0) * REAL_STEPS + 0.5
    real = jnp.where(code >= 0, real, -real)
    share = jnp.concatenate([real * (REMAINDER / REAL_STEPS), imag * (REMAINDER / IMAG_STEPS)], axis=1)
    return high + share * jnp.abs(high)


def store_pieces(outs, place, meta, index, count):
    own_a, own_b, up_first, down_first, up_second, down_second = outs
    x_lo, y = meta[0], meta[1]
    half = place.shape[0] // 2
    rows = half // RING
    target = {
        (0, 0): (own_a, 0),
        (0, 1): (own_b, 0),
        (2, 0): (up_first, 0),
        (1, 1): (up_first, count),
        (2, 1): (down_first, 0),
        (3, 0): (down_first, count),
        (1, 0): (up_second, 0),
        (3, 1): (down_second, 0),
    }
    for (d, h), (ref, base) in target.items():
        start = lax.rem(x_lo + h, 2) * half + lax.rem(y + d, RING) * rows
        value = place[pl.ds(pl.multiple_of(start, rows), rows), :]
        if ref is up_first or ref is down_first:
            encode(ref, base + index, value)
        else:
            ref[base + index] = value


def load_tile(left, right, tile, own, parts):
    traces, points = parts[0].shape[-2:]
    for i, part in enumerate(parts):
        re, im = part[0], part[1]
        low = slice(2 * i * traces, (2 * i + 1) * traces)
        high = slice((2 * i + 1) * traces, (2 * i + 2) * traces)
        right[tile, low, :points] = re
        right[tile, high, :points] = im
        right[tile, low, points:] = im
        right[tile, high, points:] = -re
        if own is not None:
            left[own, :, low] = re.T
            left[own, :, high] = im.T


def early_kernel(meta, offsets, token, green, *refs):
    outs, (left, right, acc) = refs[:6], refs[7:]
    refs[6][...] = token[...]
    slots = slot_table(offsets)
    count = 2 * len(EARLY)
    for freq in range(2):
        for tx in range(2):
            for ty in range(2):
                load_tile(left, right, freq * 4 + tx * 2 + ty, freq * 4 + tx * 2 + ty, [green.at[tx, ty, freq]])
    for b, (tx, ty, slot) in enumerate(EARLY):
        dx, dy, _ = slots[slot]
        for freq in range(2):
            place = acc.at[freq]
            tile = freq * 4 + (tx + dx) * 2 + ty + dy
            place[...] = jnp.dot(left[freq * 4 + tx * 2 + ty], right[tile], preferred_element_type=jnp.float32)
            store_pieces(outs, place, meta, 2 * b + freq, count)


def late_kernel(groups, where, *refs):
    count = 3 + len(where)
    meta, offsets, token = refs[:3]
    outs, (out_token, left, right, acc) = refs[count:-4], refs[-4:]
    out_token[...] = token[...]
    sources = {}
    for ref, tiles in zip(refs[3:count], where):
        for i, tile in enumerate(tiles):
            sources.setdefault(tile, []).append(ref.at[i])
    for (tx, ty), parts in sources.items():
        load_tile(left, right, tx * 4 + ty + 1, tx * 3 + ty if tx < 2 else None, parts)
    slots = slot_table(offsets)
    step = 0
    for g, group in enumerate(groups):
        for b, (tx, ty, slot) in enumerate(group):
            dx, dy, _ = slots[slot]
            place = acc.at[step % 2]
            step += 1
            tile = (tx + dx) * 4 + ty + dy + 1
            place[...] = jnp.dot(left[tx * 3 + ty], right[tile], preferred_element_type=jnp.float32)
            store_pieces(outs[6 * g : 6 * g + 6], place, meta, b, len(group))


def call_blocks(kernel, counts, depth, tiles, lefts, points, arrays, token, name):
    meta, offsets, *values = arrays
    smem = pl.BlockSpec(memory_space=pltpu.SMEM)
    vmem = pl.BlockSpec(memory_space=pltpu.VMEM)
    rows = points // (2 * RING)
    out_shape = []
    for count in counts:
        kept = jax.ShapeDtypeStruct((count, rows, 2 * points), jnp.float32)
        sent = jax.ShapeDtypeStruct((2 * count, rows, 3 * points), jnp.bfloat16)
        out_shape += [kept, kept, sent, sent, kept, kept]
    *pieces, token = pl.pallas_call(
        kernel,
        out_shape=out_shape + [jax.ShapeDtypeStruct(token.shape, token.dtype)],
        in_specs=[smem, smem] + [vmem] * (1 + len(values)),
        out_specs=[vmem] * (len(out_shape) + 1),
        scratch_shapes=[
            pltpu.VMEM((lefts, points, depth), jnp.bfloat16),
            pltpu.VMEM((tiles, depth, 2 * points), jnp.bfloat16),
            pltpu.VMEM((2, points, 2 * points), jnp.float32),
        ],
        compiler_params=pltpu.CompilerParams(vmem_limit_bytes=(24 if len(values) > 1 else 14) * MIB),
        cost_estimate=pl.CostEstimate(flops=0, bytes_accessed=0, transcendentals=0),
        name=name,
    )(meta, offsets, token, *values)
    return [pieces[6 * g : 6 * g + 6] for g in range(len(counts))], token


def call_step(kernel, out_shape, token, arrays, name):
    vmem = pl.BlockSpec(memory_space=pltpu.VMEM)
    *outs, token = pl.pallas_call(
        kernel,
        out_shape=list(out_shape) + [jax.ShapeDtypeStruct(token.shape, token.dtype)],
        in_specs=[vmem] * (1 + len(arrays)),
        out_specs=[vmem] * (1 + len(out_shape)),
        compiler_params=pltpu.CompilerParams(vmem_limit_bytes=6 * MIB),
        cost_estimate=pl.CostEstimate(flops=0, bytes_accessed=0, transcendentals=0),
        name=name,
    )(token, *arrays)
    return outs, token


def swapped_kernel(token, mine, theirs, above_mine, above, beside, out_token):
    for i, part in enumerate((mine, theirs)):
        beside[i] = part[0]
    for tx in range(2):
        above[tx] = theirs[tx, 0]
    out_token[...] = token[...]


def corner_kernel(token, mine, theirs, up, down, out_token):
    for i, part in enumerate((mine, theirs)):
        up[i] = part[0, 0]
        down[i] = part[0, 1]
    out_token[...] = token[...]


def keep_kernel(token, own, before, after, rows, out_token):
    count = own.shape[0]
    for i in range(count):
        rows[i] = own[i] + decode(before, i) + decode(after, count + i)
    out_token[...] = token[...]


def give_kernel(token, kept, other, rows, out_token):
    rows[0] = kept[0]
    rows[1] = other[0]
    out_token[...] = token[...]


def second_kernel(token, up_received, down_received, up_own, down_own, *refs):
    up, down, out_token = refs[-3:]
    for i in range(up_own.shape[0]):
        encode(up, i, up_own[i] + decode(up_received, i))
        encode(down, i, down_own[i] + decode(down_received, i))
    out_token[...] = token[...]


def back_kernel(token, down_arrived, own, up_received, *refs):
    out, out_token = refs[-2:]
    count = own.shape[0]
    for i in range(count):
        out[i] = own[i] + decode(up_received, count + i) + decode(down_arrived, i)
    out_token[...] = token[...]


def final_kernel(meta, offsets, *refs):
    given, _, out = refs[-3:]
    x_lo = meta[0]
    slots = slot_table(offsets)
    for g, group in enumerate((EARLY, FIRST, LAST)):
        kept, other = refs[2 * g : 2 * g + 2]
        for b, (tx, ty, slot) in enumerate(group):
            pair = slots[slot][2]
            if g == 0:
                for freq in range(2):
                    out[tx, ty, pair, freq] = kept[2 * b + freq] + other[2 * b + freq]
            elif ty == 2:
                out[tx, 0, pair, x_lo] = given[0]
                out[tx, 0, pair, 1 - x_lo] = given[1]
            else:
                out[tx, ty, pair, x_lo] = kept[b]
                out[tx, ty, pair, 1 - x_lo] = other[b]


def final(meta, offsets, parts, given, token, shape):
    smem = pl.BlockSpec(memory_space=pltpu.SMEM)
    vmem = pl.BlockSpec(memory_space=pltpu.VMEM)
    flat = [part for group in parts for part in group]
    return pl.pallas_call(
        final_kernel,
        out_shape=jax.ShapeDtypeStruct(shape, jnp.float32),
        in_specs=[smem, smem] + [vmem] * (len(flat) + 2),
        out_specs=vmem,
        compiler_params=pltpu.CompilerParams(vmem_limit_bytes=10 * MIB),
        cost_estimate=pl.CostEstimate(flops=0, bytes_accessed=0, transcendentals=0),
        name="place_blocks",
    )(meta, offsets, *flat, given, token)


def per_device(green, offsets):
    points, traces = green.shape[5], green.shape[4]
    gx, gy = lax.axis_size("gx"), lax.axis_size("gy")
    sa = lax.axis_index("sa")
    x_lo, y = sa // RING, sa % RING
    meta = jnp.stack([x_lo, y]).astype(jnp.int32)

    def swap(value):
        return lax.ppermute(value, "sa", [(i, (i + RING) % (2 * RING)) for i in range(2 * RING)])

    def around(value, steps):
        return lax.ppermute(value, "sa", [(h * RING + i, h * RING + (i + steps) % RING) for h in range(2) for i in range(RING)])

    def tiles_from(value, dx, dy):
        perm = [
            ((ix + dx) * gy + iy + dy, ix * gy + iy)
            for ix in range(gx - dx)
            for iy in range(max(0, -dy), min(gy, gy - dy))
        ]
        return lax.ppermute(value, ("gx", "gy"), perm)

    def first(pieces):
        return around(pieces[2], 1), around(pieces[3], -1)

    def second(pieces, received, token, also=()):
        up, down = pieces[4], pieces[5]
        count, rows, columns = up.shape
        sent = jax.ShapeDtypeStruct((count, rows, columns // 2 * 3), jnp.bfloat16)
        (up, down), token = call_step(second_kernel, [sent, sent], token, [*received, up, down, *also], "second")
        return (around(up, 1), around(down, -1)), token

    def back(pieces, received, arrived, token):
        own = pieces[1]
        (out,), token = call_step(back_kernel, [own], token, [arrived[1], own, received[0], arrived[0]], "back")
        return swap(out), token

    def keep(pieces, received, arrived, token):
        (rows,), token = call_step(keep_kernel, [pieces[0]], token, [pieces[0], arrived[0], received[1]], "keep")
        return rows, token

    def blocks(group, inputs, token, name):
        kernel = functools.partial(late_kernel, (group,), [where for where, _ in inputs])
        arrays = [meta, offsets] + [value for _, value in inputs]
        (pieces,), token = call_blocks(kernel, [len(group)], 4 * traces, 12, 6, points, arrays, token, name)
        return pieces, token

    token = jnp.zeros((8, 128), jnp.float32)
    theirs = swap(lax.dynamic_index_in_dim(green, 1 - x_lo, 2, keepdims=False))
    mine = lax.dynamic_index_in_dim(green, x_lo, 2, keepdims=False)
    above_mine = tiles_from(mine[:, 0], 0, 1)
    early_count = 2 * len(EARLY)
    (early,), token = call_blocks(
        early_kernel, [early_count], 2 * traces, 8, 8, points, [meta, offsets, green], token, "early_blocks"
    )
    early_first = first(early)
    dtype, shape = green.dtype, mine.shape[2:]
    pair = jax.ShapeDtypeStruct((2,) + shape, dtype)
    pairs = jax.ShapeDtypeStruct((2, 2) + shape, dtype)
    (above, beside), token = call_step(swapped_kernel, [pair, pairs], token, [mine, theirs, above_mine], "swapped")
    above_theirs = tiles_from(above, 0, 1)
    beside = tiles_from(beside, 1, 0)
    early_second, token = second(early, early_first, token)
    (corner_up, corner_down), token = call_step(corner_kernel, [pair, pair], token, [mine, theirs], "corner")
    corner_up = tiles_from(corner_up, 1, 1)
    corner_down = tiles_from(corner_down, 1, -1)
    tiles = [(OWN, mine.reshape(4, *shape)), (OWN, theirs.reshape(4, *shape)), (ABOVE, above_mine), (ABOVE, above_theirs)]
    one, token = blocks(FIRST, tiles, token, "first_blocks")
    one_first = first(one)
    early_back, token = back(early, early_first, early_second, token)
    early_kept, token = keep(early, early_first, early_second, token)
    tiles += [(BESIDE, beside[0]), (BESIDE, beside[1]), (CORNER_UP, corner_up[:1]), (CORNER_UP, corner_up[1:])]
    tiles += [(CORNER_DOWN, corner_down[:1]), (CORNER_DOWN, corner_down[1:])]
    two, token = blocks(LAST, tiles, token, "last_blocks")
    two_first = first(two)
    one_second, token = second(one, one_first, token, [early_back])
    two_second, token = second(two, two_first, token)
    one_back, token = back(one, one_first, one_second, token)
    one_kept, token = keep(one, one_first, one_second, token)
    rows = jax.ShapeDtypeStruct((2,) + one_kept.shape[1:], jnp.float32)
    (given,), token = call_step(give_kernel, [rows], token, [one_kept, one_back], "give")
    given = tiles_from(given, 0, -1)
    two_back, token = back(two, two_first, two_second, token)
    two_kept, token = keep(two, two_first, two_second, token)
    parts = [(early_kept, early_back), (one_kept, one_back), (two_kept, two_back)]
    shape = green.shape[:2] + (NPAIR, green.shape[2], points // (2 * RING), 2 * points)
    return final(meta, offsets, parts, given, token, shape)


def solution(mesh):
    return jax.shard_map(
        per_device,
        mesh=mesh,
        in_specs=(P("gx", "gy", None, None, "sa", None), P()),
        out_specs=P("gx", "gy", None, None, "sa", None),
        check_vma=False,
    )
```

time: 120 us -> 115 us (0.958)
  the two profiles are of different devices: /device:TPU:100 before, /device:TPU:96 now
where the time goes in v4:
time: 115 us; the launch traced here: 114 us
  waiting for transfers between devices  54.5 us (47%)
  starting transfers between devices  32.1 us (28%)
  Pallas kernels  23.9 us (21%)
  local copies, waits for them, and re-layouts  3.62 us (3%)
    ppermute x6, waiting for transfers between devices, tiles_from(): return lax.ppermute(value, ('gx', 'gy'), perm)  22.7 us
    ppermute x12, waiting for transfers between devices, around(): lax.ppermute(value, 'sa', [(h * RING + i, h * RING + (i + steps) % RING)...  18.1 us
    ppermute x12, starting transfers between devices, around(): lax.ppermute(value, 'sa', [(h * RING + i, h * RING + (i + steps) % RING)...  16.7 us
    ppermute x4, waiting for transfers between devices, swap(): lax.ppermute(value, 'sa', [(i, (i + RING) % (2 * RING)) for i in range(2...  13.7 us
    pallas_call x3, Pallas kernels, call_blocks(): pl.pallas_call(kernel, out_shape=out_shape + [jax.ShapeDtypeStruct(token....  12.3 us
    ppermute x6, starting transfers between devices, tiles_from(): return lax.ppermute(value, ('gx', 'gy'), perm)  11.5 us
    pallas_call x12, Pallas kernels, call_step(): pl.pallas_call(kernel, out_shape=list(out_shape) + [jax.ShapeDtypeStruct(...  9.55 us
    ppermute x4, starting transfers between devices, swap(): lax.ppermute(value, 'sa', [(i, (i + RING) % (2 * RING)) for i in range(2...  3.92 us
  transfers between devices with their start and end apart: 22, of which 17 were waited for; matrix products, arithmetic and copies ran while one was open for 0% of the time, Pallas kernels for 18%

profile of v4, /device:TPU:96, one launch (start us, length us, event | category | flops | bytes accessed | tf_op | source)
XLA Modules:
  0.0 114.4 jit_solution(16644629640359524796)
XLA Ops:
  0.0 1.7 %dynamic-slice_bitcast_fusion = (bf16[2,2,2,256,256]{4,3,2,1,0:T(8,128)(2,1)S(1)}, bf16[2,2,1,2,256,256]{5,4,3,2,1,0:T(8,128)(2,1)S(1)}) fusion(bf16[2,2,2,2,256,256]{5,4,3,2,1,0:T(8,128)(2,1)} %green.1, s32[]{:T(128)S(6)} %select_n.21, s32[]{:T(128)S(6)} %select_n.20), kind=kLoop, calls=%fused_computation.1 | loop fusion | bytes 4194312 | tf_op jit(solution)/shard_map/jit(dynamic_index_in_dim)/squeeze | solution.py:329
  1.7 1.6 %collective-permute-start = (bf16[2,2,2,256,256]{4,3,2,1,0:T(8,128)(2,1)S(1)}, bf16[2,2,2,256,256]{4,3,2,1,0:T(8,128)(2,1)S(1)}, u32[]{:S(2)}, u32[]{:S(2)}) collective-permute-start(bf16[2,2,2,256,256]{4,3,2,1,0:T(8,128)(2,1)S(1)} %get-tuple-element.105), channel_id=1, source_target_pairs={{0,4},{1,5},{2,6},{3,7},{4,0},{5,1},{6,2},{7,3},{8,12},{9,13},{10,... | collective-permute-start | bytes 3145736 | tf_op jit(solution)/shard_map/ppermute | solution.py:290
  3.3 0.1 copy.9.offsets.refs_1_
  3.4 0.1 pad_add_fusion.meta.refs_0_
  3.4 1.6 %copy-done = bf16[2,2,2,2,256,256]{5,4,3,2,1,0:T(8,128)(2,1)S(1)} copy-done((bf16[2,2,2,2,256,256]{5,4,3,2,1,0:T(8,128)(2,1)S(1)}, bf16[2,2,2,2,256,256]{5,4,3,2,1,0:T(8,128)(2,1)}, u32[]{:S(2)}) %copy-start) | copy-done | bytes 2097176
  5.0 4.3 %early_blocks.1 = (f32[10,32,512]{2,1,0:T(8,128)S(1)}, f32[10,32,512]{2,1,0:T(8,128)S(1)}, bf16[20,32,768]{2,1,0:T(8,128)(2,1)S(1)}, bf16[20,32,768]{2,1,0:T(8,1...) custom-call(s32[2]{0:T(128)S(1)} %pad_add_fusion.meta.refs_0_, ...), custom_call_target="tpu_custom_call" | custom-call | tf_op jit(solution)/shard_map/early_blocks/pallas_call | solution.py:173
  9.4 1.7 %collective-permute-start.2 = (bf16[20,32,768]{2,1,0:T(8,128)(2,1)S(1)}, bf16[20,32,768]{2,1,0:T(8,128)(2,1)S(1)}, u32[]{:S(2)}, u32[]{:S(2)}) collective-permute-start(bf16[20,32,768]{2,1,0:T(8,128)(2,1)S(1)} %get-tuple-element.57), channel_id=1, source_target_pairs={{0,1},{1,2},{2,3},{3,0},{4,5},{5,6},{6,7},{7,4},{8,9},{9,10},{10,1... | collective-permute-start | bytes 2949128 | tf_op jit(solution)/shard_map/ppermute | solution.py:293
  11.0 1.7 %collective-permute-start.3 = (bf16[20,32,768]{2,1,0:T(8,128)(2,1)S(1)}, bf16[20,32,768]{2,1,0:T(8,128)(2,1)S(1)}, u32[]{:S(2)}, u32[]{:S(2)}) collective-permute-start(bf16[20,32,768]{2,1,0:T(8,128)(2,1)S(1)} %get-tuple-element.58), channel_id=1, source_target_pairs={{0,3},{1,0},{2,1},{3,2},{4,7},{5,4},{6,5},{7,6},{8,11},{9,8},{10,9... | collective-permute-start | bytes 2949128 | tf_op jit(solution)/shard_map/ppermute | solution.py:293
  12.7 0.1 copy.12
  12.8 2.0 %collective-permute-start.1 = (bf16[2,2,256,256]{3,2,1,0:T(8,128)(2,1)S(1)}, bf16[2,2,256,256]{3,2,1,0:T(8,128)(2,1)S(1)}, u32[]{:S(2)}, u32[]{:S(2)}) collective-permute-start(bf16[2,2,256,256]{3,2,1,0:T(8,128)(2,1)S(1)} %slice_bitcast_fusion.2), channel_id=1, source_target_pairs={{8,0},{16,8},{24,16},{32,24},{40,32},{48,40},{56,48},{72,64},{80,7... | collective-permute-start | bytes 1572872 | tf_op jit(solution)/shard_map/ppermute | solution.py:301
  14.8 14.2 %collective-permute-done.1.above_mine.refs_5_ = bf16[2,2,256,256]{3,2,1,0:T(8,128)(2,1)S(1)} collective-permute-done((bf16[2,2,256,256]{3,2,1,0:T(8,128)(2,1)S(1)}, bf16[2,2,256,256]{3,2,1,0:T(8,128)(2,1)S(1)}, u32[]{:S(2)}, u32[]{:S(2)}) %collective-permute-start.1) | collective-permute-done | bytes 524320 | tf_op jit(solution)/shard_map/ppermute | solution.py:301
  29.1 0.0 collective-permute-done.theirs
  29.1 0.1 swapped.1
  29.2 1.9 %collective-permute-start.4 = (bf16[2,2,256,256]{3,2,1,0:T(8,128)(2,1)S(1)}, bf16[2,2,256,256]{3,2,1,0:T(8,128)(2,1)S(1)}, u32[]{:S(2)}, u32[]{:S(2)}) collective-permute-start(bf16[2,2,256,256]{3,2,1,0:T(8,128)(2,1)S(1)} %get-tuple-element.63), channel_id=1, source_target_pairs={{8,0},{16,8},{24,16},{32,24},{40,32},{48,40},{56,48},{72,64},{80,7... | collective-permute-start | bytes 1572872 | tf_op jit(solution)/shard_map/ppermute | solution.py:301
  31.1 1.3 %collective-permute-start.8 = (bf16[2,2,2,256,256]{4,3,2,1,0:T(8,128)(2,1)S(1)}, bf16[2,2,2,256,256]{4,3,2,1,0:T(8,128)(2,1)S(1)}, u32[]{:S(2)}, u32[]{:S(2)}) collective-permute-start(bf16[2,2,2,256,256]{4,3,2,1,0:T(8,128)(2,1)S(1)} %get-tuple-element.73), channel_id=1, source_target_pairs={{64,0},{72,8},{80,16},{88,24},{96,32},{104,40},{112,48},{120,56},{... | collective-permute-start | bytes 3145736 | tf_op jit(solution)/shard_map/ppermute | solution.py:301
  32.4 1.5 %collective-permute-done.2.up_received = bf16[20,32,768]{2,1,0:T(8,128)(2,1)S(1)} collective-permute-done((bf16[20,32,768]{2,1,0:T(8,128)(2,1)S(1)}, bf16[20,32,768]{2,1,0:T(8,128)(2,1)S(1)}, u32[]{:S(2)}, u32[]{:S(2)}) %collective-permute-start.2) | collective-permute-done | bytes 983072 | tf_op jit(solution)/shard_map/ppermute | solution.py:293
  34.0 0.0 collective-permute-done.3.down_received.after
  34.0 2.3 %second.3 = (bf16[10,32,768]{2,1,0:T(8,128)(2,1)S(1)}, bf16[10,32,768]{2,1,0:T(8,128)(2,1)S(1)}, f32[8,128]{1,0:T(8,128)S(1)}) custom-call(f32[8,128]{1,0:T(8,128)S(1)} %get-tuple-element.56.token, bf16[20,32,768]{2,1,0:T(8,128)(2,1)S(1)} %collective-permute-done.2.up_received, bf16[20,32,768]{2,1,0:T(8,128)(2,1)S(1)} %collective-permute-done.3.down_received.after, ...), custom_call_target="tpu_custom_call" | custom-call | tf_op jit(solution)/shard_map/second/pallas_call | solution.py:192
  36.3 0.1 corner.1
  36.3 1.3 %collective-permute-start.9 = (bf16[2,2,256,256]{3,2,1,0:T(8,128)(2,1)S(1)}, bf16[2,2,256,256]{3,2,1,0:T(8,128)(2,1)S(1)}, u32[]{:S(2)}, u32[]{:S(2)}) collective-permute-start(bf16[2,2,256,256]{3,2,1,0:T(8,128)(2,1)S(1)} %get-tuple-element.74), channel_id=1, source_target_pairs={{72,0},{80,8},{88,16},{96,24},{104,32},{112,40},{120,48},{136,64},... | collective-permute-start | bytes 1572872 | tf_op jit(solution)/shard_map/ppermute | solution.py:301
  37.6 3.1 %collective-permute-start.5 = (bf16[10,32,768]{2,1,0:T(8,128)(2,1)S(1)}, bf16[10,32,768]{2,1,0:T(8,128)(2,1)S(1)}, u32[]{:S(2)}, u32[]{:S(2)}) collective-permute-start(bf16[10,32,768]{2,1,0:T(8,128)(2,1)S(1)} %get-tuple-element.65), channel_id=1, source_target_pairs={{0,3},{1,0},{2,1},{3,2},{4,7},{5,4},{6,5},{7,6},{8,11},{9,8},{10,9... | collective-permute-start | bytes 1474568 | tf_op jit(solution)/shard_map/ppermute | solution.py:293
  40.7 0.0 collective-permute-start.6
  40.7 5.8 %collective-permute-done.4.refs_6_ = bf16[2,2,256,256]{3,2,1,0:T(8,128)(2,1)S(1)} collective-permute-done((bf16[2,2,256,256]{3,2,1,0:T(8,128)(2,1)S(1)}, bf16[2,2,256,256]{3,2,1,0:T(8,128)(2,1)S(1)}, u32[]{:S(2)}, u32[]{:S(2)}) %collective-permute-start.4) | collective-permute-done | bytes 524320 | tf_op jit(solution)/shard_map/ppermute | solution.py:301
  46.6 1.5 %collective-permute-start.10 = (bf16[2,2,256,256]{3,2,1,0:T(8,128)(2,1)S(1)}, bf16[2,2,256,256]{3,2,1,0:T(8,128)(2,1)S(1)}, u32[]{:S(2)}, u32[]{:S(2)}) collective-permute-start(bf16[2,2,256,256]{3,2,1,0:T(8,128)(2,1)S(1)} %get-tuple-element.75), channel_id=1, source_target_pairs={{64,8},{72,16},{80,24},{88,32},{96,40},{104,48},{112,56},{128,72},... | collective-permute-start | bytes 1572872 | tf_op jit(solution)/shard_map/ppermute | solution.py:301
  48.0 3.6 %first_blocks.1 = (f32[5,32,512]{2,1,0:T(8,128)S(1)}, f32[5,32,512]{2,1,0:T(8,128)S(1)}, bf16[10,32,768]{2,1,0:T(8,128)(2,1)S(1)}, bf16[10,32,768]{2,1,0:T(8,128...) custom-call(s32[2]{0:T(128)S(1)} %pad_add_fusion.meta.refs_0_, ...), custom_call_target="tpu_custom_call" | custom-call | tf_op jit(solution)/shard_map/first_blocks/pallas_call | solution.py:173
  51.7 0.6 collective-permute-done.5.down_arrived
  52.2 1.0 collective-permute-start.11
  53.3 2.4 %collective-permute-done.6.refs_0_.before = bf16[10,32,768]{2,1,0:T(8,128)(2,1)S(1)} collective-permute-done((bf16[10,32,768]{2,1,0:T(8,128)(2,1)S(1)}, bf16[10,32,768]{2,1,0:T(8,128)(2,1)S(1)}, u32[]{:S(2)}, u32[]{:S(2)}) %collective-permute-start.6) | collective-permute-done | bytes 491552 | tf_op jit(solution)/shard_map/ppermute | solution.py:293
  55.6 0.3 collective-permute-start.12
  55.9 1.1 back.3
  57.0 0.0 collective-permute-done.9
  57.0 0.6 collective-permute-start.7
  57.7 0.0 collective-permute-done.10
  57.7 1.1 keep.3
  58.8 0.0 collective-permute-done.8
  58.8 0.1 slice_bitcast_fusion
  58.9 4.3 %last_blocks.1 = (f32[6,32,512]{2,1,0:T(8,128)S(1)}, f32[6,32,512]{2,1,0:T(8,128)S(1)}, bf16[12,32,768]{2,1,0:T(8,128)(2,1)S(1)}, bf16[12,32,768]{2,1,0:T(8,128)...) custom-call(s32[2]{0:T(128)S(1)} %pad_add_fusion.meta.refs_0_, ...), custom_call_target="tpu_custom_call" | custom-call | tf_op jit(solution)/shard_map/last_blocks/pallas_call | solution.py:173
  63.2 1.8 %collective-permute-start.13 = (bf16[12,32,768]{2,1,0:T(8,128)(2,1)S(1)}, bf16[12,32,768]{2,1,0:T(8,128)(2,1)S(1)}, u32[]{:S(2)}, u32[]{:S(2)}) collective-permute-start(bf16[12,32,768]{2,1,0:T(8,128)(2,1)S(1)} %get-tuple-element.82), channel_id=1, source_target_pairs={{0,1},{1,2},{2,3},{3,0},{4,5},{5,6},{6,7},{7,4},{8,9},{9,10},{10,1... | collective-permute-start | bytes 1769480 | tf_op jit(solution)/shard_map/ppermute | solution.py:293
  65.1 1.5 %collective-permute-start.14 = (bf16[12,32,768]{2,1,0:T(8,128)(2,1)S(1)}, bf16[12,32,768]{2,1,0:T(8,128)(2,1)S(1)}, u32[]{:S(2)}, u32[]{:S(2)}) collective-permute-start(bf16[12,32,768]{2,1,0:T(8,128)(2,1)S(1)} %get-tuple-element.83), channel_id=1, source_target_pairs={{0,3},{1,0},{2,1},{3,2},{4,7},{5,4},{6,5},{7,6},{8,11},{9,8},{10,9... | collective-permute-start | bytes 1769480 | tf_op jit(solution)/shard_map/ppermute | solution.py:293
  66.6 0.7 collective-permute-done.11.up_received
  67.3 1.3 %collective-permute-done.12.down_received.after = bf16[10,32,768]{2,1,0:T(8,128)(2,1)S(1)} collective-permute-done((bf16[10,32,768]{2,1,0:T(8,128)(2,1)S(1)}, bf16[10,32,768]{2,1,0:T(8,128)(2,1)S(1)}, u32[]{:S(2)}, u32[]{:S(2)}) %collective-permute-start.12) | collective-permute-done | bytes 491552 | tf_op jit(solution)/shard_map/ppermute | solution.py:293
  68.6 4.4 %collective-permute-done.7.refs_0_.refs_1_ = f32[10,32,512]{2,1,0:T(8,128)S(1)} collective-permute-done((f32[10,32,512]{2,1,0:T(8,128)S(1)}, f32[10,32,512]{2,1,0:T(8,128)S(1)}, u32[]{:S(2)}, u32[]{:S(2)}) %collective-permute-start.7) | collective-permute-done | bytes 655392 | tf_op jit(solution)/shard_map/ppermute | solution.py:290
  73.0 1.1 second.4
  74.1 3.6 %collective-permute-start.15 = (bf16[5,32,768]{2,1,0:T(8,128)(2,1)S(1)}, bf16[5,32,768]{2,1,0:T(8,128)(2,1)S(1)}, u32[]{:S(2)}, u32[]{:S(2)}) collective-permute-start(bf16[5,32,768]{2,1,0:T(8,128)(2,1)S(1)} %get-tuple-element.87), channel_id=1, source_target_pairs={{0,3},{1,0},{2,1},{3,2},{4,7},{5,4},{6,5},{7,6},{8,11},{9,8},{10,9... | collective-permute-start | bytes 737288 | tf_op jit(solution)/shard_map/ppermute | solution.py:293
  77.7 0.1 collective-permute-done.13.up_received
  77.8 2.0 %collective-permute-done.14.down_received.after = bf16[12,32,768]{2,1,0:T(8,128)(2,1)S(1)} collective-permute-done((bf16[12,32,768]{2,1,0:T(8,128)(2,1)S(1)}, bf16[12,32,768]{2,1,0:T(8,128)(2,1)S(1)}, u32[]{:S(2)}, u32[]{:S(2)}) %collective-permute-start.14) | collective-permute-done | bytes 589856 | tf_op jit(solution)/shard_map/ppermute | solution.py:293
  79.9 1.4 %second.5 = (bf16[6,32,768]{2,1,0:T(8,128)(2,1)S(1)}, bf16[6,32,768]{2,1,0:T(8,128)(2,1)S(1)}, f32[8,128]{1,0:T(8,128)S(1)}) custom-call(f32[8,128]{1,0:T(8,128)S(1)} %get-tuple-element.81.token, bf16[12,32,768]{2,1,0:T(8,128)(2,1)S(1)} %collective-permute-done.13.up_received, bf16[12,32,768]{2,1,0:T(8,128)(2,1)S(1)} %collective-permute-done.14.down_received.after, ...), custom_call_target="tpu_custom_call" | custom-call | tf_op jit(solution)/shard_map/second/pallas_call | solution.py:192
  81.3 3.9 %collective-permute-done.15.down_arrived = bf16[5,32,768]{2,1,0:T(8,128)(2,1)S(1)} collective-permute-done((bf16[5,32,768]{2,1,0:T(8,128)(2,1)S(1)}, bf16[5,32,768]{2,1,0:T(8,128)(2,1)S(1)}, u32[]{:S(2)}, u32[]{:S(2)}) %collective-permute-start.15) | collective-permute-done | bytes 245792 | tf_op jit(solution)/shard_map/ppermute | solution.py:293
  85.2 1.7 %collective-permute-done.16.refs_0_.before = bf16[5,32,768]{2,1,0:T(8,128)(2,1)S(1)} collective-permute-done((bf16[5,32,768]{2,1,0:T(8,128)(2,1)S(1)}, bf16[5,32,768]{2,1,0:T(8,128)(2,1)S(1)}, u32[]{:S(2)}, u32[]{:S(2)}) %collective-permute-start.16) | collective-permute-done | bytes 245792 | tf_op jit(solution)/shard_map/ppermute | solution.py:293
  86.9 0.5 back.4
  87.4 1.1 collective-permute-start.17
  88.5 1.5 %collective-permute-start.18 = (bf16[6,32,768]{2,1,0:T(8,128)(2,1)S(1)}, bf16[6,32,768]{2,1,0:T(8,128)(2,1)S(1)}, u32[]{:S(2)}, u32[]{:S(2)}) collective-permute-start(bf16[6,32,768]{2,1,0:T(8,128)(2,1)S(1)} %get-tuple-element.96), channel_id=1, source_target_pairs={{0,3},{1,0},{2,1},{3,2},{4,7},{5,4},{6,5},{7,6},{8,11},{9,8},{10,9... | collective-permute-start | bytes 884744 | tf_op jit(solution)/shard_map/ppermute | solution.py:293
  90.0 0.5 collective-permute-start.19
  90.5 0.5 keep.4
  91.1 5.9 %collective-permute-done.17.other.refs_3_ = f32[5,32,512]{2,1,0:T(8,128)S(1)} collective-permute-done((f32[5,32,512]{2,1,0:T(8,128)S(1)}, f32[5,32,512]{2,1,0:T(8,128)S(1)}, u32[]{:S(2)}, u32[]{:S(2)}) %collective-permute-start.17) | collective-permute-done | bytes 327712 | tf_op jit(solution)/shard_map/ppermute | solution.py:290
  96.9 0.4 collective-permute-done.18.down_arrived
  97.3 3.4 %collective-permute-done.19.refs_0_.before = bf16[6,32,768]{2,1,0:T(8,128)(2,1)S(1)} collective-permute-done((bf16[6,32,768]{2,1,0:T(8,128)(2,1)S(1)}, bf16[6,32,768]{2,1,0:T(8,128)(2,1)S(1)}, u32[]{:S(2)}, u32[]{:S(2)}) %collective-permute-start.19) | collective-permute-done | bytes 294944 | tf_op jit(solution)/shard_map/ppermute | solution.py:293
  100.8 0.7 back.5
  101.4 0.6 collective-permute-start.20
  102.0 3.5 %collective-permute-start.21 = (f32[2,32,512]{2,1,0:T(8,128)S(1)}, f32[2,32,512]{2,1,0:T(8,128)S(1)}, u32[]{:S(2)}, u32[]{:S(2)}) collective-permute-start(f32[2,32,512]{2,1,0:T(8,128)S(1)} %get-tuple-element.103), channel_id=1, source_target_pairs={{0,8},{8,16},{16,24},{24,32},{32,40},{40,48},{48,56},{64,72},{72,8... | collective-permute-start | bytes 393224 | tf_op jit(solution)/shard_map/ppermute | solution.py:301
  105.5 0.7 keep.5
  106.2 2.7 %collective-permute-done.21.refs_6_ = f32[2,32,512]{2,1,0:T(8,128)S(1)} collective-permute-done((f32[2,32,512]{2,1,0:T(8,128)S(1)}, f32[2,32,512]{2,1,0:T(8,128)S(1)}, u32[]{:S(2)}, u32[]{:S(2)}) %collective-permute-start.21) | collective-permute-done | bytes 131104 | tf_op jit(solution)/shard_map/ppermute | solution.py:301
  108.9 3.5 %collective-permute-done.20.refs_5_ = f32[6,32,512]{2,1,0:T(8,128)S(1)} collective-permute-done((f32[6,32,512]{2,1,0:T(8,128)S(1)}, f32[6,32,512]{2,1,0:T(8,128)S(1)}, u32[]{:S(2)}, u32[]{:S(2)}) %collective-permute-start.20) | collective-permute-done | bytes 393248 | tf_op jit(solution)/shard_map/ppermute | solution.py:290
  112.3 2.1 %place_blocks.1 = f32[2,2,4,2,32,512]{5,4,3,2,1,0:T(8,128)} custom-call(s32[2]{0:T(128)S(1)} %pad_add_fusion.meta.refs_0_, s32[4,2]{1,0:T(4,128)S(1)} %copy.9.offsets.refs_1_, f32[10,32,512]{2,1,0:T(8,128)S(1)} %get-tuple-element.70.refs_0_, f32[10,32,512]{2,1,0:T(8,128)S(1)} %collective-permute-done.7.refs_0_.refs_1_, ...), custom_call_target="tpu_custom_call" | custom-call | tf_op jit(solution)/shard_map/place_blocks/pallas_call | solution.py:271
  (9 shorter events, 0.1 us)
Async XLA Ops:
  0.0 3.3 %copy-start.1 = (s32[4,2]{0,1:T(2,128)S(1)}, s32[4,2]{0,1:T(2,128)}, u32[]{:S(2)}) copy-start(s32[4,2]{0,1:T(2,128)} %param.3) | copy-start | bytes 100
  1.7 27.4 %collective-permute-start = (bf16[2,2,2,256,256]{4,3,2,1,0:T(8,128)(2,1)S(1)}, bf16[2,2,2,256,256]{4,3,2,1,0:T(8,128)(2,1)S(1)}, u32[]{:S(2)}, u32[]{:S(2)}) collective-permute-start(bf16[2,2,2,256,256]{4,3,2,1,0:T(8,128)(2,1)S(1)} %get-tuple-element.105), channel_id=1, source_target_pairs={{0,4},{1,5},{2,6},{3,7},{4,0},{5,1},{6,2},{7,3},{8,12},{9,13},{10,... | collective-permute-start | bytes 3145736 | tf_op jit(solution)/shard_map/ppermute | solution.py:290
  3.4 1.6 %copy-start = (bf16[2,2,2,2,256,256]{5,4,3,2,1,0:T(8,128)(2,1)S(1)}, bf16[2,2,2,2,256,256]{5,4,3,2,1,0:T(8,128)(2,1)}, u32[]{:S(2)}) copy-start(bf16[2,2,2,2,256,256]{5,4,3,2,1,0:T(8,128)(2,1)} %green.1) | copy-start | bytes 6291460
  9.4 24.6 %collective-permute-start.2 = (bf16[20,32,768]{2,1,0:T(8,128)(2,1)S(1)}, bf16[20,32,768]{2,1,0:T(8,128)(2,1)S(1)}, u32[]{:S(2)}, u32[]{:S(2)}) collective-permute-start(bf16[20,32,768]{2,1,0:T(8,128)(2,1)S(1)} %get-tuple-element.57), channel_id=1, source_target_pairs={{0,1},{1,2},{2,3},{3,0},{4,5},{5,6},{6,7},{7,4},{8,9},{9,10},{10,1... | collective-permute-start | bytes 2949128 | tf_op jit(solution)/shard_map/ppermute | solution.py:293
  11.0 22.9 %collective-permute-start.3 = (bf16[20,32,768]{2,1,0:T(8,128)(2,1)S(1)}, bf16[20,32,768]{2,1,0:T(8,128)(2,1)S(1)}, u32[]{:S(2)}, u32[]{:S(2)}) collective-permute-start(bf16[20,32,768]{2,1,0:T(8,128)(2,1)S(1)} %get-tuple-element.58), channel_id=1, source_target_pairs={{0,3},{1,0},{2,1},{3,2},{4,7},{5,4},{6,5},{7,6},{8,11},{9,8},{10,9... | collective-permute-start | bytes 2949128 | tf_op jit(solution)/shard_map/ppermute | solution.py:293
  12.8 16.3 %collective-permute-start.1 = (bf16[2,2,256,256]{3,2,1,0:T(8,128)(2,1)S(1)}, bf16[2,2,256,256]{3,2,1,0:T(8,128)(2,1)S(1)}, u32[]{:S(2)}, u32[]{:S(2)}) collective-permute-start(bf16[2,2,256,256]{3,2,1,0:T(8,128)(2,1)S(1)} %slice_bitcast_fusion.2), channel_id=1, source_target_pairs={{8,0},{16,8},{24,16},{32,24},{40,32},{48,40},{56,48},{72,64},{80,7... | collective-permute-start | bytes 1572872 | tf_op jit(solution)/shard_map/ppermute | solution.py:301
  29.2 17.4 %collective-permute-start.4 = (bf16[2,2,256,256]{3,2,1,0:T(8,128)(2,1)S(1)}, bf16[2,2,256,256]{3,2,1,0:T(8,128)(2,1)S(1)}, u32[]{:S(2)}, u32[]{:S(2)}) collective-permute-start(bf16[2,2,256,256]{3,2,1,0:T(8,128)(2,1)S(1)} %get-tuple-element.63), channel_id=1, source_target_pairs={{8,0},{16,8},{24,16},{32,24},{40,32},{48,40},{56,48},{72,64},{80,7... | collective-permute-start | bytes 1572872 | tf_op jit(solution)/shard_map/ppermute | solution.py:301
  31.1 27.7 %collective-permute-start.8 = (bf16[2,2,2,256,256]{4,3,2,1,0:T(8,128)(2,1)S(1)}, bf16[2,2,2,256,256]{4,3,2,1,0:T(8,128)(2,1)S(1)}, u32[]{:S(2)}, u32[]{:S(2)}) collective-permute-start(bf16[2,2,2,256,256]{4,3,2,1,0:T(8,128)(2,1)S(1)} %get-tuple-element.73), channel_id=1, source_target_pairs={{64,0},{72,8},{80,16},{88,24},{96,32},{104,40},{112,48},{120,56},{... | collective-permute-start | bytes 3145736 | tf_op jit(solution)/shard_map/ppermute | solution.py:301
  36.3 20.7 %collective-permute-start.9 = (bf16[2,2,256,256]{3,2,1,0:T(8,128)(2,1)S(1)}, bf16[2,2,256,256]{3,2,1,0:T(8,128)(2,1)S(1)}, u32[]{:S(2)}, u32[]{:S(2)}) collective-permute-start(bf16[2,2,256,256]{3,2,1,0:T(8,128)(2,1)S(1)} %get-tuple-element.74), channel_id=1, source_target_pairs={{72,0},{80,8},{88,16},{96,24},{104,32},{112,40},{120,48},{136,64},... | collective-permute-start | bytes 1572872 | tf_op jit(solution)/shard_map/ppermute | solution.py:301
  37.6 14.6 %collective-permute-start.5 = (bf16[10,32,768]{2,1,0:T(8,128)(2,1)S(1)}, bf16[10,32,768]{2,1,0:T(8,128)(2,1)S(1)}, u32[]{:S(2)}, u32[]{:S(2)}) collective-permute-start(bf16[10,32,768]{2,1,0:T(8,128)(2,1)S(1)} %get-tuple-element.65), channel_id=1, source_target_pairs={{0,3},{1,0},{2,1},{3,2},{4,7},{5,4},{6,5},{7,6},{8,11},{9,8},{10,9... | collective-permute-start | bytes 1474568 | tf_op jit(solution)/shard_map/ppermute | solution.py:293
  40.7 14.9 %collective-permute-start.6 = (bf16[10,32,768]{2,1,0:T(8,128)(2,1)S(1)}, bf16[10,32,768]{2,1,0:T(8,128)(2,1)S(1)}, u32[]{:S(2)}, u32[]{:S(2)}) collective-permute-start(bf16[10,32,768]{2,1,0:T(8,128)(2,1)S(1)} %get-tuple-element.67), channel_id=1, source_target_pairs={{0,1},{1,2},{2,3},{3,0},{4,5},{5,6},{6,7},{7,4},{8,9},{9,10},{10,1... | collective-permute-start | bytes 1474568 | tf_op jit(solution)/shard_map/ppermute | solution.py:293
  46.6 11.1 %collective-permute-start.10 = (bf16[2,2,256,256]{3,2,1,0:T(8,128)(2,1)S(1)}, bf16[2,2,256,256]{3,2,1,0:T(8,128)(2,1)S(1)}, u32[]{:S(2)}, u32[]{:S(2)}) collective-permute-start(bf16[2,2,256,256]{3,2,1,0:T(8,128)(2,1)S(1)} %get-tuple-element.75), channel_id=1, source_target_pairs={{64,8},{72,16},{80,24},{88,32},{96,40},{104,48},{112,56},{128,72},... | collective-permute-start | bytes 1572872 | tf_op jit(solution)/shard_map/ppermute | solution.py:301
  52.2 15.1 %collective-permute-start.11 = (bf16[10,32,768]{2,1,0:T(8,128)(2,1)S(1)}, bf16[10,32,768]{2,1,0:T(8,128)(2,1)S(1)}, u32[]{:S(2)}, u32[]{:S(2)}) collective-permute-start(bf16[10,32,768]{2,1,0:T(8,128)(2,1)S(1)} %get-tuple-element.77), channel_id=1, source_target_pairs={{0,1},{1,2},{2,3},{3,0},{4,5},{5,6},{6,7},{7,4},{8,9},{9,10},{10,1... | collective-permute-start | bytes 1474568 | tf_op jit(solution)/shard_map/ppermute | solution.py:293
  55.6 12.9 %collective-permute-start.12 = (bf16[10,32,768]{2,1,0:T(8,128)(2,1)S(1)}, bf16[10,32,768]{2,1,0:T(8,128)(2,1)S(1)}, u32[]{:S(2)}, u32[]{:S(2)}) collective-permute-start(bf16[10,32,768]{2,1,0:T(8,128)(2,1)S(1)} %get-tuple-element.78), channel_id=1, source_target_pairs={{0,3},{1,0},{2,1},{3,2},{4,7},{5,4},{6,5},{7,6},{8,11},{9,8},{10,9... | collective-permute-start | bytes 1474568 | tf_op jit(solution)/shard_map/ppermute | solution.py:293
  57.0 16.0 %collective-permute-start.7 = (f32[10,32,512]{2,1,0:T(8,128)S(1)}, f32[10,32,512]{2,1,0:T(8,128)S(1)}, u32[]{:S(2)}, u32[]{:S(2)}) collective-permute-start(f32[10,32,512]{2,1,0:T(8,128)S(1)} %get-tuple-element.71), channel_id=1, source_target_pairs={{0,4},{1,5},{2,6},{3,7},{4,0},{5,1},{6,2},{7,3},{8,12},{9,13},{10,... | collective-permute-start | bytes 1966088 | tf_op jit(solution)/shard_map/ppermute | solution.py:290
  63.2 14.6 %collective-permute-start.13 = (bf16[12,32,768]{2,1,0:T(8,128)(2,1)S(1)}, bf16[12,32,768]{2,1,0:T(8,128)(2,1)S(1)}, u32[]{:S(2)}, u32[]{:S(2)}) collective-permute-start(bf16[12,32,768]{2,1,0:T(8,128)(2,1)S(1)} %get-tuple-element.82), channel_id=1, source_target_pairs={{0,1},{1,2},{2,3},{3,0},{4,5},{5,6},{6,7},{7,4},{8,9},{9,10},{10,1... | collective-permute-start | bytes 1769480 | tf_op jit(solution)/shard_map/ppermute | solution.py:293
  65.1 14.8 %collective-permute-start.14 = (bf16[12,32,768]{2,1,0:T(8,128)(2,1)S(1)}, bf16[12,32,768]{2,1,0:T(8,128)(2,1)S(1)}, u32[]{:S(2)}, u32[]{:S(2)}) collective-permute-start(bf16[12,32,768]{2,1,0:T(8,128)(2,1)S(1)} %get-tuple-element.83), channel_id=1, source_target_pairs={{0,3},{1,0},{2,1},{3,2},{4,7},{5,4},{6,5},{7,6},{8,11},{9,8},{10,9... | collective-permute-start | bytes 1769480 | tf_op jit(solution)/shard_map/ppermute | solution.py:293
  74.1 11.0 %collective-permute-start.15 = (bf16[5,32,768]{2,1,0:T(8,128)(2,1)S(1)}, bf16[5,32,768]{2,1,0:T(8,128)(2,1)S(1)}, u32[]{:S(2)}, u32[]{:S(2)}) collective-permute-start(bf16[5,32,768]{2,1,0:T(8,128)(2,1)S(1)} %get-tuple-element.87), channel_id=1, source_target_pairs={{0,3},{1,0},{2,1},{3,2},{4,7},{5,4},{6,5},{7,6},{8,11},{9,8},{10,9... | collective-permute-start | bytes 737288 | tf_op jit(solution)/shard_map/ppermute | solution.py:293
  77.7 9.2 %collective-permute-start.16 = (bf16[5,32,768]{2,1,0:T(8,128)(2,1)S(1)}, bf16[5,32,768]{2,1,0:T(8,128)(2,1)S(1)}, u32[]{:S(2)}, u32[]{:S(2)}) collective-permute-start(bf16[5,32,768]{2,1,0:T(8,128)(2,1)S(1)} %get-tuple-element.89), channel_id=1, source_target_pairs={{0,1},{1,2},{2,3},{3,0},{4,5},{5,6},{6,7},{7,4},{8,9},{9,10},{10,1... | collective-permute-start | bytes 737288 | tf_op jit(solution)/shard_map/ppermute | solution.py:293
  87.4 9.5 %collective-permute-start.17 = (f32[5,32,512]{2,1,0:T(8,128)S(1)}, f32[5,32,512]{2,1,0:T(8,128)S(1)}, u32[]{:S(2)}, u32[]{:S(2)}) collective-permute-start(f32[5,32,512]{2,1,0:T(8,128)S(1)} %get-tuple-element.93), channel_id=1, source_target_pairs={{0,4},{1,5},{2,6},{3,7},{4,0},{5,1},{6,2},{7,3},{8,12},{9,13},{10,... | collective-permute-start | bytes 983048 | tf_op jit(solution)/shard_map/ppermute | solution.py:290
  88.5 8.8 %collective-permute-start.18 = (bf16[6,32,768]{2,1,0:T(8,128)(2,1)S(1)}, bf16[6,32,768]{2,1,0:T(8,128)(2,1)S(1)}, u32[]{:S(2)}, u32[]{:S(2)}) collective-permute-start(bf16[6,32,768]{2,1,0:T(8,128)(2,1)S(1)} %get-tuple-element.96), channel_id=1, source_target_pairs={{0,3},{1,0},{2,1},{3,2},{4,7},{5,4},{6,5},{7,6},{8,11},{9,8},{10,9... | collective-permute-start | bytes 884744 | tf_op jit(solution)/shard_map/ppermute | solution.py:293
  90.0 10.7 %collective-permute-start.19 = (bf16[6,32,768]{2,1,0:T(8,128)(2,1)S(1)}, bf16[6,32,768]{2,1,0:T(8,128)(2,1)S(1)}, u32[]{:S(2)}, u32[]{:S(2)}) collective-permute-start(bf16[6,32,768]{2,1,0:T(8,128)(2,1)S(1)} %get-tuple-element.98), channel_id=1, source_target_pairs={{0,1},{1,2},{2,3},{3,0},{4,5},{5,6},{6,7},{7,4},{8,9},{9,10},{10,1... | collective-permute-start | bytes 884744 | tf_op jit(solution)/shard_map/ppermute | solution.py:293
  101.4 10.9 %collective-permute-start.20 = (f32[6,32,512]{2,1,0:T(8,128)S(1)}, f32[6,32,512]{2,1,0:T(8,128)S(1)}, u32[]{:S(2)}, u32[]{:S(2)}) collective-permute-start(f32[6,32,512]{2,1,0:T(8,128)S(1)} %get-tuple-element.102), channel_id=1, source_target_pairs={{0,4},{1,5},{2,6},{3,7},{4,0},{5,1},{6,2},{7,3},{8,12},{9,13},{10,... | collective-permute-start | bytes 1179656 | tf_op jit(solution)/shard_map/ppermute | solution.py:290
  102.0 6.8 %collective-permute-start.21 = (f32[2,32,512]{2,1,0:T(8,128)S(1)}, f32[2,32,512]{2,1,0:T(8,128)S(1)}, u32[]{:S(2)}, u32[]{:S(2)}) collective-permute-start(f32[2,32,512]{2,1,0:T(8,128)S(1)} %get-tuple-element.103), channel_id=1, source_target_pairs={{0,8},{8,16},{16,24},{24,32},{32,40},{40,48},{48,56},{64,72},{72,8... | collective-permute-start | bytes 393224 | tf_op jit(solution)/shard_map/ppermute | solution.py:301

commit v5 on v4

--- a/solution.py
+++ b/solution.py
@@ -12,13 +12,13 @@
 LOOSE0, LOOSE1, DOWN, UP = range(4)
 MIB = 1024 * 1024
 EARLY = ((0, 0, UP), (0, 0, LOOSE0), (0, 0, LOOSE1), (0, 1, DOWN), (1, 0, LOOSE0))
-FIRST = ((0, 2, DOWN), (0, 1, LOOSE0), (0, 1, LOOSE1), (0, 1, UP), (1, 1, LOOSE0))
-LAST = ((1, 0, LOOSE1), (1, 0, DOWN), (1, 0, UP), (1, 1, LOOSE1), (1, 1, DOWN), (1, 1, UP))
+GIVEN = 2
+FIRST = ((0, 2, DOWN), (1, 2, DOWN), (0, 1, LOOSE0), (0, 1, LOOSE1), (0, 1, UP), (1, 1, LOOSE0))
+LAST = ((1, 0, LOOSE1), (1, 0, UP), (1, 1, LOOSE1), (1, 1, DOWN), (1, 1, UP))
 OWN = ((0, 0), (0, 1), (1, 0), (1, 1))
 BESIDE = ((2, 0), (2, 1))
 ABOVE = ((0, 2), (1, 2))
-CORNER_UP = ((2, 2),)
-CORNER_DOWN = ((2, -1),)
+CORNER = ((2, 2),)
 
 
 def slot_table(offsets):
@@ -39,9 +39,8 @@
 
 
 REMAINDER = 2.0**-8
-REAL_STEPS = 128
-IMAG_STEPS = 32
-LADDER = (32, 16, 8, 4, 2, 1)
+REAL_STEPS = 127
+IMAG_STEPS = 31
 
 
 def encode(ref, index, value):
@@ -52,30 +51,23 @@
     size = jnp.abs(high)
     inverse = jnp.where(size > 1e-37, 1.0 / jnp.maximum(size, 1e-37), 0.0)
     share = (value - high) * inverse
-    real = jnp.floor(share[:, :points] * (REAL_STEPS / REMAINDER))
-    real = jnp.clip(real, -REAL_STEPS, REAL_STEPS - 1)
-    code = jnp.where(real >= 0, real + REAL_STEPS, real - (REAL_STEPS - 1))
-    rest = jnp.floor(share[:, points:] * (IMAG_STEPS / REMAINDER)) + IMAG_STEPS
-    rest = jnp.clip(rest, 0, 2 * IMAG_STEPS - 1)
-    for k in LADDER:
-        over = rest >= k
-        code = jnp.where(over, code * 2.0**k, code)
-        rest = jnp.where(over, rest - k, rest)
-    ref[index, :, 2 * points :] = code.astype(jnp.bfloat16)
+    real = jnp.floor(share[:, :points] * (REAL_STEPS / REMAINDER) + 0.5)
+    real = jnp.clip(real, -REAL_STEPS, REAL_STEPS)
+    code = jnp.where(real >= 0, real + 128, real - 127)
+    rest = jnp.floor(share[:, points:] * (IMAG_STEPS / REMAINDER) + 0.5)
+    rest = jnp.clip(rest, -IMAG_STEPS, IMAG_STEPS) + IMAG_STEPS
+    ref[index, :, 2 * points :] = (code * jnp.exp2(rest)).astype(jnp.bfloat16)
 
 
 def decode(ref, index):
     points = ref.shape[2] // 3
     high = ref[index, :, : 2 * points].astype(jnp.float32)
     code = ref[index, :, 2 * points :].astype(jnp.float32)
-    size = jnp.abs(code) * (1.0 / REAL_STEPS)
-    imag = jnp.full_like(size, 0.5 - IMAG_STEPS)
-    for k in LADDER:
-        over = size >= 2.0**k
-        size = jnp.where(over, size * 2.0**-k, size)
-        imag = jnp.where(over, imag + k, imag)
-    real = (size - 1.0) * REAL_STEPS + 0.5
-    real = jnp.where(code >= 0, real, -real)
+    size = jnp.maximum(jnp.abs(code) * (1.0 / 128), 1.0)
+    power = jnp.floor(jnp.log2(size) + 0.002)
+    imag = power - IMAG_STEPS
+    real = size * jnp.exp2(-power) * 128 - 128
+    real = jnp.where(code >= 0, real, -1 - real)
     share = jnp.concatenate([real * (REMAINDER / REAL_STEPS), imag * (REMAINDER / IMAG_STEPS)], axis=1)
     return high + share * jnp.abs(high)
 
@@ -147,7 +139,7 @@
         for i, tile in enumerate(tiles):
             sources.setdefault(tile, []).append(ref.at[i])
     for (tx, ty), parts in sources.items():
-        load_tile(left, right, tx * 4 + ty + 1, tx * 3 + ty if tx < 2 else None, parts)
+        load_tile(left, right, tx * 3 + ty, tx * 3 + ty if tx < 2 else None, parts)
     slots = slot_table(offsets)
     step = 0
     for g, group in enumerate(groups):
@@ -155,7 +147,7 @@
             dx, dy, _ = slots[slot]
             place = acc.at[step % 2]
             step += 1
-            tile = (tx + dx) * 4 + ty + dy + 1
+            tile = (tx + dx) * 3 + ty + dy
             place[...] = jnp.dot(left[tx * 3 + ty], right[tile], preferred_element_type=jnp.float32)
             store_pieces(outs[6 * g : 6 * g + 6], place, meta, b, len(group))
 
@@ -187,7 +179,7 @@
     return [pieces[6 * g : 6 * g + 6] for g in range(len(counts))], token
 
 
-def call_step(kernel, out_shape, token, arrays, name):
+def call_step(kernel, out_shape, token, arrays, name, size=0):
     vmem = pl.BlockSpec(memory_space=pltpu.VMEM)
     *outs, token = pl.pallas_call(
         kernel,
@@ -195,24 +187,18 @@
         in_specs=[vmem] * (1 + len(arrays)),
         out_specs=[vmem] * (1 + len(out_shape)),
         compiler_params=pltpu.CompilerParams(vmem_limit_bytes=6 * MIB),
-        cost_estimate=pl.CostEstimate(flops=0, bytes_accessed=0, transcendentals=0),
+        cost_estimate=pl.CostEstimate(flops=0, bytes_accessed=size, transcendentals=0),
         name=name,
     )(token, *arrays)
     return outs, token
 
 
-def swapped_kernel(token, mine, theirs, above_mine, above, beside, out_token):
+def swapped_kernel(token, mine, theirs, above_mine, above, beside, corner, out_token):
     for i, part in enumerate((mine, theirs)):
         beside[i] = part[0]
+        corner[i] = part[0, 0]
     for tx in range(2):
         above[tx] = theirs[tx, 0]
-    out_token[...] = token[...]
-
-
-def corner_kernel(token, mine, theirs, up, down, out_token):
-    for i, part in enumerate((mine, theirs)):
-        up[i] = part[0, 0]
-        down[i] = part[0, 1]
     out_token[...] = token[...]
 
 
@@ -224,8 +210,9 @@
 
 
 def give_kernel(token, kept, other, rows, out_token):
-    rows[0] = kept[0]
-    rows[1] = other[0]
+    for i in range(GIVEN):
+        encode(rows, i, kept[i])
+        rows[GIVEN + i] = other[i]
     out_token[...] = token[...]
 
 
@@ -234,6 +221,9 @@
     for i in range(up_own.shape[0]):
         encode(up, i, up_own[i] + decode(up_received, i))
         encode(down, i, down_own[i] + decode(down_received, i))
+    for i in range(up_own.shape[0], up.shape[0]):
+        up[i] = jnp.zeros_like(up[i])
+        down[i] = jnp.zeros_like(down[i])
     out_token[...] = token[...]
 
 
@@ -241,7 +231,7 @@
     out, out_token = refs[-2:]
     count = own.shape[0]
     for i in range(count):
-        out[i] = own[i] + decode(up_received, count + i) + decode(down_arrived, i)
+        encode(out, i, own[i] + decode(up_received, count + i) + decode(down_arrived, i))
     out_token[...] = token[...]
 
 
@@ -255,13 +245,13 @@
             pair = slots[slot][2]
             if g == 0:
                 for freq in range(2):
-                    out[tx, ty, pair, freq] = kept[2 * b + freq] + other[2 * b + freq]
+                    out[tx, ty, pair, freq] = kept[2 * b + freq] + decode(other, 2 * b + freq)
             elif ty == 2:
-                out[tx, 0, pair, x_lo] = given[0]
-                out[tx, 0, pair, 1 - x_lo] = given[1]
+                out[tx, 0, pair, x_lo] = decode(given, b)
+                out[tx, 0, pair, 1 - x_lo] = decode(given, GIVEN + b)
             else:
                 out[tx, ty, pair, x_lo] = kept[b]
-                out[tx, ty, pair, 1 - x_lo] = other[b]
+                out[tx, ty, pair, 1 - x_lo] = decode(other, b)
 
 
 def final(meta, offsets, parts, given, token, shape):
@@ -300,30 +290,31 @@
         ]
         return lax.ppermute(value, ("gx", "gy"), perm)
 
+    def coded(value, spare=0):
+        count, rows, columns = value.shape
+        return jax.ShapeDtypeStruct((count + spare, rows, columns // 2 * 3), jnp.bfloat16)
+
     def first(pieces):
         return around(pieces[2], 1), around(pieces[3], -1)
 
-    def second(pieces, received, token, also=()):
+    def second(pieces, received, token, also=(), spare=0):
         up, down = pieces[4], pieces[5]
-        count, rows, columns = up.shape
-        sent = jax.ShapeDtypeStruct((count, rows, columns // 2 * 3), jnp.bfloat16)
-        (up, down), token = call_step(second_kernel, [sent, sent], token, [*received, up, down, *also], "second")
+        (up, down), token = call_step(second_kernel, [coded(up, spare), coded(down, spare)], token, [*received, up, down, *also], "second")
         return (around(up, 1), around(down, -1)), token
 
     def back(pieces, received, arrived, token):
         own = pieces[1]
-        (out,), token = call_step(back_kernel, [own], token, [arrived[1], own, received[0], arrived[0]], "back")
+        (out,), token = call_step(back_kernel, [coded(own)], token, [arrived[1], own, received[0], arrived[0]], "back")
         return swap(out), token
 
     def keep(pieces, received, arrived, token):
-        (rows,), token = call_step(keep_kernel, [pieces[0]], token, [pieces[0], arrived[0], received[1]], "keep")
+        (rows,), token = call_step(keep_kernel, [pieces[0]], token, [pieces[0], arrived[0], received[1]], "keep", 16 * MIB)
         return rows, token
 
-    def blocks(group, inputs, token, name):
-        kernel = functools.partial(late_kernel, (group,), [where for where, _ in inputs])
+    def blocks(groups, inputs, token, name):
+        kernel = functools.partial(late_kernel, groups, [where for where, _ in inputs])
         arrays = [meta, offsets] + [value for _, value in inputs]
-        (pieces,), token = call_blocks(kernel, [len(group)], 4 * traces, 12, 6, points, arrays, token, name)
-        return pieces, token
+        return call_blocks(kernel, [len(group) for group in groups], 4 * traces, 9, 6, points, arrays, token, name)
 
     token = jnp.zeros((8, 128), jnp.float32)
     theirs = swap(lax.dynamic_index_in_dim(green, 1 - x_lo, 2, keepdims=False))
@@ -337,30 +328,29 @@
     dtype, shape = green.dtype, mine.shape[2:]
     pair = jax.ShapeDtypeStruct((2,) + shape, dtype)
     pairs = jax.ShapeDtypeStruct((2, 2) + shape, dtype)
-    (above, beside), token = call_step(swapped_kernel, [pair, pairs], token, [mine, theirs, above_mine], "swapped")
+    sent, token = call_step(swapped_kernel, [pair, pairs, pair], token, [mine, theirs, above_mine], "swapped")
+    above, beside, corner = sent
     above_theirs = tiles_from(above, 0, 1)
     beside = tiles_from(beside, 1, 0)
+    corner = tiles_from(corner, 1, 1)
     early_second, token = second(early, early_first, token)
-    (corner_up, corner_down), token = call_step(corner_kernel, [pair, pair], token, [mine, theirs], "corner")
-    corner_up = tiles_from(corner_up, 1, 1)
-    corner_down = tiles_from(corner_down, 1, -1)
     tiles = [(OWN, mine.reshape(4, *shape)), (OWN, theirs.reshape(4, *shape)), (ABOVE, above_mine), (ABOVE, above_theirs)]
-    one, token = blocks(FIRST, tiles, token, "first_blocks")
+    tiles += [(BESIDE, beside[0]), (BESIDE, beside[1])]
+    (one,), token = blocks((FIRST,), tiles, token, "first_blocks")
     one_first = first(one)
     early_back, token = back(early, early_first, early_second, token)
-    early_kept, token = keep(early, early_first, early_second, token)
-    tiles += [(BESIDE, beside[0]), (BESIDE, beside[1]), (CORNER_UP, corner_up[:1]), (CORNER_UP, corner_up[1:])]
-    tiles += [(CORNER_DOWN, corner_down[:1]), (CORNER_DOWN, corner_down[1:])]
-    two, token = blocks(LAST, tiles, token, "last_blocks")
+    tiles += [(CORNER, corner[:1]), (CORNER, corner[1:])]
+    (two,), token = blocks((LAST,), tiles, token, "last_blocks")
     two_first = first(two)
     one_second, token = second(one, one_first, token, [early_back])
     two_second, token = second(two, two_first, token)
     one_back, token = back(one, one_first, one_second, token)
+    two_back, token = back(two, two_first, two_second, token)
     one_kept, token = keep(one, one_first, one_second, token)
-    rows = jax.ShapeDtypeStruct((2,) + one_kept.shape[1:], jnp.float32)
+    rows = jax.ShapeDtypeStruct((2 * GIVEN,) + one_back.shape[1:], one_back.dtype)
     (given,), token = call_step(give_kernel, [rows], token, [one_kept, one_back], "give")
     given = tiles_from(given, 0, -1)
-    two_back, token = back(two, two_first, two_second, token)
+    early_kept, token = keep(early, early_first, early_second, token)
     two_kept, token = keep(two, two_first, two_second, token)
     parts = [(early_kept, early_back), (one_kept, one_back), (two_kept, two_back)]
     shape = green.shape[:2] + (NPAIR, green.shape[2], points // (2 * RING), 2 * points)

time: 115 us -> 107 us (0.930)
  the two profiles are of different devices: /device:TPU:96 before, /device:TPU:100 now
where the time goes in v5:
time: 107 us
  waiting for transfers between devices  46.2 us (43%)
  starting transfers between devices  36.3 us (34%)
  Pallas kernels  19.4 us (18%)
  local copies, waits for them, and re-layouts  4.58 us (4%)
    ppermute x12, starting transfers between devices, around(): lax.ppermute(value, 'sa', [(h * RING + i, h * RING + (i + steps) % RING)...  19.1 us
    ppermute x12, waiting for transfers between devices, around(): lax.ppermute(value, 'sa', [(h * RING + i, h * RING + (i + steps) % RING)...  16.2 us
    ppermute x5, waiting for transfers between devices, tiles_from(): return lax.ppermute(value, ('gx', 'gy'), perm)  15.7 us
    ppermute x4, waiting for transfers between devices, swap(): lax.ppermute(value, 'sa', [(i, (i + RING) % (2 * RING)) for i in range(2...  14.3 us
    ppermute x5, starting transfers between devices, tiles_from(): return lax.ppermute(value, ('gx', 'gy'), perm)  11.9 us
    pallas_call x3, Pallas kernels, call_blocks(): pl.pallas_call(kernel, out_shape=out_shape + [jax.ShapeDtypeStruct(token....  10.5 us
    pallas_call x11, Pallas kernels, call_step(): pl.pallas_call(kernel, out_shape=list(out_shape) + [jax.ShapeDtypeStruct(...  6.37 us
    ppermute x4, starting transfers between devices, swap(): lax.ppermute(value, 'sa', [(i, (i + RING) % (2 * RING)) for i in range(2...  5.26 us
  transfers between devices with their start and end apart: 21, of which 15 were waited for; matrix products, arithmetic and copies ran while one was open for 0% of the time, Pallas kernels for 16%

profile of v5, /device:TPU:100, one launch (start us, length us, event | category | flops | bytes accessed | tf_op | source)
XLA Modules:
  0.0 106.7 jit_solution(178475502401842154)
XLA Ops:
  0.0 2.7 %dynamic-slice_bitcast_fusion = (bf16[2,2,2,256,256]{4,3,2,1,0:T(8,128)(2,1)}, bf16[2,2,1,2,256,256]{5,4,3,2,1,0:T(8,128)(2,1)S(1)}) fusion(bf16[2,2,2,2,256,256]{5,4,3,2,1,0:T(8,128)(2,1)} %green.1, s32[]{:T(128)S(6)} %select_n.21, s32[]{:T(128)S(6)} %select_n.20), kind=kLoop, calls=%fused_computation.1 | loop fusion | bytes 4194312 | tf_op jit(solution)/shard_map/jit(dynamic_index_in_dim)/squeeze | solution.py:320
  2.7 1.2 %collective-permute-start = (bf16[2,2,2,256,256]{4,3,2,1,0:T(8,128)(2,1)}, bf16[2,2,2,256,256]{4,3,2,1,0:T(8,128)(2,1)S(1)}, u32[]{:S(2)}, u32[]{:S(2)}) collective-permute-start(bf16[2,2,2,256,256]{4,3,2,1,0:T(8,128)(2,1)} %get-tuple-element.101), channel_id=1, source_target_pairs={{0,4},{1,5},{2,6},{3,7},{4,0},{5,1},{6,2},{7,3},{8,12},{9,13},{10,... | collective-permute-start | bytes 3145736 | tf_op jit(solution)/shard_map/ppermute | solution.py:280
  3.9 0.1 copy.11
  4.0 2.0 %collective-permute-start.1 = (bf16[2,2,256,256]{3,2,1,0:T(8,128)(2,1)S(1)}, bf16[2,2,256,256]{3,2,1,0:T(8,128)(2,1)S(1)}, u32[]{:S(2)}, u32[]{:S(2)}) collective-permute-start(bf16[2,2,256,256]{3,2,1,0:T(8,128)(2,1)S(1)} %slice_bitcast_fusion.2), channel_id=1, source_target_pairs={{8,0},{16,8},{24,16},{32,24},{40,32},{48,40},{56,48},{72,64},{80,7... | collective-permute-start | bytes 1572872 | tf_op jit(solution)/shard_map/ppermute | solution.py:291
  6.0 0.0 copy-done.1
  6.0 0.1 copy.8.offsets.refs_1_
  6.1 0.1 pad_add_fusion.meta.refs_0_
  6.2 1.6 %copy-done = bf16[2,2,2,2,256,256]{5,4,3,2,1,0:T(8,128)(2,1)S(1)} copy-done((bf16[2,2,2,2,256,256]{5,4,3,2,1,0:T(8,128)(2,1)S(1)}, bf16[2,2,2,2,256,256]{5,4,3,2,1,0:T(8,128)(2,1)}, u32[]{:S(2)}) %copy-start) | copy-done | bytes 2097176
  7.8 3.4 %early_blocks.1 = (f32[10,32,512]{2,1,0:T(8,128)S(1)}, f32[10,32,512]{2,1,0:T(8,128)S(1)}, bf16[20,32,768]{2,1,0:T(8,128)(2,1)S(1)}, bf16[20,32,768]{2,1,0:T(8,1...) custom-call(s32[2]{0:T(128)S(1)} %pad_add_fusion.meta.refs_0_, ...), custom_call_target="tpu_custom_call" | custom-call | tf_op jit(solution)/shard_map/early_blocks/pallas_call | solution.py:165
  11.2 1.7 %collective-permute-start.2 = (bf16[20,32,768]{2,1,0:T(8,128)(2,1)S(1)}, bf16[20,32,768]{2,1,0:T(8,128)(2,1)S(1)}, u32[]{:S(2)}, u32[]{:S(2)}) collective-permute-start(bf16[20,32,768]{2,1,0:T(8,128)(2,1)S(1)} %get-tuple-element.55), channel_id=1, source_target_pairs={{0,1},{1,2},{2,3},{3,0},{4,5},{5,6},{6,7},{7,4},{8,9},{9,10},{10,1... | collective-permute-start | bytes 2949128 | tf_op jit(solution)/shard_map/ppermute | solution.py:283
  12.8 1.7 %collective-permute-start.3 = (bf16[20,32,768]{2,1,0:T(8,128)(2,1)S(1)}, bf16[20,32,768]{2,1,0:T(8,128)(2,1)S(1)}, u32[]{:S(2)}, u32[]{:S(2)}) collective-permute-start(bf16[20,32,768]{2,1,0:T(8,128)(2,1)S(1)} %get-tuple-element.56), channel_id=1, source_target_pairs={{0,3},{1,0},{2,1},{3,2},{4,7},{5,4},{6,5},{7,6},{8,11},{9,8},{10,9... | collective-permute-start | bytes 2949128 | tf_op jit(solution)/shard_map/ppermute | solution.py:283
  14.5 6.2 %collective-permute-done.1.above_mine.refs_5_ = bf16[2,2,256,256]{3,2,1,0:T(8,128)(2,1)S(1)} collective-permute-done((bf16[2,2,256,256]{3,2,1,0:T(8,128)(2,1)S(1)}, bf16[2,2,256,256]{3,2,1,0:T(8,128)(2,1)S(1)}, u32[]{:S(2)}, u32[]{:S(2)}) %collective-permute-start.1) | collective-permute-done | bytes 524320 | tf_op jit(solution)/shard_map/ppermute | solution.py:291
  20.7 7.1 %collective-permute-done.theirs = bf16[2,2,2,256,256]{4,3,2,1,0:T(8,128)(2,1)S(1)} collective-permute-done((bf16[2,2,2,256,256]{4,3,2,1,0:T(8,128)(2,1)}, bf16[2,2,2,256,256]{4,3,2,1,0:T(8,128)(2,1)S(1)}, u32[]{:S(2)}, u32[]{:S(2)}) %collective-permute-start) | collective-permute-done | bytes 1048608 | tf_op jit(solution)/shard_map/ppermute | solution.py:280
  27.8 0.1 swapped.1
  27.9 1.9 %collective-permute-start.5 = (bf16[2,2,2,256,256]{4,3,2,1,0:T(8,128)(2,1)S(1)}, bf16[2,2,2,256,256]{4,3,2,1,0:T(8,128)(2,1)S(1)}, u32[]{:S(2)}, u32[]{:S(2)}) collective-permute-start(bf16[2,2,2,256,256]{4,3,2,1,0:T(8,128)(2,1)S(1)} %get-tuple-element.61), channel_id=1, source_target_pairs={{64,0},{72,8},{80,16},{88,24},{96,32},{104,40},{112,48},{120,56},{... | collective-permute-start | bytes 3145736 | tf_op jit(solution)/shard_map/ppermute | solution.py:291
  29.9 2.0 %collective-permute-start.4 = (bf16[2,2,256,256]{3,2,1,0:T(8,128)(2,1)S(1)}, bf16[2,2,256,256]{3,2,1,0:T(8,128)(2,1)S(1)}, u32[]{:S(2)}, u32[]{:S(2)}) collective-permute-start(bf16[2,2,256,256]{3,2,1,0:T(8,128)(2,1)S(1)} %get-tuple-element.60), channel_id=1, source_target_pairs={{8,0},{16,8},{24,16},{32,24},{40,32},{48,40},{56,48},{72,64},{80,7... | collective-permute-start | bytes 1572872 | tf_op jit(solution)/shard_map/ppermute | solution.py:291
  31.9 3.8 %collective-permute-done.2.up_received = bf16[20,32,768]{2,1,0:T(8,128)(2,1)S(1)} collective-permute-done((bf16[20,32,768]{2,1,0:T(8,128)(2,1)S(1)}, bf16[20,32,768]{2,1,0:T(8,128)(2,1)S(1)}, u32[]{:S(2)}, u32[]{:S(2)}) %collective-permute-start.2) | collective-permute-done | bytes 983072 | tf_op jit(solution)/shard_map/ppermute | solution.py:283
  35.6 0.0 collective-permute-done.3.down_received.after
  35.7 1.3 %second.3 = (bf16[10,32,768]{2,1,0:T(8,128)(2,1)S(1)}, bf16[10,32,768]{2,1,0:T(8,128)(2,1)S(1)}, f32[8,128]{1,0:T(8,128)S(1)}) custom-call(f32[8,128]{1,0:T(8,128)S(1)} %get-tuple-element.54.token, bf16[20,32,768]{2,1,0:T(8,128)(2,1)S(1)} %collective-permute-done.2.up_received, bf16[20,32,768]{2,1,0:T(8,128)(2,1)S(1)} %collective-permute-done.3.down_received.after, ...), custom_call_target="tpu_custom_call" | custom-call | tf_op jit(solution)/shard_map/second/pallas_call | solution.py:184
  37.0 3.1 %collective-permute-start.6 = (bf16[10,32,768]{2,1,0:T(8,128)(2,1)S(1)}, bf16[10,32,768]{2,1,0:T(8,128)(2,1)S(1)}, u32[]{:S(2)}, u32[]{:S(2)}) collective-permute-start(bf16[10,32,768]{2,1,0:T(8,128)(2,1)S(1)} %get-tuple-element.63), channel_id=1, source_target_pairs={{0,3},{1,0},{2,1},{3,2},{4,7},{5,4},{6,5},{7,6},{8,11},{9,8},{10,9... | collective-permute-start | bytes 1474568 | tf_op jit(solution)/shard_map/ppermute | solution.py:283
  40.1 0.0 collective-permute-start.7
  40.1 1.9 %collective-permute-start.8 = (bf16[2,2,256,256]{3,2,1,0:T(8,128)(2,1)S(1)}, bf16[2,2,256,256]{3,2,1,0:T(8,128)(2,1)S(1)}, u32[]{:S(2)}, u32[]{:S(2)}) collective-permute-start(bf16[2,2,256,256]{3,2,1,0:T(8,128)(2,1)S(1)} %get-tuple-element.67), channel_id=1, source_target_pairs={{72,0},{80,8},{88,16},{96,24},{104,32},{112,40},{120,48},{136,64},... | collective-permute-start | bytes 1572872 | tf_op jit(solution)/shard_map/ppermute | solution.py:291
  42.0 0.1 collective-permute-done.5
  42.2 0.1 slice_bitcast_fusion
  42.2 5.5 %collective-permute-done.4.refs_6_ = bf16[2,2,256,256]{3,2,1,0:T(8,128)(2,1)S(1)} collective-permute-done((bf16[2,2,256,256]{3,2,1,0:T(8,128)(2,1)S(1)}, bf16[2,2,256,256]{3,2,1,0:T(8,128)(2,1)S(1)}, u32[]{:S(2)}, u32[]{:S(2)}) %collective-permute-start.4) | collective-permute-done | bytes 524320 | tf_op jit(solution)/shard_map/ppermute | solution.py:291
  47.8 3.8 %first_blocks.1 = (f32[6,32,512]{2,1,0:T(8,128)S(1)}, f32[6,32,512]{2,1,0:T(8,128)S(1)}, bf16[12,32,768]{2,1,0:T(8,128)(2,1)S(1)}, bf16[12,32,768]{2,1,0:T(8,128...) custom-call(s32[2]{0:T(128)S(1)} %pad_add_fusion.meta.refs_0_, ...), custom_call_target="tpu_custom_call" | custom-call | tf_op jit(solution)/shard_map/first_blocks/pallas_call | solution.py:165
  51.6 1.8 %collective-permute-start.9 = (bf16[12,32,768]{2,1,0:T(8,128)(2,1)S(1)}, bf16[12,32,768]{2,1,0:T(8,128)(2,1)S(1)}, u32[]{:S(2)}, u32[]{:S(2)}) collective-permute-start(bf16[12,32,768]{2,1,0:T(8,128)(2,1)S(1)} %get-tuple-element.69), channel_id=1, source_target_pairs={{0,1},{1,2},{2,3},{3,0},{4,5},{5,6},{6,7},{7,4},{8,9},{9,10},{10,1... | collective-permute-start | bytes 1769480 | tf_op jit(solution)/shard_map/ppermute | solution.py:283
  53.4 1.7 %collective-permute-start.10 = (bf16[12,32,768]{2,1,0:T(8,128)(2,1)S(1)}, bf16[12,32,768]{2,1,0:T(8,128)(2,1)S(1)}, u32[]{:S(2)}, u32[]{:S(2)}) collective-permute-start(bf16[12,32,768]{2,1,0:T(8,128)(2,1)S(1)} %get-tuple-element.70), channel_id=1, source_target_pairs={{0,3},{1,0},{2,1},{3,2},{4,7},{5,4},{6,5},{7,6},{8,11},{9,8},{10,9... | collective-permute-start | bytes 1769480 | tf_op jit(solution)/shard_map/ppermute | solution.py:283
  55.0 0.0 collective-permute-done.6.down_arrived
  55.1 0.0 collective-permute-done.7.refs_0_.before
  55.1 1.0 back.3
  56.0 1.3 %collective-permute-start.11 = (bf16[10,32,768]{2,1,0:T(8,128)(2,1)S(1)}, bf16[10,32,768]{2,1,0:T(8,128)(2,1)S(1)}, u32[]{:S(2)}, u32[]{:S(2)}) collective-permute-start(bf16[10,32,768]{2,1,0:T(8,128)(2,1)S(1)} %get-tuple-element.73), channel_id=1, source_target_pairs={{0,4},{1,5},{2,6},{3,7},{4,0},{5,1},{6,2},{7,3},{8,12},{9,13},{10,... | collective-permute-start | bytes 1474568 | tf_op jit(solution)/shard_map/ppermute | solution.py:280
  57.3 1.2 %collective-permute-done.8 = bf16[2,2,256,256]{3,2,1,0:T(8,128)(2,1)S(1)} collective-permute-done((bf16[2,2,256,256]{3,2,1,0:T(8,128)(2,1)S(1)}, bf16[2,2,256,256]{3,2,1,0:T(8,128)(2,1)S(1)}, u32[]{:S(2)}, u32[]{:S(2)}) %collective-permute-start.8) | collective-permute-done | bytes 524320 | tf_op jit(solution)/shard_map/ppermute | solution.py:291
  58.6 3.3 %last_blocks.1 = (f32[5,32,512]{2,1,0:T(8,128)S(1)}, f32[5,32,512]{2,1,0:T(8,128)S(1)}, bf16[10,32,768]{2,1,0:T(8,128)(2,1)S(1)}, bf16[10,32,768]{2,1,0:T(8,128)...) custom-call(s32[2]{0:T(128)S(1)} %pad_add_fusion.meta.refs_0_, ...), custom_call_target="tpu_custom_call" | custom-call | tf_op jit(solution)/shard_map/last_blocks/pallas_call | solution.py:165
  61.9 1.7 %collective-permute-start.12 = (bf16[10,32,768]{2,1,0:T(8,128)(2,1)S(1)}, bf16[10,32,768]{2,1,0:T(8,128)(2,1)S(1)}, u32[]{:S(2)}, u32[]{:S(2)}) collective-permute-start(bf16[10,32,768]{2,1,0:T(8,128)(2,1)S(1)} %get-tuple-element.75), channel_id=1, source_target_pairs={{0,1},{1,2},{2,3},{3,0},{4,5},{5,6},{6,7},{7,4},{8,9},{9,10},{10,1... | collective-permute-start | bytes 1474568 | tf_op jit(solution)/shard_map/ppermute | solution.py:283
  63.6 1.7 %collective-permute-start.13 = (bf16[10,32,768]{2,1,0:T(8,128)(2,1)S(1)}, bf16[10,32,768]{2,1,0:T(8,128)(2,1)S(1)}, u32[]{:S(2)}, u32[]{:S(2)}) collective-permute-start(bf16[10,32,768]{2,1,0:T(8,128)(2,1)S(1)} %get-tuple-element.76), channel_id=1, source_target_pairs={{0,3},{1,0},{2,1},{3,2},{4,7},{5,4},{6,5},{7,6},{8,11},{9,8},{10,9... | collective-permute-start | bytes 1474568 | tf_op jit(solution)/shard_map/ppermute | solution.py:283
  65.2 4.1 %collective-permute-done.11.refs_0_.refs_1_ = bf16[10,32,768]{2,1,0:T(8,128)(2,1)S(1)} collective-permute-done((bf16[10,32,768]{2,1,0:T(8,128)(2,1)S(1)}, bf16[10,32,768]{2,1,0:T(8,128)(2,1)S(1)}, u32[]{:S(2)}, u32[]{:S(2)}) %collective-permute-start.11) | collective-permute-done | bytes 491552 | tf_op jit(solution)/shard_map/ppermute | solution.py:280
  69.3 0.0 collective-permute-done.9.up_received
  69.3 0.3 collective-permute-done.10.down_received.after
  69.6 0.8 second.4
  70.4 3.0 %collective-permute-start.14 = (bf16[6,32,768]{2,1,0:T(8,128)(2,1)S(1)}, bf16[6,32,768]{2,1,0:T(8,128)(2,1)S(1)}, u32[]{:S(2)}, u32[]{:S(2)}) collective-permute-start(bf16[6,32,768]{2,1,0:T(8,128)(2,1)S(1)} %get-tuple-element.80), channel_id=1, source_target_pairs={{0,3},{1,0},{2,1},{3,2},{4,7},{5,4},{6,5},{7,6},{8,11},{9,8},{10,9... | collective-permute-start | bytes 884744 | tf_op jit(solution)/shard_map/ppermute | solution.py:283
  73.4 0.0 collective-permute-start.15
  73.4 6.4 %collective-permute-done.12.up_received = bf16[10,32,768]{2,1,0:T(8,128)(2,1)S(1)} collective-permute-done((bf16[10,32,768]{2,1,0:T(8,128)(2,1)S(1)}, bf16[10,32,768]{2,1,0:T(8,128)(2,1)S(1)}, u32[]{:S(2)}, u32[]{:S(2)}) %collective-permute-start.12) | collective-permute-done | bytes 491552 | tf_op jit(solution)/shard_map/ppermute | solution.py:283
  79.8 0.4 collective-permute-done.13.down_received.after
  80.2 0.7 second.5
  80.8 3.0 %collective-permute-start.16 = (bf16[5,32,768]{2,1,0:T(8,128)(2,1)S(1)}, bf16[5,32,768]{2,1,0:T(8,128)(2,1)S(1)}, u32[]{:S(2)}, u32[]{:S(2)}) collective-permute-start(bf16[5,32,768]{2,1,0:T(8,128)(2,1)S(1)} %get-tuple-element.84), channel_id=1, source_target_pairs={{0,3},{1,0},{2,1},{3,2},{4,7},{5,4},{6,5},{7,6},{8,11},{9,8},{10,9... | collective-permute-start | bytes 737288 | tf_op jit(solution)/shard_map/ppermute | solution.py:283
  83.8 0.0 collective-permute-start.17
  83.8 2.7 %collective-permute-done.14.down_arrived = bf16[6,32,768]{2,1,0:T(8,128)(2,1)S(1)} collective-permute-done((bf16[6,32,768]{2,1,0:T(8,128)(2,1)S(1)}, bf16[6,32,768]{2,1,0:T(8,128)(2,1)S(1)}, u32[]{:S(2)}, u32[]{:S(2)}) %collective-permute-start.14) | collective-permute-done | bytes 294944 | tf_op jit(solution)/shard_map/ppermute | solution.py:283
  86.5 0.0 collective-permute-done.15.refs_0_.before
  86.5 0.6 back.4
  87.1 1.5 %collective-permute-start.18 = (bf16[6,32,768]{2,1,0:T(8,128)(2,1)S(1)}, bf16[6,32,768]{2,1,0:T(8,128)(2,1)S(1)}, u32[]{:S(2)}, u32[]{:S(2)}) collective-permute-start(bf16[6,32,768]{2,1,0:T(8,128)(2,1)S(1)} %get-tuple-element.91), channel_id=1, source_target_pairs={{0,4},{1,5},{2,6},{3,7},{4,0},{5,1},{6,2},{7,3},{8,12},{9,13},{10,... | collective-permute-start | bytes 884744 | tf_op jit(solution)/shard_map/ppermute | solution.py:280
  88.6 1.5 %collective-permute-done.16.down_arrived = bf16[5,32,768]{2,1,0:T(8,128)(2,1)S(1)} collective-permute-done((bf16[5,32,768]{2,1,0:T(8,128)(2,1)S(1)}, bf16[5,32,768]{2,1,0:T(8,128)(2,1)S(1)}, u32[]{:S(2)}, u32[]{:S(2)}) %collective-permute-start.16) | collective-permute-done | bytes 245792 | tf_op jit(solution)/shard_map/ppermute | solution.py:283
  90.1 1.1 %collective-permute-done.17.refs_0_.before = bf16[5,32,768]{2,1,0:T(8,128)(2,1)S(1)} collective-permute-done((bf16[5,32,768]{2,1,0:T(8,128)(2,1)S(1)}, bf16[5,32,768]{2,1,0:T(8,128)(2,1)S(1)}, u32[]{:S(2)}, u32[]{:S(2)}) %collective-permute-start.17) | collective-permute-done | bytes 245792 | tf_op jit(solution)/shard_map/ppermute | solution.py:283
  91.2 0.5 back.5
  91.7 1.3 %collective-permute-start.19 = (bf16[5,32,768]{2,1,0:T(8,128)(2,1)S(1)}, bf16[5,32,768]{2,1,0:T(8,128)(2,1)S(1)}, u32[]{:S(2)}, u32[]{:S(2)}) collective-permute-start(bf16[5,32,768]{2,1,0:T(8,128)(2,1)S(1)} %get-tuple-element.98), channel_id=1, source_target_pairs={{0,4},{1,5},{2,6},{3,7},{4,0},{5,1},{6,2},{7,3},{8,12},{9,13},{10,... | collective-permute-start | bytes 737288 | tf_op jit(solution)/shard_map/ppermute | solution.py:280
  93.0 0.4 keep.3
  93.4 3.1 %collective-permute-done.18.other.refs_3_ = bf16[6,32,768]{2,1,0:T(8,128)(2,1)S(1)} collective-permute-done((bf16[6,32,768]{2,1,0:T(8,128)(2,1)S(1)}, bf16[6,32,768]{2,1,0:T(8,128)(2,1)S(1)}, u32[]{:S(2)}, u32[]{:S(2)}) %collective-permute-start.18) | collective-permute-done | bytes 294944 | tf_op jit(solution)/shard_map/ppermute | solution.py:280
  96.5 0.1 give.1
  96.6 4.0 %collective-permute-start.20 = (bf16[4,32,768]{2,1,0:T(8,128)(2,1)S(1)}, bf16[4,32,768]{2,1,0:T(8,128)(2,1)S(1)}, u32[]{:S(2)}, u32[]{:S(2)}) collective-permute-start(bf16[4,32,768]{2,1,0:T(8,128)(2,1)S(1)} %get-tuple-element.99), channel_id=1, source_target_pairs={{0,8},{8,16},{16,24},{24,32},{32,40},{40,48},{48,56},{64,72},{72,8... | collective-permute-start | bytes 589832 | tf_op jit(solution)/shard_map/ppermute | solution.py:291
  100.6 0.6 keep.4
  101.2 0.3 keep.5
  101.5 0.0 collective-permute-done.19.refs_5_
  101.5 2.6 %collective-permute-done.20.refs_6_ = bf16[4,32,768]{2,1,0:T(8,128)(2,1)S(1)} collective-permute-done((bf16[4,32,768]{2,1,0:T(8,128)(2,1)S(1)}, bf16[4,32,768]{2,1,0:T(8,128)(2,1)S(1)}, u32[]{:S(2)}, u32[]{:S(2)}) %collective-permute-start.20) | collective-permute-done | bytes 196640 | tf_op jit(solution)/shard_map/ppermute | solution.py:291
  104.1 2.6 %place_blocks.1 = f32[2,2,4,2,32,512]{5,4,3,2,1,0:T(8,128)} custom-call(s32[2]{0:T(128)S(1)} %pad_add_fusion.meta.refs_0_, s32[4,2]{1,0:T(4,128)S(1)} %copy.8.offsets.refs_1_, f32[10,32,512]{2,1,0:T(8,128)S(1)} %get-tuple-element.94.refs_0_, bf16[10,32,768]{2,1,0:T(8,128)(2,1)S(1)} %collective-permute-done.11.refs_0_.refs_1_, ...), custom_call_target="tpu_custom_call" | custom-call | tf_op jit(solution)/shard_map/place_blocks/pallas_call | solution.py:261
  (5 shorter events, 0.1 us)
Async XLA Ops:
  2.7 3.4 %copy-start.1 = (s32[4,2]{0,1:T(2,128)S(1)}, s32[4,2]{0,1:T(2,128)}, u32[]{:S(2)}) copy-start(s32[4,2]{0,1:T(2,128)} %param.3) | copy-start | bytes 100
  2.7 25.1 %collective-permute-start = (bf16[2,2,2,256,256]{4,3,2,1,0:T(8,128)(2,1)}, bf16[2,2,2,256,256]{4,3,2,1,0:T(8,128)(2,1)S(1)}, u32[]{:S(2)}, u32[]{:S(2)}) collective-permute-start(bf16[2,2,2,256,256]{4,3,2,1,0:T(8,128)(2,1)} %get-tuple-element.101), channel_id=1, source_target_pairs={{0,4},{1,5},{2,6},{3,7},{4,0},{5,1},{6,2},{7,3},{8,12},{9,13},{10,... | collective-permute-start | bytes 3145736 | tf_op jit(solution)/shard_map/ppermute | solution.py:280
  4.0 16.7 %collective-permute-start.1 = (bf16[2,2,256,256]{3,2,1,0:T(8,128)(2,1)S(1)}, bf16[2,2,256,256]{3,2,1,0:T(8,128)(2,1)S(1)}, u32[]{:S(2)}, u32[]{:S(2)}) collective-permute-start(bf16[2,2,256,256]{3,2,1,0:T(8,128)(2,1)S(1)} %slice_bitcast_fusion.2), channel_id=1, source_target_pairs={{8,0},{16,8},{24,16},{32,24},{40,32},{48,40},{56,48},{72,64},{80,7... | collective-permute-start | bytes 1572872 | tf_op jit(solution)/shard_map/ppermute | solution.py:291
  6.2 1.6 %copy-start = (bf16[2,2,2,2,256,256]{5,4,3,2,1,0:T(8,128)(2,1)S(1)}, bf16[2,2,2,2,256,256]{5,4,3,2,1,0:T(8,128)(2,1)}, u32[]{:S(2)}) copy-start(bf16[2,2,2,2,256,256]{5,4,3,2,1,0:T(8,128)(2,1)} %green.1) | copy-start | bytes 6291460
  11.2 24.5 %collective-permute-start.2 = (bf16[20,32,768]{2,1,0:T(8,128)(2,1)S(1)}, bf16[20,32,768]{2,1,0:T(8,128)(2,1)S(1)}, u32[]{:S(2)}, u32[]{:S(2)}) collective-permute-start(bf16[20,32,768]{2,1,0:T(8,128)(2,1)S(1)} %get-tuple-element.55), channel_id=1, source_target_pairs={{0,1},{1,2},{2,3},{3,0},{4,5},{5,6},{6,7},{7,4},{8,9},{9,10},{10,1... | collective-permute-start | bytes 2949128 | tf_op jit(solution)/shard_map/ppermute | solution.py:283
  12.8 22.8 %collective-permute-start.3 = (bf16[20,32,768]{2,1,0:T(8,128)(2,1)S(1)}, bf16[20,32,768]{2,1,0:T(8,128)(2,1)S(1)}, u32[]{:S(2)}, u32[]{:S(2)}) collective-permute-start(bf16[20,32,768]{2,1,0:T(8,128)(2,1)S(1)} %get-tuple-element.56), channel_id=1, source_target_pairs={{0,3},{1,0},{2,1},{3,2},{4,7},{5,4},{6,5},{7,6},{8,11},{9,8},{10,9... | collective-permute-start | bytes 2949128 | tf_op jit(solution)/shard_map/ppermute | solution.py:283
  27.9 14.2 %collective-permute-start.5 = (bf16[2,2,2,256,256]{4,3,2,1,0:T(8,128)(2,1)S(1)}, bf16[2,2,2,256,256]{4,3,2,1,0:T(8,128)(2,1)S(1)}, u32[]{:S(2)}, u32[]{:S(2)}) collective-permute-start(bf16[2,2,2,256,256]{4,3,2,1,0:T(8,128)(2,1)S(1)} %get-tuple-element.61), channel_id=1, source_target_pairs={{64,0},{72,8},{80,16},{88,24},{96,32},{104,40},{112,48},{120,56},{... | collective-permute-start | bytes 3145736 | tf_op jit(solution)/shard_map/ppermute | solution.py:291
  29.9 17.9 %collective-permute-start.4 = (bf16[2,2,256,256]{3,2,1,0:T(8,128)(2,1)S(1)}, bf16[2,2,256,256]{3,2,1,0:T(8,128)(2,1)S(1)}, u32[]{:S(2)}, u32[]{:S(2)}) collective-permute-start(bf16[2,2,256,256]{3,2,1,0:T(8,128)(2,1)S(1)} %get-tuple-element.60), channel_id=1, source_target_pairs={{8,0},{16,8},{24,16},{32,24},{40,32},{48,40},{56,48},{72,64},{80,7... | collective-permute-start | bytes 1572872 | tf_op jit(solution)/shard_map/ppermute | solution.py:291
  37.0 18.1 %collective-permute-start.6 = (bf16[10,32,768]{2,1,0:T(8,128)(2,1)S(1)}, bf16[10,32,768]{2,1,0:T(8,128)(2,1)S(1)}, u32[]{:S(2)}, u32[]{:S(2)}) collective-permute-start(bf16[10,32,768]{2,1,0:T(8,128)(2,1)S(1)} %get-tuple-element.63), channel_id=1, source_target_pairs={{0,3},{1,0},{2,1},{3,2},{4,7},{5,4},{6,5},{7,6},{8,11},{9,8},{10,9... | collective-permute-start | bytes 1474568 | tf_op jit(solution)/shard_map/ppermute | solution.py:283
  40.1 15.0 %collective-permute-start.7 = (bf16[10,32,768]{2,1,0:T(8,128)(2,1)S(1)}, bf16[10,32,768]{2,1,0:T(8,128)(2,1)S(1)}, u32[]{:S(2)}, u32[]{:S(2)}) collective-permute-start(bf16[10,32,768]{2,1,0:T(8,128)(2,1)S(1)} %get-tuple-element.65), channel_id=1, source_target_pairs={{0,1},{1,2},{2,3},{3,0},{4,5},{5,6},{6,7},{7,4},{8,9},{9,10},{10,1... | collective-permute-start | bytes 1474568 | tf_op jit(solution)/shard_map/ppermute | solution.py:283
  40.1 18.4 %collective-permute-start.8 = (bf16[2,2,256,256]{3,2,1,0:T(8,128)(2,1)S(1)}, bf16[2,2,256,256]{3,2,1,0:T(8,128)(2,1)S(1)}, u32[]{:S(2)}, u32[]{:S(2)}) collective-permute-start(bf16[2,2,256,256]{3,2,1,0:T(8,128)(2,1)S(1)} %get-tuple-element.67), channel_id=1, source_target_pairs={{72,0},{80,8},{88,16},{96,24},{104,32},{112,40},{120,48},{136,64},... | collective-permute-start | bytes 1572872 | tf_op jit(solution)/shard_map/ppermute | solution.py:291
  51.6 17.8 %collective-permute-start.9 = (bf16[12,32,768]{2,1,0:T(8,128)(2,1)S(1)}, bf16[12,32,768]{2,1,0:T(8,128)(2,1)S(1)}, u32[]{:S(2)}, u32[]{:S(2)}) collective-permute-start(bf16[12,32,768]{2,1,0:T(8,128)(2,1)S(1)} %get-tuple-element.69), channel_id=1, source_target_pairs={{0,1},{1,2},{2,3},{3,0},{4,5},{5,6},{6,7},{7,4},{8,9},{9,10},{10,1... | collective-permute-start | bytes 1769480 | tf_op jit(solution)/shard_map/ppermute | solution.py:283
  53.4 16.3 %collective-permute-start.10 = (bf16[12,32,768]{2,1,0:T(8,128)(2,1)S(1)}, bf16[12,32,768]{2,1,0:T(8,128)(2,1)S(1)}, u32[]{:S(2)}, u32[]{:S(2)}) collective-permute-start(bf16[12,32,768]{2,1,0:T(8,128)(2,1)S(1)} %get-tuple-element.70), channel_id=1, source_target_pairs={{0,3},{1,0},{2,1},{3,2},{4,7},{5,4},{6,5},{7,6},{8,11},{9,8},{10,9... | collective-permute-start | bytes 1769480 | tf_op jit(solution)/shard_map/ppermute | solution.py:283
  56.0 13.3 %collective-permute-start.11 = (bf16[10,32,768]{2,1,0:T(8,128)(2,1)S(1)}, bf16[10,32,768]{2,1,0:T(8,128)(2,1)S(1)}, u32[]{:S(2)}, u32[]{:S(2)}) collective-permute-start(bf16[10,32,768]{2,1,0:T(8,128)(2,1)S(1)} %get-tuple-element.73), channel_id=1, source_target_pairs={{0,4},{1,5},{2,6},{3,7},{4,0},{5,1},{6,2},{7,3},{8,12},{9,13},{10,... | collective-permute-start | bytes 1474568 | tf_op jit(solution)/shard_map/ppermute | solution.py:280
  61.9 17.9 %collective-permute-start.12 = (bf16[10,32,768]{2,1,0:T(8,128)(2,1)S(1)}, bf16[10,32,768]{2,1,0:T(8,128)(2,1)S(1)}, u32[]{:S(2)}, u32[]{:S(2)}) collective-permute-start(bf16[10,32,768]{2,1,0:T(8,128)(2,1)S(1)} %get-tuple-element.75), channel_id=1, source_target_pairs={{0,1},{1,2},{2,3},{3,0},{4,5},{5,6},{6,7},{7,4},{8,9},{9,10},{10,1... | collective-permute-start | bytes 1474568 | tf_op jit(solution)/shard_map/ppermute | solution.py:283
  63.6 16.6 %collective-permute-start.13 = (bf16[10,32,768]{2,1,0:T(8,128)(2,1)S(1)}, bf16[10,32,768]{2,1,0:T(8,128)(2,1)S(1)}, u32[]{:S(2)}, u32[]{:S(2)}) collective-permute-start(bf16[10,32,768]{2,1,0:T(8,128)(2,1)S(1)} %get-tuple-element.76), channel_id=1, source_target_pairs={{0,3},{1,0},{2,1},{3,2},{4,7},{5,4},{6,5},{7,6},{8,11},{9,8},{10,9... | collective-permute-start | bytes 1474568 | tf_op jit(solution)/shard_map/ppermute | solution.py:283
  70.4 16.0 %collective-permute-start.14 = (bf16[6,32,768]{2,1,0:T(8,128)(2,1)S(1)}, bf16[6,32,768]{2,1,0:T(8,128)(2,1)S(1)}, u32[]{:S(2)}, u32[]{:S(2)}) collective-permute-start(bf16[6,32,768]{2,1,0:T(8,128)(2,1)S(1)} %get-tuple-element.80), channel_id=1, source_target_pairs={{0,3},{1,0},{2,1},{3,2},{4,7},{5,4},{6,5},{7,6},{8,11},{9,8},{10,9... | collective-permute-start | bytes 884744 | tf_op jit(solution)/shard_map/ppermute | solution.py:283
  73.4 13.1 %collective-permute-start.15 = (bf16[6,32,768]{2,1,0:T(8,128)(2,1)S(1)}, bf16[6,32,768]{2,1,0:T(8,128)(2,1)S(1)}, u32[]{:S(2)}, u32[]{:S(2)}) collective-permute-start(bf16[6,32,768]{2,1,0:T(8,128)(2,1)S(1)} %get-tuple-element.82), channel_id=1, source_target_pairs={{0,1},{1,2},{2,3},{3,0},{4,5},{5,6},{6,7},{7,4},{8,9},{9,10},{10,1... | collective-permute-start | bytes 884744 | tf_op jit(solution)/shard_map/ppermute | solution.py:283
  80.8 9.3 %collective-permute-start.16 = (bf16[5,32,768]{2,1,0:T(8,128)(2,1)S(1)}, bf16[5,32,768]{2,1,0:T(8,128)(2,1)S(1)}, u32[]{:S(2)}, u32[]{:S(2)}) collective-permute-start(bf16[5,32,768]{2,1,0:T(8,128)(2,1)S(1)} %get-tuple-element.84), channel_id=1, source_target_pairs={{0,3},{1,0},{2,1},{3,2},{4,7},{5,4},{6,5},{7,6},{8,11},{9,8},{10,9... | collective-permute-start | bytes 737288 | tf_op jit(solution)/shard_map/ppermute | solution.py:283
  83.8 7.4 %collective-permute-start.17 = (bf16[5,32,768]{2,1,0:T(8,128)(2,1)S(1)}, bf16[5,32,768]{2,1,0:T(8,128)(2,1)S(1)}, u32[]{:S(2)}, u32[]{:S(2)}) collective-permute-start(bf16[5,32,768]{2,1,0:T(8,128)(2,1)S(1)} %get-tuple-element.86), channel_id=1, source_target_pairs={{0,1},{1,2},{2,3},{3,0},{4,5},{5,6},{6,7},{7,4},{8,9},{9,10},{10,1... | collective-permute-start | bytes 737288 | tf_op jit(solution)/shard_map/ppermute | solution.py:283
  87.1 9.4 %collective-permute-start.18 = (bf16[6,32,768]{2,1,0:T(8,128)(2,1)S(1)}, bf16[6,32,768]{2,1,0:T(8,128)(2,1)S(1)}, u32[]{:S(2)}, u32[]{:S(2)}) collective-permute-start(bf16[6,32,768]{2,1,0:T(8,128)(2,1)S(1)} %get-tuple-element.91), channel_id=1, source_target_pairs={{0,4},{1,5},{2,6},{3,7},{4,0},{5,1},{6,2},{7,3},{8,12},{9,13},{10,... | collective-permute-start | bytes 884744 | tf_op jit(solution)/shard_map/ppermute | solution.py:280
  91.7 9.8 %collective-permute-start.19 = (bf16[5,32,768]{2,1,0:T(8,128)(2,1)S(1)}, bf16[5,32,768]{2,1,0:T(8,128)(2,1)S(1)}, u32[]{:S(2)}, u32[]{:S(2)}) collective-permute-start(bf16[5,32,768]{2,1,0:T(8,128)(2,1)S(1)} %get-tuple-element.98), channel_id=1, source_target_pairs={{0,4},{1,5},{2,6},{3,7},{4,0},{5,1},{6,2},{7,3},{8,12},{9,13},{10,... | collective-permute-start | bytes 737288 | tf_op jit(solution)/shard_map/ppermute | solution.py:280
  96.6 7.6 %collective-permute-start.20 = (bf16[4,32,768]{2,1,0:T(8,128)(2,1)S(1)}, bf16[4,32,768]{2,1,0:T(8,128)(2,1)S(1)}, u32[]{:S(2)}, u32[]{:S(2)}) collective-permute-start(bf16[4,32,768]{2,1,0:T(8,128)(2,1)S(1)} %get-tuple-element.99), channel_id=1, source_target_pairs={{0,8},{8,16},{16,24},{24,32},{32,40},{40,48},{48,56},{64,72},{72,8... | collective-permute-start | bytes 589832 | tf_op jit(solution)/shard_map/ppermute | solution.py:291

commit v6 on v5

--- a/solution.py
+++ b/solution.py
@@ -15,6 +15,8 @@
 GIVEN = 2
 FIRST = ((0, 2, DOWN), (1, 2, DOWN), (0, 1, LOOSE0), (0, 1, LOOSE1), (0, 1, UP), (1, 1, LOOSE0))
 LAST = ((1, 0, LOOSE1), (1, 0, UP), (1, 1, LOOSE1), (1, 1, DOWN), (1, 1, UP))
+
+WAITING = 100_000_000_000
 OWN = ((0, 0), (0, 1), (1, 0), (1, 1))
 BESIDE = ((2, 0), (2, 1))
 ABOVE = ((0, 2), (1, 2))
@@ -187,7 +189,7 @@
         in_specs=[vmem] * (1 + len(arrays)),
         out_specs=[vmem] * (1 + len(out_shape)),
         compiler_params=pltpu.CompilerParams(vmem_limit_bytes=6 * MIB),
-        cost_estimate=pl.CostEstimate(flops=0, bytes_accessed=size, transcendentals=0),
+        cost_estimate=pl.CostEstimate(flops=size, bytes_accessed=0, transcendentals=0),
         name=name,
     )(token, *arrays)
     return outs, token
@@ -202,10 +204,14 @@
     out_token[...] = token[...]
 
 
-def keep_kernel(token, own, before, after, rows, out_token):
+def keep_kernel(token, own, before, after, *refs):
+    rows, out_token = refs[-2:]
     count = own.shape[0]
     for i in range(count):
-        rows[i] = own[i] + decode(before, i) + decode(after, count + i)
+        value = own[i] + decode(before, i) + decode(after, count + i)
+        for other in refs[:-2]:
+            value = value + decode(other, i)
+        rows[i] = value
     out_token[...] = token[...]
 
 
@@ -213,6 +219,12 @@
     for i in range(GIVEN):
         encode(rows, i, kept[i])
         rows[GIVEN + i] = other[i]
+    out_token[...] = token[...]
+
+
+def read_kernel(token, sums, rows, out_token):
+    for i in range(sums.shape[0]):
+        rows[i] = decode(sums, i)
     out_token[...] = token[...]
 
 
@@ -221,52 +233,48 @@
     for i in range(up_own.shape[0]):
         encode(up, i, up_own[i] + decode(up_received, i))
         encode(down, i, down_own[i] + decode(down_received, i))
-    for i in range(up_own.shape[0], up.shape[0]):
-        up[i] = jnp.zeros_like(up[i])
-        down[i] = jnp.zeros_like(down[i])
     out_token[...] = token[...]
 
 
 def back_kernel(token, down_arrived, own, up_received, *refs):
-    out, out_token = refs[-2:]
+    outs, out_token = refs[1:-1], refs[-1]
     count = own.shape[0]
     for i in range(count):
-        encode(out, i, own[i] + decode(up_received, count + i) + decode(down_arrived, i))
-    out_token[...] = token[...]
-
-
-def final_kernel(meta, offsets, *refs):
-    given, _, out = refs[-3:]
+        value = own[i] + decode(up_received, count + i) + decode(down_arrived, i)
+        first = outs[0].shape[0]
+        encode(outs[0] if i < first else outs[1], i if i < first else i - first, value)
+    out_token[...] = token[...]
+
+
+def final_kernel(meta, offsets, early, kept_one, kept_two, other_one, other_two, given, token, out):
     x_lo = meta[0]
     slots = slot_table(offsets)
-    for g, group in enumerate((EARLY, FIRST, LAST)):
-        kept, other = refs[2 * g : 2 * g + 2]
-        for b, (tx, ty, slot) in enumerate(group):
-            pair = slots[slot][2]
-            if g == 0:
-                for freq in range(2):
-                    out[tx, ty, pair, freq] = kept[2 * b + freq] + decode(other, 2 * b + freq)
-            elif ty == 2:
-                out[tx, 0, pair, x_lo] = decode(given, b)
-                out[tx, 0, pair, 1 - x_lo] = decode(given, GIVEN + b)
-            else:
-                out[tx, ty, pair, x_lo] = kept[b]
-                out[tx, ty, pair, 1 - x_lo] = decode(other, b)
-
-
-def final(meta, offsets, parts, given, token, shape):
+    for b, (tx, ty, slot) in enumerate(EARLY):
+        for freq in range(2):
+            out[tx, ty, slots[slot][2], freq] = early[2 * b + freq]
+    for b, (tx, ty, slot) in enumerate(FIRST + LAST):
+        pair = slots[slot][2]
+        if b < GIVEN:
+            out[tx, 0, pair, x_lo] = decode(given, b)
+            out[tx, 0, pair, 1 - x_lo] = decode(given, GIVEN + b)
+        else:
+            late = b >= len(FIRST)
+            out[tx, ty, pair, x_lo] = kept_two[b - len(FIRST)] if late else kept_one[b]
+            out[tx, ty, pair, 1 - x_lo] = other_two[b - len(FIRST)] if late else other_one[b - GIVEN]
+
+
+def final(meta, offsets, parts, token, shape):
     smem = pl.BlockSpec(memory_space=pltpu.SMEM)
     vmem = pl.BlockSpec(memory_space=pltpu.VMEM)
-    flat = [part for group in parts for part in group]
     return pl.pallas_call(
         final_kernel,
         out_shape=jax.ShapeDtypeStruct(shape, jnp.float32),
-        in_specs=[smem, smem] + [vmem] * (len(flat) + 2),
+        in_specs=[smem, smem] + [vmem] * (len(parts) + 1),
         out_specs=vmem,
         compiler_params=pltpu.CompilerParams(vmem_limit_bytes=10 * MIB),
         cost_estimate=pl.CostEstimate(flops=0, bytes_accessed=0, transcendentals=0),
         name="place_blocks",
-    )(meta, offsets, *flat, given, token)
+    )(meta, offsets, *parts, token)
 
 
 def per_device(green, offsets):
@@ -290,25 +298,28 @@
         ]
         return lax.ppermute(value, ("gx", "gy"), perm)
 
-    def coded(value, spare=0):
+    def coded(value):
         count, rows, columns = value.shape
-        return jax.ShapeDtypeStruct((count + spare, rows, columns // 2 * 3), jnp.bfloat16)
+        return jax.ShapeDtypeStruct((count, rows, columns // 2 * 3), jnp.bfloat16)
 
     def first(pieces):
         return around(pieces[2], 1), around(pieces[3], -1)
 
-    def second(pieces, received, token, also=(), spare=0):
+    def second(pieces, received, token, also=(), size=0):
         up, down = pieces[4], pieces[5]
-        (up, down), token = call_step(second_kernel, [coded(up, spare), coded(down, spare)], token, [*received, up, down, *also], "second")
+        arrays = [*received, up, down, *also]
+        (up, down), token = call_step(second_kernel, [coded(up), coded(down)], token, arrays, "second", size)
         return (around(up, 1), around(down, -1)), token
 
-    def back(pieces, received, arrived, token):
+    def back(pieces, received, arrived, token, apart=0):
         own = pieces[1]
-        (out,), token = call_step(back_kernel, [coded(own)], token, [arrived[1], own, received[0], arrived[0]], "back")
-        return swap(out), token
-
-    def keep(pieces, received, arrived, token):
-        (rows,), token = call_step(keep_kernel, [pieces[0]], token, [pieces[0], arrived[0], received[1]], "keep", 16 * MIB)
+        outs = [coded(own[:apart]), coded(own[apart:])] if apart else [coded(own)]
+        outs, token = call_step(back_kernel, outs, token, [arrived[1], own, received[0], arrived[0]], "back")
+        return [swap(out) for out in outs], token
+
+    def keep(pieces, received, arrived, token, others=()):
+        arrays = [pieces[0], arrived[0], received[1], *others]
+        (rows,), token = call_step(keep_kernel, [pieces[0]], token, arrays, "keep")
         return rows, token
 
     def blocks(groups, inputs, token, name):
@@ -333,28 +344,32 @@
     above_theirs = tiles_from(above, 0, 1)
     beside = tiles_from(beside, 1, 0)
     corner = tiles_from(corner, 1, 1)
-    early_second, token = second(early, early_first, token)
+    early_second, token = second(early, early_first, token, size=WAITING)
     tiles = [(OWN, mine.reshape(4, *shape)), (OWN, theirs.reshape(4, *shape)), (ABOVE, above_mine), (ABOVE, above_theirs)]
     tiles += [(BESIDE, beside[0]), (BESIDE, beside[1])]
     (one,), token = blocks((FIRST,), tiles, token, "first_blocks")
     one_first = first(one)
-    early_back, token = back(early, early_first, early_second, token)
     tiles += [(CORNER, corner[:1]), (CORNER, corner[1:])]
     (two,), token = blocks((LAST,), tiles, token, "last_blocks")
     two_first = first(two)
-    one_second, token = second(one, one_first, token, [early_back])
+    early_back, token = back(early, early_first, early_second, token)
+    one_second, token = second(one, one_first, token, early_back)
     two_second, token = second(two, two_first, token)
-    one_back, token = back(one, one_first, one_second, token)
-    two_back, token = back(two, two_first, two_second, token)
+    (one_given, one_back), token = back(one, one_first, one_second, token, GIVEN)
+    (two_back,), token = back(two, two_first, two_second, token)
     one_kept, token = keep(one, one_first, one_second, token)
     rows = jax.ShapeDtypeStruct((2 * GIVEN,) + one_back.shape[1:], one_back.dtype)
-    (given,), token = call_step(give_kernel, [rows], token, [one_kept, one_back], "give")
+    (given,), token = call_step(give_kernel, [rows], token, [one_kept, one_given], "give")
     given = tiles_from(given, 0, -1)
-    early_kept, token = keep(early, early_first, early_second, token)
+    early_kept, token = keep(early, early_first, early_second, token, early_back)
     two_kept, token = keep(two, two_first, two_second, token)
-    parts = [(early_kept, early_back), (one_kept, one_back), (two_kept, two_back)]
+    rows = jax.ShapeDtypeStruct((one_back.shape[0],) + one_kept.shape[1:], jnp.float32)
+    (one_other,), token = call_step(read_kernel, [rows], token, [one_back], "read", WAITING)
+    rows = jax.ShapeDtypeStruct((two_back.shape[0],) + one_kept.shape[1:], jnp.float32)
+    (two_other,), token = call_step(read_kernel, [rows], token, [two_back], "read")
+    parts = [early_kept, one_kept, two_kept, one_other, two_other, given]
     shape = green.shape[:2] + (NPAIR, green.shape[2], points // (2 * RING), 2 * points)
-    return final(meta, offsets, parts, given, token, shape)
+    return final(meta, offsets, parts, token, shape)
 
 
 def solution(mesh):

time: 107 us -> 106 us (level); the launches traced: 107 us -> 104 us
  waiting for transfers between devices: 46.2 us -> 40.9 us
  starting transfers between devices: 36.3 us -> 39.7 us
    ppermute x4 -> x5, waiting for transfers between devices: 14.3 us -> 3.58 us  [swap(): lax.ppermute(value, 'sa', [(i, (i + RING) % (2 * RING)) for i in range(2...]
    ppermute x5, waiting for transfers between devices: 15.7 us -> 25.4 us  [tiles_from(): return lax.ppermute(value, ('gx', 'gy'), perm)]
    ppermute x4 -> x5, starting transfers between devices: 5.26 us -> 10.1 us  [swap(): lax.ppermute(value, 'sa', [(i, (i + RING) % (2 * RING)) for i in range(2...]
    ppermute x12, waiting for transfers between devices: 16.2 us -> 11.9 us  [around(): lax.ppermute(value, 'sa', [(h * RING + i, h * RING + (i + steps) % RING)...]
    ppermute x12, starting transfers between devices: 19.1 us -> 16.6 us  [around(): lax.ppermute(value, 'sa', [(h * RING + i, h * RING + (i + steps) % RING)...]
    pallas_call x11 -> x13, Pallas kernels: 6.37 us -> 6.96 us  [call_step(): pl.pallas_call(kernel, out_shape=list(out_shape) + [jax.ShapeDtypeStruct(...]
  transfers between devices with their start and end apart: 21 -> 22, of which waited for: 15 -> 8; matrix products, arithmetic and copies ran while one was open for 0% -> 0% of each run, Pallas kernels for 16% -> 17%
where the time goes in v6:
time: 106 us; the launch traced here: 104 us
  waiting for transfers between devices  40.9 us (39%)
  starting transfers between devices  39.7 us (37%)
  Pallas kernels  19.6 us (18%)
  local copies, waits for them, and re-layouts  3.59 us (3%)
    ppermute x5, waiting for transfers between devices, tiles_from(): return lax.ppermute(value, ('gx', 'gy'), perm)  25.4 us
    ppermute x12, starting transfers between devices, around(): lax.ppermute(value, 'sa', [(h * RING + i, h * RING + (i + steps) % RING)...  16.6 us
    ppermute x5, starting transfers between devices, tiles_from(): return lax.ppermute(value, ('gx', 'gy'), perm)  12.9 us
    ppermute x12, waiting for transfers between devices, around(): lax.ppermute(value, 'sa', [(h * RING + i, h * RING + (i + steps) % RING)...  11.9 us
    pallas_call x3, Pallas kernels, call_blocks(): pl.pallas_call(kernel, out_shape=out_shape + [jax.ShapeDtypeStruct(token....  10.5 us
    ppermute x5, starting transfers between devices, swap(): lax.ppermute(value, 'sa', [(i, (i + RING) % (2 * RING)) for i in range(2...  10.1 us
    pallas_call x13, Pallas kernels, call_step(): pl.pallas_call(kernel, out_shape=list(out_shape) + [jax.ShapeDtypeStruct(...  6.96 us
    ppermute x5, waiting for transfers between devices, swap(): lax.ppermute(value, 'sa', [(i, (i + RING) % (2 * RING)) for i in range(2...  3.58 us
  transfers between devices with their start and end apart: 22, of which 8 were waited for; matrix products, arithmetic and copies ran while one was open for 0% of the time, Pallas kernels for 17%

profile of v6, /device:TPU:100, one launch (start us, length us, event | category | flops | bytes accessed | tf_op | source)
XLA Modules:
  0.0 104.1 jit_solution(16969813700312782780)
XLA Ops:
  0.0 1.7 %dynamic-slice_bitcast_fusion = (bf16[2,2,2,256,256]{4,3,2,1,0:T(8,128)(2,1)S(1)}, bf16[2,2,1,2,256,256]{5,4,3,2,1,0:T(8,128)(2,1)S(1)}) fusion(bf16[2,2,2,2,256,256]{5,4,3,2,1,0:T(8,128)(2,1)} %green.1, s32[]{:T(128)S(6)} %select_n.21, s32[]{:T(128)S(6)} %select_n.20), kind=kLoop, calls=%fused_computation.1 | loop fusion | bytes 4194312 | tf_op jit(solution)/shard_map/jit(dynamic_index_in_dim)/squeeze | solution.py:331
  1.7 1.3 %collective-permute-start = (bf16[2,2,2,256,256]{4,3,2,1,0:T(8,128)(2,1)S(1)}, bf16[2,2,2,256,256]{4,3,2,1,0:T(8,128)(2,1)S(1)}, u32[]{:S(2)}, u32[]{:S(2)}) collective-permute-start(bf16[2,2,2,256,256]{4,3,2,1,0:T(8,128)(2,1)S(1)} %get-tuple-element.111), channel_id=1, source_target_pairs={{0,4},{1,5},{2,6},{3,7},{4,0},{5,1},{6,2},{7,3},{8,12},{9,13},{10,... | collective-permute-start | bytes 3145736 | tf_op jit(solution)/shard_map/ppermute | solution.py:288
  3.0 0.1 copy.8.offsets.refs_1_
  3.1 0.1 pad_add_fusion.meta.refs_0_
  3.2 1.6 %copy-done = bf16[2,2,2,2,256,256]{5,4,3,2,1,0:T(8,128)(2,1)S(1)} copy-done((bf16[2,2,2,2,256,256]{5,4,3,2,1,0:T(8,128)(2,1)S(1)}, bf16[2,2,2,2,256,256]{5,4,3,2,1,0:T(8,128)(2,1)}, u32[]{:S(2)}) %copy-start) | copy-done | bytes 2097176
  4.7 3.3 %early_blocks.1 = (f32[10,32,512]{2,1,0:T(8,128)S(1)}, f32[10,32,512]{2,1,0:T(8,128)S(1)}, bf16[20,32,768]{2,1,0:T(8,128)(2,1)S(1)}, bf16[20,32,768]{2,1,0:T(8,1...) custom-call(s32[2]{0:T(128)S(1)} %pad_add_fusion.meta.refs_0_, ...), custom_call_target="tpu_custom_call" | custom-call | tf_op jit(solution)/shard_map/early_blocks/pallas_call | solution.py:167
  8.1 1.7 %collective-permute-start.2 = (bf16[20,32,768]{2,1,0:T(8,128)(2,1)S(1)}, bf16[20,32,768]{2,1,0:T(8,128)(2,1)S(1)}, u32[]{:S(2)}, u32[]{:S(2)}) collective-permute-start(bf16[20,32,768]{2,1,0:T(8,128)(2,1)S(1)} %get-tuple-element.60), channel_id=1, source_target_pairs={{0,1},{1,2},{2,3},{3,0},{4,5},{5,6},{6,7},{7,4},{8,9},{9,10},{10,1... | collective-permute-start | bytes 2949128 | tf_op jit(solution)/shard_map/ppermute | solution.py:291
  9.8 1.7 %collective-permute-start.3 = (bf16[20,32,768]{2,1,0:T(8,128)(2,1)S(1)}, bf16[20,32,768]{2,1,0:T(8,128)(2,1)S(1)}, u32[]{:S(2)}, u32[]{:S(2)}) collective-permute-start(bf16[20,32,768]{2,1,0:T(8,128)(2,1)S(1)} %get-tuple-element.61), channel_id=1, source_target_pairs={{0,3},{1,0},{2,1},{3,2},{4,7},{5,4},{6,5},{7,6},{8,11},{9,8},{10,9... | collective-permute-start | bytes 2949128 | tf_op jit(solution)/shard_map/ppermute | solution.py:291
  11.4 0.1 copy.11
  11.5 2.0 %collective-permute-start.1 = (bf16[2,2,256,256]{3,2,1,0:T(8,128)(2,1)S(1)}, bf16[2,2,256,256]{3,2,1,0:T(8,128)(2,1)S(1)}, u32[]{:S(2)}, u32[]{:S(2)}) collective-permute-start(bf16[2,2,256,256]{3,2,1,0:T(8,128)(2,1)S(1)} %slice_bitcast_fusion.2), channel_id=1, source_target_pairs={{8,0},{16,8},{24,16},{32,24},{40,32},{48,40},{56,48},{72,64},{80,7... | collective-permute-start | bytes 1572872 | tf_op jit(solution)/shard_map/ppermute | solution.py:299
  13.6 14.2 %collective-permute-done.1.above_mine.refs_5_ = bf16[2,2,256,256]{3,2,1,0:T(8,128)(2,1)S(1)} collective-permute-done((bf16[2,2,256,256]{3,2,1,0:T(8,128)(2,1)S(1)}, bf16[2,2,256,256]{3,2,1,0:T(8,128)(2,1)S(1)}, u32[]{:S(2)}, u32[]{:S(2)}) %collective-permute-start.1) | collective-permute-done | bytes 524320 | tf_op jit(solution)/shard_map/ppermute | solution.py:299
  27.8 0.0 collective-permute-done.theirs
  27.8 0.1 swapped.1
  27.9 1.9 %collective-permute-start.4 = (bf16[2,2,256,256]{3,2,1,0:T(8,128)(2,1)S(1)}, bf16[2,2,256,256]{3,2,1,0:T(8,128)(2,1)S(1)}, u32[]{:S(2)}, u32[]{:S(2)}) collective-permute-start(bf16[2,2,256,256]{3,2,1,0:T(8,128)(2,1)S(1)} %get-tuple-element.65), channel_id=1, source_target_pairs={{8,0},{16,8},{24,16},{32,24},{40,32},{48,40},{56,48},{72,64},{80,7... | collective-permute-start | bytes 1572872 | tf_op jit(solution)/shard_map/ppermute | solution.py:299
  29.9 1.9 %collective-permute-start.6 = (bf16[2,2,256,256]{3,2,1,0:T(8,128)(2,1)S(1)}, bf16[2,2,256,256]{3,2,1,0:T(8,128)(2,1)S(1)}, u32[]{:S(2)}, u32[]{:S(2)}) collective-permute-start(bf16[2,2,256,256]{3,2,1,0:T(8,128)(2,1)S(1)} %get-tuple-element.68), channel_id=1, source_target_pairs={{72,0},{80,8},{88,16},{96,24},{104,32},{112,40},{120,48},{136,64},... | collective-permute-start | bytes 1572872 | tf_op jit(solution)/shard_map/ppermute | solution.py:299
  31.8 1.9 %collective-permute-start.5 = (bf16[2,2,2,256,256]{4,3,2,1,0:T(8,128)(2,1)S(1)}, bf16[2,2,2,256,256]{4,3,2,1,0:T(8,128)(2,1)S(1)}, u32[]{:S(2)}, u32[]{:S(2)}) collective-permute-start(bf16[2,2,2,256,256]{4,3,2,1,0:T(8,128)(2,1)S(1)} %get-tuple-element.66), channel_id=1, source_target_pairs={{64,0},{72,8},{80,16},{88,24},{96,32},{104,40},{112,48},{120,56},{... | collective-permute-start | bytes 3145736 | tf_op jit(solution)/shard_map/ppermute | solution.py:299
  33.7 0.0 collective-permute-done.2.up_received
  33.7 0.0 collective-permute-done.3.down_received.after
  33.7 1.3 %second.3 = (bf16[10,32,768]{2,1,0:T(8,128)(2,1)S(1)}, bf16[10,32,768]{2,1,0:T(8,128)(2,1)S(1)}, f32[8,128]{1,0:T(8,128)S(1)}) custom-call(f32[8,128]{1,0:T(8,128)S(1)} %get-tuple-element.59.token, bf16[20,32,768]{2,1,0:T(8,128)(2,1)S(1)} %collective-permute-done.2.up_received, bf16[20,32,768]{2,1,0:T(8,128)(2,1)S(1)} %collective-permute-done.3.down_received.after, ...), custom_call_target="tpu_custom_call" | custom-call | flops 99999997952 | tf_op jit(solution)/shard_map/second/pallas_call | solution.py:186
  35.1 2.4 %collective-permute-start.7 = (bf16[10,32,768]{2,1,0:T(8,128)(2,1)S(1)}, bf16[10,32,768]{2,1,0:T(8,128)(2,1)S(1)}, u32[]{:S(2)}, u32[]{:S(2)}) collective-permute-start(bf16[10,32,768]{2,1,0:T(8,128)(2,1)S(1)} %get-tuple-element.70), channel_id=1, source_target_pairs={{0,3},{1,0},{2,1},{3,2},{4,7},{5,4},{6,5},{7,6},{8,11},{9,8},{10,9... | collective-permute-start | bytes 1474568 | tf_op jit(solution)/shard_map/ppermute | solution.py:291
  37.5 0.0 collective-permute-start.8
  37.5 9.5 %collective-permute-done.5 = bf16[2,2,2,256,256]{4,3,2,1,0:T(8,128)(2,1)S(1)} collective-permute-done((bf16[2,2,2,256,256]{4,3,2,1,0:T(8,128)(2,1)S(1)}, bf16[2,2,2,256,256]{4,3,2,1,0:T(8,128)(2,1)S(1)}, u32[]{:S(2)}, u32[]{:S(2)}) %collective-permute-start.5) | collective-permute-done | bytes 1048608 | tf_op jit(solution)/shard_map/ppermute | solution.py:299
  47.0 0.1 slice_bitcast_fusion
  47.1 0.0 collective-permute-done.4.refs_6_
  47.1 3.8 %first_blocks.1 = (f32[6,32,512]{2,1,0:T(8,128)S(1)}, f32[6,32,512]{2,1,0:T(8,128)S(1)}, bf16[12,32,768]{2,1,0:T(8,128)(2,1)S(1)}, bf16[12,32,768]{2,1,0:T(8,128...) custom-call(s32[2]{0:T(128)S(1)} %pad_add_fusion.meta.refs_0_, ...), custom_call_target="tpu_custom_call" | custom-call | tf_op jit(solution)/shard_map/first_blocks/pallas_call | solution.py:167
  50.9 1.5 %collective-permute-start.9 = (bf16[12,32,768]{2,1,0:T(8,128)(2,1)S(1)}, bf16[12,32,768]{2,1,0:T(8,128)(2,1)S(1)}, u32[]{:S(2)}, u32[]{:S(2)}) collective-permute-start(bf16[12,32,768]{2,1,0:T(8,128)(2,1)S(1)} %get-tuple-element.74), channel_id=1, source_target_pairs={{0,1},{1,2},{2,3},{3,0},{4,5},{5,6},{6,7},{7,4},{8,9},{9,10},{10,1... | collective-permute-start | bytes 1769480 | tf_op jit(solution)/shard_map/ppermute | solution.py:291
  52.4 2.0 %collective-permute-start.10 = (bf16[12,32,768]{2,1,0:T(8,128)(2,1)S(1)}, bf16[12,32,768]{2,1,0:T(8,128)(2,1)S(1)}, u32[]{:S(2)}, u32[]{:S(2)}) collective-permute-start(bf16[12,32,768]{2,1,0:T(8,128)(2,1)S(1)} %get-tuple-element.75), channel_id=1, source_target_pairs={{0,3},{1,0},{2,1},{3,2},{4,7},{5,4},{6,5},{7,6},{8,11},{9,8},{10,9... | collective-permute-start | bytes 1769480 | tf_op jit(solution)/shard_map/ppermute | solution.py:291
  54.4 0.0 collective-permute-done.6
  54.4 3.3 %last_blocks.1 = (f32[5,32,512]{2,1,0:T(8,128)S(1)}, f32[5,32,512]{2,1,0:T(8,128)S(1)}, bf16[10,32,768]{2,1,0:T(8,128)(2,1)S(1)}, bf16[10,32,768]{2,1,0:T(8,128)...) custom-call(s32[2]{0:T(128)S(1)} %pad_add_fusion.meta.refs_0_, ...), custom_call_target="tpu_custom_call" | custom-call | tf_op jit(solution)/shard_map/last_blocks/pallas_call | solution.py:167
  57.8 0.0 collective-permute-done.7.down_arrived
  57.8 0.0 collective-permute-done.8.refs_0_.before
  57.8 1.0 back.3
  58.8 2.7 %collective-permute-start.11 = (bf16[10,32,768]{2,1,0:T(8,128)(2,1)S(1)}, bf16[10,32,768]{2,1,0:T(8,128)(2,1)S(1)}, u32[]{:S(2)}, u32[]{:S(2)}) collective-permute-start(bf16[10,32,768]{2,1,0:T(8,128)(2,1)S(1)} %get-tuple-element.78), channel_id=1, source_target_pairs={{0,4},{1,5},{2,6},{3,7},{4,0},{5,1},{6,2},{7,3},{8,12},{9,13},{10,... | collective-permute-start | bytes 1474568 | tf_op jit(solution)/shard_map/ppermute | solution.py:288
  61.4 0.5 collective-permute-start.12
  61.9 2.7 %collective-permute-start.13 = (bf16[10,32,768]{2,1,0:T(8,128)(2,1)S(1)}, bf16[10,32,768]{2,1,0:T(8,128)(2,1)S(1)}, u32[]{:S(2)}, u32[]{:S(2)}) collective-permute-start(bf16[10,32,768]{2,1,0:T(8,128)(2,1)S(1)} %get-tuple-element.81), channel_id=1, source_target_pairs={{0,3},{1,0},{2,1},{3,2},{4,7},{5,4},{6,5},{7,6},{8,11},{9,8},{10,9... | collective-permute-start | bytes 1474568 | tf_op jit(solution)/shard_map/ppermute | solution.py:291
  64.7 3.6 %collective-permute-done.11.refs_0_ = bf16[10,32,768]{2,1,0:T(8,128)(2,1)S(1)} collective-permute-done((bf16[10,32,768]{2,1,0:T(8,128)(2,1)S(1)}, bf16[10,32,768]{2,1,0:T(8,128)(2,1)S(1)}, u32[]{:S(2)}, u32[]{:S(2)}) %collective-permute-start.11) | collective-permute-done | bytes 491552 | tf_op jit(solution)/shard_map/ppermute | solution.py:288
  68.2 0.4 collective-permute-done.9.up_received
  68.6 0.8 second.4
  69.4 1.6 %collective-permute-start.14 = (bf16[6,32,768]{2,1,0:T(8,128)(2,1)S(1)}, bf16[6,32,768]{2,1,0:T(8,128)(2,1)S(1)}, u32[]{:S(2)}, u32[]{:S(2)}) collective-permute-start(bf16[6,32,768]{2,1,0:T(8,128)(2,1)S(1)} %get-tuple-element.85), channel_id=1, source_target_pairs={{0,3},{1,0},{2,1},{3,2},{4,7},{5,4},{6,5},{7,6},{8,11},{9,8},{10,9... | collective-permute-start | bytes 884744 | tf_op jit(solution)/shard_map/ppermute | solution.py:291
  71.1 0.5 collective-permute-start.15
  71.5 7.6 %collective-permute-done.12.up_received = bf16[10,32,768]{2,1,0:T(8,128)(2,1)S(1)} collective-permute-done((bf16[10,32,768]{2,1,0:T(8,128)(2,1)S(1)}, bf16[10,32,768]{2,1,0:T(8,128)(2,1)S(1)}, u32[]{:S(2)}, u32[]{:S(2)}) %collective-permute-start.12) | collective-permute-done | bytes 491552 | tf_op jit(solution)/shard_map/ppermute | solution.py:291
  79.1 0.0 collective-permute-done.13.down_received.after
  79.1 0.7 second.5
  79.8 1.3 %collective-permute-start.16 = (bf16[5,32,768]{2,1,0:T(8,128)(2,1)S(1)}, bf16[5,32,768]{2,1,0:T(8,128)(2,1)S(1)}, u32[]{:S(2)}, u32[]{:S(2)}) collective-permute-start(bf16[5,32,768]{2,1,0:T(8,128)(2,1)S(1)} %get-tuple-element.89), channel_id=1, source_target_pairs={{0,3},{1,0},{2,1},{3,2},{4,7},{5,4},{6,5},{7,6},{8,11},{9,8},{10,9... | collective-permute-start | bytes 737288 | tf_op jit(solution)/shard_map/ppermute | solution.py:291
  81.2 0.8 collective-permute-start.17
  81.9 0.0 collective-permute-done.14.down_arrived
  81.9 2.0 %collective-permute-done.15.refs_0_.before = bf16[6,32,768]{2,1,0:T(8,128)(2,1)S(1)} collective-permute-done((bf16[6,32,768]{2,1,0:T(8,128)(2,1)S(1)}, bf16[6,32,768]{2,1,0:T(8,128)(2,1)S(1)}, u32[]{:S(2)}, u32[]{:S(2)}) %collective-permute-start.15) | collective-permute-done | bytes 294944 | tf_op jit(solution)/shard_map/ppermute | solution.py:291
  83.9 0.6 back.4
  84.5 1.3 %collective-permute-start.19 = (bf16[4,32,768]{2,1,0:T(8,128)(2,1)S(1)}, bf16[4,32,768]{2,1,0:T(8,128)(2,1)S(1)}, u32[]{:S(2)}, u32[]{:S(2)}) collective-permute-start(bf16[4,32,768]{2,1,0:T(8,128)(2,1)S(1)} %get-tuple-element.104), channel_id=1, source_target_pairs={{0,4},{1,5},{2,6},{3,7},{4,0},{5,1},{6,2},{7,3},{8,12},{9,13},{10,... | collective-permute-start | bytes 589832 | tf_op jit(solution)/shard_map/ppermute | solution.py:288
  85.8 0.8 collective-permute-start.18
  86.6 0.0 collective-permute-done.16.down_arrived
  86.6 1.9 %collective-permute-done.17.refs_0_.before = bf16[5,32,768]{2,1,0:T(8,128)(2,1)S(1)} collective-permute-done((bf16[5,32,768]{2,1,0:T(8,128)(2,1)S(1)}, bf16[5,32,768]{2,1,0:T(8,128)(2,1)S(1)}, u32[]{:S(2)}, u32[]{:S(2)}) %collective-permute-start.17) | collective-permute-done | bytes 245792 | tf_op jit(solution)/shard_map/ppermute | solution.py:291
  88.6 0.5 back.5
  89.1 4.0 %collective-permute-start.20 = (bf16[5,32,768]{2,1,0:T(8,128)(2,1)S(1)}, bf16[5,32,768]{2,1,0:T(8,128)(2,1)S(1)}, u32[]{:S(2)}, u32[]{:S(2)}) collective-permute-start(bf16[5,32,768]{2,1,0:T(8,128)(2,1)S(1)} %get-tuple-element.107), channel_id=1, source_target_pairs={{0,4},{1,5},{2,6},{3,7},{4,0},{5,1},{6,2},{7,3},{8,12},{9,13},{10,... | collective-permute-start | bytes 737288 | tf_op jit(solution)/shard_map/ppermute | solution.py:288
  93.1 0.4 keep.3
  93.5 0.0 collective-permute-done.18.other
  93.5 0.1 give.1
  93.6 5.1 %collective-permute-start.21 = (bf16[4,32,768]{2,1,0:T(8,128)(2,1)S(1)}, bf16[4,32,768]{2,1,0:T(8,128)(2,1)S(1)}, u32[]{:S(2)}, u32[]{:S(2)}) collective-permute-start(bf16[4,32,768]{2,1,0:T(8,128)(2,1)S(1)} %get-tuple-element.109), channel_id=1, source_target_pairs={{0,8},{8,16},{16,24},{24,32},{32,40},{40,48},{48,56},{64,72},{72,8... | collective-permute-start | bytes 589832 | tf_op jit(solution)/shard_map/ppermute | solution.py:299
  98.7 0.9 keep.4
  99.6 0.3 keep.5
  100.0 0.1 read.2
  100.1 0.2 read.3
  100.3 1.6 %collective-permute-done.21.given = bf16[4,32,768]{2,1,0:T(8,128)(2,1)S(1)} collective-permute-done((bf16[4,32,768]{2,1,0:T(8,128)(2,1)S(1)}, bf16[4,32,768]{2,1,0:T(8,128)(2,1)S(1)}, u32[]{:S(2)}, u32[]{:S(2)}) %collective-permute-start.21) | collective-permute-done | bytes 196640 | tf_op jit(solution)/shard_map/ppermute | solution.py:299
  101.9 2.2 %place_blocks.1 = f32[2,2,4,2,32,512]{5,4,3,2,1,0:T(8,128)} custom-call(s32[2]{0:T(128)S(1)} %pad_add_fusion.meta.refs_0_, s32[4,2]{1,0:T(4,128)S(1)} %copy.8.offsets.refs_1_, f32[10,32,512]{2,1,0:T(8,128)S(1)} %get-tuple-element.99.early, f32[6,32,512]{2,1,0:T(8,128)S(1)} %get-tuple-element.95.kept.kept_one, f32[5,32,512]{2,1,0:T(8,128)S(1)} %get-tuple-element.102.kept_two, ...), custom_call_target="tpu_custom_call" | custom-call | tf_op jit(solution)/shard_map/place_blocks/pallas_call | solution.py:269
  (9 shorter events, 0.1 us)
Async XLA Ops:
  0.0 3.0 %copy-start.1 = (s32[4,2]{0,1:T(2,128)S(1)}, s32[4,2]{0,1:T(2,128)}, u32[]{:S(2)}) copy-start(s32[4,2]{0,1:T(2,128)} %param.3) | copy-start | bytes 100
  1.7 26.1 %collective-permute-start = (bf16[2,2,2,256,256]{4,3,2,1,0:T(8,128)(2,1)S(1)}, bf16[2,2,2,256,256]{4,3,2,1,0:T(8,128)(2,1)S(1)}, u32[]{:S(2)}, u32[]{:S(2)}) collective-permute-start(bf16[2,2,2,256,256]{4,3,2,1,0:T(8,128)(2,1)S(1)} %get-tuple-element.111), channel_id=1, source_target_pairs={{0,4},{1,5},{2,6},{3,7},{4,0},{5,1},{6,2},{7,3},{8,12},{9,13},{10,... | collective-permute-start | bytes 3145736 | tf_op jit(solution)/shard_map/ppermute | solution.py:288
  3.2 1.6 %copy-start = (bf16[2,2,2,2,256,256]{5,4,3,2,1,0:T(8,128)(2,1)S(1)}, bf16[2,2,2,2,256,256]{5,4,3,2,1,0:T(8,128)(2,1)}, u32[]{:S(2)}) copy-start(bf16[2,2,2,2,256,256]{5,4,3,2,1,0:T(8,128)(2,1)} %green.1) | copy-start | bytes 6291460
  8.1 25.6 %collective-permute-start.2 = (bf16[20,32,768]{2,1,0:T(8,128)(2,1)S(1)}, bf16[20,32,768]{2,1,0:T(8,128)(2,1)S(1)}, u32[]{:S(2)}, u32[]{:S(2)}) collective-permute-start(bf16[20,32,768]{2,1,0:T(8,128)(2,1)S(1)} %get-tuple-element.60), channel_id=1, source_target_pairs={{0,1},{1,2},{2,3},{3,0},{4,5},{5,6},{6,7},{7,4},{8,9},{9,10},{10,1... | collective-permute-start | bytes 2949128 | tf_op jit(solution)/shard_map/ppermute | solution.py:291
  9.8 24.0 %collective-permute-start.3 = (bf16[20,32,768]{2,1,0:T(8,128)(2,1)S(1)}, bf16[20,32,768]{2,1,0:T(8,128)(2,1)S(1)}, u32[]{:S(2)}, u32[]{:S(2)}) collective-permute-start(bf16[20,32,768]{2,1,0:T(8,128)(2,1)S(1)} %get-tuple-element.61), channel_id=1, source_target_pairs={{0,3},{1,0},{2,1},{3,2},{4,7},{5,4},{6,5},{7,6},{8,11},{9,8},{10,9... | collective-permute-start | bytes 2949128 | tf_op jit(solution)/shard_map/ppermute | solution.py:291
  11.5 16.3 %collective-permute-start.1 = (bf16[2,2,256,256]{3,2,1,0:T(8,128)(2,1)S(1)}, bf16[2,2,256,256]{3,2,1,0:T(8,128)(2,1)S(1)}, u32[]{:S(2)}, u32[]{:S(2)}) collective-permute-start(bf16[2,2,256,256]{3,2,1,0:T(8,128)(2,1)S(1)} %slice_bitcast_fusion.2), channel_id=1, source_target_pairs={{8,0},{16,8},{24,16},{32,24},{40,32},{48,40},{56,48},{72,64},{80,7... | collective-permute-start | bytes 1572872 | tf_op jit(solution)/shard_map/ppermute | solution.py:299
  27.9 19.1 %collective-permute-start.4 = (bf16[2,2,256,256]{3,2,1,0:T(8,128)(2,1)S(1)}, bf16[2,2,256,256]{3,2,1,0:T(8,128)(2,1)S(1)}, u32[]{:S(2)}, u32[]{:S(2)}) collective-permute-start(bf16[2,2,256,256]{3,2,1,0:T(8,128)(2,1)S(1)} %get-tuple-element.65), channel_id=1, source_target_pairs={{8,0},{16,8},{24,16},{32,24},{40,32},{48,40},{56,48},{72,64},{80,7... | collective-permute-start | bytes 1572872 | tf_op jit(solution)/shard_map/ppermute | solution.py:299
  29.9 24.5 %collective-permute-start.6 = (bf16[2,2,256,256]{3,2,1,0:T(8,128)(2,1)S(1)}, bf16[2,2,256,256]{3,2,1,0:T(8,128)(2,1)S(1)}, u32[]{:S(2)}, u32[]{:S(2)}) collective-permute-start(bf16[2,2,256,256]{3,2,1,0:T(8,128)(2,1)S(1)} %get-tuple-element.68), channel_id=1, source_target_pairs={{72,0},{80,8},{88,16},{96,24},{104,32},{112,40},{120,48},{136,64},... | collective-permute-start | bytes 1572872 | tf_op jit(solution)/shard_map/ppermute | solution.py:299
  31.8 15.2 %collective-permute-start.5 = (bf16[2,2,2,256,256]{4,3,2,1,0:T(8,128)(2,1)S(1)}, bf16[2,2,2,256,256]{4,3,2,1,0:T(8,128)(2,1)S(1)}, u32[]{:S(2)}, u32[]{:S(2)}) collective-permute-start(bf16[2,2,2,256,256]{4,3,2,1,0:T(8,128)(2,1)S(1)} %get-tuple-element.66), channel_id=1, source_target_pairs={{64,0},{72,8},{80,16},{88,24},{96,32},{104,40},{112,48},{120,56},{... | collective-permute-start | bytes 3145736 | tf_op jit(solution)/shard_map/ppermute | solution.py:299
  35.1 22.7 %collective-permute-start.7 = (bf16[10,32,768]{2,1,0:T(8,128)(2,1)S(1)}, bf16[10,32,768]{2,1,0:T(8,128)(2,1)S(1)}, u32[]{:S(2)}, u32[]{:S(2)}) collective-permute-start(bf16[10,32,768]{2,1,0:T(8,128)(2,1)S(1)} %get-tuple-element.70), channel_id=1, source_target_pairs={{0,3},{1,0},{2,1},{3,2},{4,7},{5,4},{6,5},{7,6},{8,11},{9,8},{10,9... | collective-permute-start | bytes 1474568 | tf_op jit(solution)/shard_map/ppermute | solution.py:291
  37.5 20.3 %collective-permute-start.8 = (bf16[10,32,768]{2,1,0:T(8,128)(2,1)S(1)}, bf16[10,32,768]{2,1,0:T(8,128)(2,1)S(1)}, u32[]{:S(2)}, u32[]{:S(2)}) collective-permute-start(bf16[10,32,768]{2,1,0:T(8,128)(2,1)S(1)} %get-tuple-element.72), channel_id=1, source_target_pairs={{0,1},{1,2},{2,3},{3,0},{4,5},{5,6},{6,7},{7,4},{8,9},{9,10},{10,1... | collective-permute-start | bytes 1474568 | tf_op jit(solution)/shard_map/ppermute | solution.py:291
  50.9 17.7 %collective-permute-start.9 = (bf16[12,32,768]{2,1,0:T(8,128)(2,1)S(1)}, bf16[12,32,768]{2,1,0:T(8,128)(2,1)S(1)}, u32[]{:S(2)}, u32[]{:S(2)}) collective-permute-start(bf16[12,32,768]{2,1,0:T(8,128)(2,1)S(1)} %get-tuple-element.74), channel_id=1, source_target_pairs={{0,1},{1,2},{2,3},{3,0},{4,5},{5,6},{6,7},{7,4},{8,9},{9,10},{10,1... | collective-permute-start | bytes 1769480 | tf_op jit(solution)/shard_map/ppermute | solution.py:291
  52.4 16.2 %collective-permute-start.10 = (bf16[12,32,768]{2,1,0:T(8,128)(2,1)S(1)}, bf16[12,32,768]{2,1,0:T(8,128)(2,1)S(1)}, u32[]{:S(2)}, u32[]{:S(2)}) collective-permute-start(bf16[12,32,768]{2,1,0:T(8,128)(2,1)S(1)} %get-tuple-element.75), channel_id=1, source_target_pairs={{0,3},{1,0},{2,1},{3,2},{4,7},{5,4},{6,5},{7,6},{8,11},{9,8},{10,9... | collective-permute-start | bytes 1769480 | tf_op jit(solution)/shard_map/ppermute | solution.py:291
  58.8 9.5 %collective-permute-start.11 = (bf16[10,32,768]{2,1,0:T(8,128)(2,1)S(1)}, bf16[10,32,768]{2,1,0:T(8,128)(2,1)S(1)}, u32[]{:S(2)}, u32[]{:S(2)}) collective-permute-start(bf16[10,32,768]{2,1,0:T(8,128)(2,1)S(1)} %get-tuple-element.78), channel_id=1, source_target_pairs={{0,4},{1,5},{2,6},{3,7},{4,0},{5,1},{6,2},{7,3},{8,12},{9,13},{10,... | collective-permute-start | bytes 1474568 | tf_op jit(solution)/shard_map/ppermute | solution.py:288
  61.4 17.7 %collective-permute-start.12 = (bf16[10,32,768]{2,1,0:T(8,128)(2,1)S(1)}, bf16[10,32,768]{2,1,0:T(8,128)(2,1)S(1)}, u32[]{:S(2)}, u32[]{:S(2)}) collective-permute-start(bf16[10,32,768]{2,1,0:T(8,128)(2,1)S(1)} %get-tuple-element.80), channel_id=1, source_target_pairs={{0,1},{1,2},{2,3},{3,0},{4,5},{5,6},{6,7},{7,4},{8,9},{9,10},{10,1... | collective-permute-start | bytes 1474568 | tf_op jit(solution)/shard_map/ppermute | solution.py:291
  61.9 17.2 %collective-permute-start.13 = (bf16[10,32,768]{2,1,0:T(8,128)(2,1)S(1)}, bf16[10,32,768]{2,1,0:T(8,128)(2,1)S(1)}, u32[]{:S(2)}, u32[]{:S(2)}) collective-permute-start(bf16[10,32,768]{2,1,0:T(8,128)(2,1)S(1)} %get-tuple-element.81), channel_id=1, source_target_pairs={{0,3},{1,0},{2,1},{3,2},{4,7},{5,4},{6,5},{7,6},{8,11},{9,8},{10,9... | collective-permute-start | bytes 1474568 | tf_op jit(solution)/shard_map/ppermute | solution.py:291
  69.4 12.5 %collective-permute-start.14 = (bf16[6,32,768]{2,1,0:T(8,128)(2,1)S(1)}, bf16[6,32,768]{2,1,0:T(8,128)(2,1)S(1)}, u32[]{:S(2)}, u32[]{:S(2)}) collective-permute-start(bf16[6,32,768]{2,1,0:T(8,128)(2,1)S(1)} %get-tuple-element.85), channel_id=1, source_target_pairs={{0,3},{1,0},{2,1},{3,2},{4,7},{5,4},{6,5},{7,6},{8,11},{9,8},{10,9... | collective-permute-start | bytes 884744 | tf_op jit(solution)/shard_map/ppermute | solution.py:291
  71.1 12.8 %collective-permute-start.15 = (bf16[6,32,768]{2,1,0:T(8,128)(2,1)S(1)}, bf16[6,32,768]{2,1,0:T(8,128)(2,1)S(1)}, u32[]{:S(2)}, u32[]{:S(2)}) collective-permute-start(bf16[6,32,768]{2,1,0:T(8,128)(2,1)S(1)} %get-tuple-element.87), channel_id=1, source_target_pairs={{0,1},{1,2},{2,3},{3,0},{4,5},{5,6},{6,7},{7,4},{8,9},{9,10},{10,1... | collective-permute-start | bytes 884744 | tf_op jit(solution)/shard_map/ppermute | solution.py:291
  79.8 6.8 %collective-permute-start.16 = (bf16[5,32,768]{2,1,0:T(8,128)(2,1)S(1)}, bf16[5,32,768]{2,1,0:T(8,128)(2,1)S(1)}, u32[]{:S(2)}, u32[]{:S(2)}) collective-permute-start(bf16[5,32,768]{2,1,0:T(8,128)(2,1)S(1)} %get-tuple-element.89), channel_id=1, source_target_pairs={{0,3},{1,0},{2,1},{3,2},{4,7},{5,4},{6,5},{7,6},{8,11},{9,8},{10,9... | collective-permute-start | bytes 737288 | tf_op jit(solution)/shard_map/ppermute | solution.py:291
  81.2 7.4 %collective-permute-start.17 = (bf16[5,32,768]{2,1,0:T(8,128)(2,1)S(1)}, bf16[5,32,768]{2,1,0:T(8,128)(2,1)S(1)}, u32[]{:S(2)}, u32[]{:S(2)}) collective-permute-start(bf16[5,32,768]{2,1,0:T(8,128)(2,1)S(1)} %get-tuple-element.91), channel_id=1, source_target_pairs={{0,1},{1,2},{2,3},{3,0},{4,5},{5,6},{6,7},{7,4},{8,9},{9,10},{10,1... | collective-permute-start | bytes 737288 | tf_op jit(solution)/shard_map/ppermute | solution.py:291
  84.5 15.5 %collective-permute-start.19 = (bf16[4,32,768]{2,1,0:T(8,128)(2,1)S(1)}, bf16[4,32,768]{2,1,0:T(8,128)(2,1)S(1)}, u32[]{:S(2)}, u32[]{:S(2)}) collective-permute-start(bf16[4,32,768]{2,1,0:T(8,128)(2,1)S(1)} %get-tuple-element.104), channel_id=1, source_target_pairs={{0,4},{1,5},{2,6},{3,7},{4,0},{5,1},{6,2},{7,3},{8,12},{9,13},{10,... | collective-permute-start | bytes 589832 | tf_op jit(solution)/shard_map/ppermute | solution.py:288
  85.8 7.7 %collective-permute-start.18 = (bf16[2,32,768]{2,1,0:T(8,128)(2,1)S(1)}, bf16[2,32,768]{2,1,0:T(8,128)(2,1)S(1)}, u32[]{:S(2)}, u32[]{:S(2)}) collective-permute-start(bf16[2,32,768]{2,1,0:T(8,128)(2,1)S(1)} %get-tuple-element.96), channel_id=1, source_target_pairs={{0,4},{1,5},{2,6},{3,7},{4,0},{5,1},{6,2},{7,3},{8,12},{9,13},{10,... | collective-permute-start | bytes 294920 | tf_op jit(solution)/shard_map/ppermute | solution.py:288
  89.1 11.0 %collective-permute-start.20 = (bf16[5,32,768]{2,1,0:T(8,128)(2,1)S(1)}, bf16[5,32,768]{2,1,0:T(8,128)(2,1)S(1)}, u32[]{:S(2)}, u32[]{:S(2)}) collective-permute-start(bf16[5,32,768]{2,1,0:T(8,128)(2,1)S(1)} %get-tuple-element.107), channel_id=1, source_target_pairs={{0,4},{1,5},{2,6},{3,7},{4,0},{5,1},{6,2},{7,3},{8,12},{9,13},{10,... | collective-permute-start | bytes 737288 | tf_op jit(solution)/shard_map/ppermute | solution.py:288
  93.6 8.3 %collective-permute-start.21 = (bf16[4,32,768]{2,1,0:T(8,128)(2,1)S(1)}, bf16[4,32,768]{2,1,0:T(8,128)(2,1)S(1)}, u32[]{:S(2)}, u32[]{:S(2)}) collective-permute-start(bf16[4,32,768]{2,1,0:T(8,128)(2,1)S(1)} %get-tuple-element.109), channel_id=1, source_target_pairs={{0,8},{8,16},{16,24},{24,32},{32,40},{40,48},{48,56},{64,72},{72,8... | collective-permute-start | bytes 589832 | tf_op jit(solution)/shard_map/ppermute | solution.py:299

commit v7 on v6

--- a/solution.py
+++ b/solution.py
@@ -13,8 +13,8 @@
 MIB = 1024 * 1024
 EARLY = ((0, 0, UP), (0, 0, LOOSE0), (0, 0, LOOSE1), (0, 1, DOWN), (1, 0, LOOSE0))
 GIVEN = 2
-FIRST = ((0, 2, DOWN), (1, 2, DOWN), (0, 1, LOOSE0), (0, 1, LOOSE1), (0, 1, UP), (1, 1, LOOSE0))
-LAST = ((1, 0, LOOSE1), (1, 0, UP), (1, 1, LOOSE1), (1, 1, DOWN), (1, 1, UP))
+FIRST = ((0, 2, DOWN), (1, 2, DOWN), (0, 1, LOOSE0), (0, 1, LOOSE1), (0, 1, UP), (1, 1, LOOSE0), (1, 0, UP))
+LAST = ((1, 0, LOOSE1), (1, 1, LOOSE1), (1, 1, DOWN), (1, 1, UP))
 
 WAITING = 100_000_000_000
 OWN = ((0, 0), (0, 1), (1, 0), (1, 1))
@@ -344,7 +344,7 @@
     above_theirs = tiles_from(above, 0, 1)
     beside = tiles_from(beside, 1, 0)
     corner = tiles_from(corner, 1, 1)
-    early_second, token = second(early, early_first, token, size=WAITING)
+    early_second, token = second(early, early_first, token, size=8_000_000_000)
     tiles = [(OWN, mine.reshape(4, *shape)), (OWN, theirs.reshape(4, *shape)), (ABOVE, above_mine), (ABOVE, above_theirs)]
     tiles += [(BESIDE, beside[0]), (BESIDE, beside[1])]
     (one,), token = blocks((FIRST,), tiles, token, "first_blocks")

time: 106 us -> 110 us (1.038); the launches traced: 104 us -> 109 us
  waiting for transfers between devices: 40.9 us -> 51.8 us
  starting transfers between devices: 39.7 us -> 34 us
    ppermute x5, waiting for transfers between devices: 25.4 us -> 30.7 us  [tiles_from(): return lax.ppermute(value, ('gx', 'gy'), perm)]
    ppermute x5, starting transfers between devices: 10.1 us -> 5.6 us  [swap(): lax.ppermute(value, 'sa', [(i, (i + RING) % (2 * RING)) for i in range(2...]
    ppermute x12, waiting for transfers between devices: 11.9 us -> 15.1 us  [around(): lax.ppermute(value, 'sa', [(h * RING + i, h * RING + (i + steps) % RING)...]
    ppermute x5, waiting for transfers between devices: 3.58 us -> 5.97 us  [swap(): lax.ppermute(value, 'sa', [(i, (i + RING) % (2 * RING)) for i in range(2...]
    ppermute x5, starting transfers between devices: 12.9 us -> 10.6 us  [tiles_from(): return lax.ppermute(value, ('gx', 'gy'), perm)]
    ppermute x12, starting transfers between devices: 16.6 us -> 17.8 us  [around(): lax.ppermute(value, 'sa', [(h * RING + i, h * RING + (i + steps) % RING)...]
  transfers between devices with their start and end apart: 22 -> 22, of which waited for: 8 -> 11; matrix products, arithmetic and copies ran while one was open for 0% -> 0% of each run, Pallas kernels for 17% -> 15%
where the time goes in v7:
time: 110 us; the launch traced here: 109 us
  waiting for transfers between devices  51.8 us (47%)
  starting transfers between devices  34 us (31%)
  Pallas kernels  19.7 us (18%)
  local copies, waits for them, and re-layouts  3.59 us (3%)
    ppermute x5, waiting for transfers between devices, tiles_from(): return lax.ppermute(value, ('gx', 'gy'), perm)  30.7 us
    ppermute x12, starting transfers between devices, around(): lax.ppermute(value, 'sa', [(h * RING + i, h * RING + (i + steps) % RING)...  17.8 us
    ppermute x12, waiting for transfers between devices, around(): lax.ppermute(value, 'sa', [(h * RING + i, h * RING + (i + steps) % RING)...  15.1 us
    ppermute x5, starting transfers between devices, tiles_from(): return lax.ppermute(value, ('gx', 'gy'), perm)  10.6 us
    pallas_call x3, Pallas kernels, call_blocks(): pl.pallas_call(kernel, out_shape=out_shape + [jax.ShapeDtypeStruct(token....  10.5 us
    pallas_call x13, Pallas kernels, call_step(): pl.pallas_call(kernel, out_shape=list(out_shape) + [jax.ShapeDtypeStruct(...  6.96 us
    ppermute x5, waiting for transfers between devices, swap(): lax.ppermute(value, 'sa', [(i, (i + RING) % (2 * RING)) for i in range(2...  5.97 us
    ppermute x5, starting transfers between devices, swap(): lax.ppermute(value, 'sa', [(i, (i + RING) % (2 * RING)) for i in range(2...  5.6 us
  transfers between devices with their start and end apart: 22, of which 11 were waited for; matrix products, arithmetic and copies ran while one was open for 0% of the time, Pallas kernels for 15%

profile of v7, /device:TPU:100, one launch (start us, length us, event | category | flops | bytes accessed | tf_op | source)
XLA Modules:
  0.0 109.4 jit_solution(5278178446634642050)
XLA Ops:
  0.0 1.7 %dynamic-slice_bitcast_fusion = (bf16[2,2,2,256,256]{4,3,2,1,0:T(8,128)(2,1)S(1)}, bf16[2,2,1,2,256,256]{5,4,3,2,1,0:T(8,128)(2,1)S(1)}) fusion(bf16[2,2,2,2,256,256]{5,4,3,2,1,0:T(8,128)(2,1)} %green.1, s32[]{:T(128)S(6)} %select_n.21, s32[]{:T(128)S(6)} %select_n.20), kind=kLoop, calls=%fused_computation.1 | loop fusion | bytes 4194312 | tf_op jit(solution)/shard_map/jit(dynamic_index_in_dim)/squeeze | solution.py:331
  1.7 1.3 %collective-permute-start = (bf16[2,2,2,256,256]{4,3,2,1,0:T(8,128)(2,1)S(1)}, bf16[2,2,2,256,256]{4,3,2,1,0:T(8,128)(2,1)S(1)}, u32[]{:S(2)}, u32[]{:S(2)}) collective-permute-start(bf16[2,2,2,256,256]{4,3,2,1,0:T(8,128)(2,1)S(1)} %get-tuple-element.111), channel_id=1, source_target_pairs={{0,4},{1,5},{2,6},{3,7},{4,0},{5,1},{6,2},{7,3},{8,12},{9,13},{10,... | collective-permute-start | bytes 3145736 | tf_op jit(solution)/shard_map/ppermute | solution.py:288
  3.0 0.1 copy.8.offsets.refs_1_
  3.1 0.1 pad_add_fusion.meta.refs_0_
  3.2 1.6 %copy-done = bf16[2,2,2,2,256,256]{5,4,3,2,1,0:T(8,128)(2,1)S(1)} copy-done((bf16[2,2,2,2,256,256]{5,4,3,2,1,0:T(8,128)(2,1)S(1)}, bf16[2,2,2,2,256,256]{5,4,3,2,1,0:T(8,128)(2,1)}, u32[]{:S(2)}) %copy-start) | copy-done | bytes 2097176
  4.7 3.3 %early_blocks.1 = (f32[10,32,512]{2,1,0:T(8,128)S(1)}, f32[10,32,512]{2,1,0:T(8,128)S(1)}, bf16[20,32,768]{2,1,0:T(8,128)(2,1)S(1)}, bf16[20,32,768]{2,1,0:T(8,1...) custom-call(s32[2]{0:T(128)S(1)} %pad_add_fusion.meta.refs_0_, ...), custom_call_target="tpu_custom_call" | custom-call | tf_op jit(solution)/shard_map/early_blocks/pallas_call | solution.py:167
  8.1 1.7 %collective-permute-start.2 = (bf16[20,32,768]{2,1,0:T(8,128)(2,1)S(1)}, bf16[20,32,768]{2,1,0:T(8,128)(2,1)S(1)}, u32[]{:S(2)}, u32[]{:S(2)}) collective-permute-start(bf16[20,32,768]{2,1,0:T(8,128)(2,1)S(1)} %get-tuple-element.60), channel_id=1, source_target_pairs={{0,1},{1,2},{2,3},{3,0},{4,5},{5,6},{6,7},{7,4},{8,9},{9,10},{10,1... | collective-permute-start | bytes 2949128 | tf_op jit(solution)/shard_map/ppermute | solution.py:291
  9.8 1.7 %collective-permute-start.3 = (bf16[20,32,768]{2,1,0:T(8,128)(2,1)S(1)}, bf16[20,32,768]{2,1,0:T(8,128)(2,1)S(1)}, u32[]{:S(2)}, u32[]{:S(2)}) collective-permute-start(bf16[20,32,768]{2,1,0:T(8,128)(2,1)S(1)} %get-tuple-element.61), channel_id=1, source_target_pairs={{0,3},{1,0},{2,1},{3,2},{4,7},{5,4},{6,5},{7,6},{8,11},{9,8},{10,9... | collective-permute-start | bytes 2949128 | tf_op jit(solution)/shard_map/ppermute | solution.py:291
  11.4 0.1 copy.11
  11.5 2.0 %collective-permute-start.1 = (bf16[2,2,256,256]{3,2,1,0:T(8,128)(2,1)S(1)}, bf16[2,2,256,256]{3,2,1,0:T(8,128)(2,1)S(1)}, u32[]{:S(2)}, u32[]{:S(2)}) collective-permute-start(bf16[2,2,256,256]{3,2,1,0:T(8,128)(2,1)S(1)} %slice_bitcast_fusion.2), channel_id=1, source_target_pairs={{8,0},{16,8},{24,16},{32,24},{40,32},{48,40},{56,48},{72,64},{80,7... | collective-permute-start | bytes 1572872 | tf_op jit(solution)/shard_map/ppermute | solution.py:299
  13.6 14.2 %collective-permute-done.1.above_mine.refs_5_ = bf16[2,2,256,256]{3,2,1,0:T(8,128)(2,1)S(1)} collective-permute-done((bf16[2,2,256,256]{3,2,1,0:T(8,128)(2,1)S(1)}, bf16[2,2,256,256]{3,2,1,0:T(8,128)(2,1)S(1)}, u32[]{:S(2)}, u32[]{:S(2)}) %collective-permute-start.1) | collective-permute-done | bytes 524320 | tf_op jit(solution)/shard_map/ppermute | solution.py:299
  27.8 0.0 collective-permute-done.theirs
  27.8 0.1 swapped.1
  27.9 1.9 %collective-permute-start.5 = (bf16[2,2,2,256,256]{4,3,2,1,0:T(8,128)(2,1)S(1)}, bf16[2,2,2,256,256]{4,3,2,1,0:T(8,128)(2,1)S(1)}, u32[]{:S(2)}, u32[]{:S(2)}) collective-permute-start(bf16[2,2,2,256,256]{4,3,2,1,0:T(8,128)(2,1)S(1)} %get-tuple-element.66), channel_id=1, source_target_pairs={{64,0},{72,8},{80,16},{88,24},{96,32},{104,40},{112,48},{120,56},{... | collective-permute-start | bytes 3145736 | tf_op jit(solution)/shard_map/ppermute | solution.py:299
  29.9 1.9 %collective-permute-start.4 = (bf16[2,2,256,256]{3,2,1,0:T(8,128)(2,1)S(1)}, bf16[2,2,256,256]{3,2,1,0:T(8,128)(2,1)S(1)}, u32[]{:S(2)}, u32[]{:S(2)}) collective-permute-start(bf16[2,2,256,256]{3,2,1,0:T(8,128)(2,1)S(1)} %get-tuple-element.65), channel_id=1, source_target_pairs={{8,0},{16,8},{24,16},{32,24},{40,32},{48,40},{56,48},{72,64},{80,7... | collective-permute-start | bytes 1572872 | tf_op jit(solution)/shard_map/ppermute | solution.py:299
  31.8 1.9 %collective-permute-start.6 = (bf16[2,2,256,256]{3,2,1,0:T(8,128)(2,1)S(1)}, bf16[2,2,256,256]{3,2,1,0:T(8,128)(2,1)S(1)}, u32[]{:S(2)}, u32[]{:S(2)}) collective-permute-start(bf16[2,2,256,256]{3,2,1,0:T(8,128)(2,1)S(1)} %get-tuple-element.68), channel_id=1, source_target_pairs={{72,0},{80,8},{88,16},{96,24},{104,32},{112,40},{120,48},{136,64},... | collective-permute-start | bytes 1572872 | tf_op jit(solution)/shard_map/ppermute | solution.py:299
  33.7 0.0 collective-permute-done.2.up_received
  33.7 0.0 collective-permute-done.3.down_received.after
  33.7 1.3 %second.3 = (bf16[10,32,768]{2,1,0:T(8,128)(2,1)S(1)}, bf16[10,32,768]{2,1,0:T(8,128)(2,1)S(1)}, f32[8,128]{1,0:T(8,128)S(1)}) custom-call(f32[8,128]{1,0:T(8,128)S(1)} %get-tuple-element.59.token, bf16[20,32,768]{2,1,0:T(8,128)(2,1)S(1)} %collective-permute-done.2.up_received, bf16[20,32,768]{2,1,0:T(8,128)(2,1)S(1)} %collective-permute-done.3.down_received.after, ...), custom_call_target="tpu_custom_call" | custom-call | flops 8000000000 | tf_op jit(solution)/shard_map/second/pallas_call | solution.py:186
  35.1 2.1 %collective-permute-start.7 = (bf16[10,32,768]{2,1,0:T(8,128)(2,1)S(1)}, bf16[10,32,768]{2,1,0:T(8,128)(2,1)S(1)}, u32[]{:S(2)}, u32[]{:S(2)}) collective-permute-start(bf16[10,32,768]{2,1,0:T(8,128)(2,1)S(1)} %get-tuple-element.70), channel_id=1, source_target_pairs={{0,3},{1,0},{2,1},{3,2},{4,7},{5,4},{6,5},{7,6},{8,11},{9,8},{10,9... | collective-permute-start | bytes 1474568 | tf_op jit(solution)/shard_map/ppermute | solution.py:291
  37.2 0.0 collective-permute-start.8
  37.2 5.0 %collective-permute-done.5 = bf16[2,2,2,256,256]{4,3,2,1,0:T(8,128)(2,1)S(1)} collective-permute-done((bf16[2,2,2,256,256]{4,3,2,1,0:T(8,128)(2,1)S(1)}, bf16[2,2,2,256,256]{4,3,2,1,0:T(8,128)(2,1)S(1)}, u32[]{:S(2)}, u32[]{:S(2)}) %collective-permute-start.5) | collective-permute-done | bytes 1048608 | tf_op jit(solution)/shard_map/ppermute | solution.py:299
  42.2 0.1 slice_bitcast_fusion
  42.2 5.4 %collective-permute-done.4.refs_6_ = bf16[2,2,256,256]{3,2,1,0:T(8,128)(2,1)S(1)} collective-permute-done((bf16[2,2,256,256]{3,2,1,0:T(8,128)(2,1)S(1)}, bf16[2,2,256,256]{3,2,1,0:T(8,128)(2,1)S(1)}, u32[]{:S(2)}, u32[]{:S(2)}) %collective-permute-start.4) | collective-permute-done | bytes 524320 | tf_op jit(solution)/shard_map/ppermute | solution.py:299
  47.7 4.2 %first_blocks.1 = (f32[7,32,512]{2,1,0:T(8,128)S(1)}, f32[7,32,512]{2,1,0:T(8,128)S(1)}, bf16[14,32,768]{2,1,0:T(8,128)(2,1)S(1)}, bf16[14,32,768]{2,1,0:T(8,128...) custom-call(s32[2]{0:T(128)S(1)} %pad_add_fusion.meta.refs_0_, ...), custom_call_target="tpu_custom_call" | custom-call | tf_op jit(solution)/shard_map/first_blocks/pallas_call | solution.py:167
  51.9 0.8 collective-permute-start.9
  52.7 2.7 %collective-permute-start.10 = (bf16[14,32,768]{2,1,0:T(8,128)(2,1)S(1)}, bf16[14,32,768]{2,1,0:T(8,128)(2,1)S(1)}, u32[]{:S(2)}, u32[]{:S(2)}) collective-permute-start(bf16[14,32,768]{2,1,0:T(8,128)(2,1)S(1)} %get-tuple-element.75), channel_id=1, source_target_pairs={{0,3},{1,0},{2,1},{3,2},{4,7},{5,4},{6,5},{7,6},{8,11},{9,8},{10,9... | collective-permute-start | bytes 2064392 | tf_op jit(solution)/shard_map/ppermute | solution.py:291
  55.4 2.9 %collective-permute-done.6 = bf16[2,2,256,256]{3,2,1,0:T(8,128)(2,1)S(1)} collective-permute-done((bf16[2,2,256,256]{3,2,1,0:T(8,128)(2,1)S(1)}, bf16[2,2,256,256]{3,2,1,0:T(8,128)(2,1)S(1)}, u32[]{:S(2)}, u32[]{:S(2)}) %collective-permute-start.6) | collective-permute-done | bytes 524320 | tf_op jit(solution)/shard_map/ppermute | solution.py:299
  58.3 3.0 %last_blocks.1 = (f32[4,32,512]{2,1,0:T(8,128)S(1)}, f32[4,32,512]{2,1,0:T(8,128)S(1)}, bf16[8,32,768]{2,1,0:T(8,128)(2,1)S(1)}, bf16[8,32,768]{2,1,0:T(8,128)(2...) custom-call(s32[2]{0:T(128)S(1)} %pad_add_fusion.meta.refs_0_, ...), custom_call_target="tpu_custom_call" | custom-call | tf_op jit(solution)/shard_map/last_blocks/pallas_call | solution.py:167
  61.3 0.0 collective-permute-done.7.down_arrived
  61.3 0.0 collective-permute-done.8.refs_0_.before
  61.3 1.0 back.3
  62.3 0.9 collective-permute-start.11
  63.2 1.1 %collective-permute-start.12 = (bf16[8,32,768]{2,1,0:T(8,128)(2,1)S(1)}, bf16[8,32,768]{2,1,0:T(8,128)(2,1)S(1)}, u32[]{:S(2)}, u32[]{:S(2)}) collective-permute-start(bf16[8,32,768]{2,1,0:T(8,128)(2,1)S(1)} %get-tuple-element.80), channel_id=1, source_target_pairs={{0,1},{1,2},{2,3},{3,0},{4,5},{5,6},{6,7},{7,4},{8,9},{9,10},{10,1... | collective-permute-start | bytes 1179656 | tf_op jit(solution)/shard_map/ppermute | solution.py:291
  64.3 2.1 %collective-permute-start.13 = (bf16[8,32,768]{2,1,0:T(8,128)(2,1)S(1)}, bf16[8,32,768]{2,1,0:T(8,128)(2,1)S(1)}, u32[]{:S(2)}, u32[]{:S(2)}) collective-permute-start(bf16[8,32,768]{2,1,0:T(8,128)(2,1)S(1)} %get-tuple-element.81), channel_id=1, source_target_pairs={{0,3},{1,0},{2,1},{3,2},{4,7},{5,4},{6,5},{7,6},{8,11},{9,8},{10,9... | collective-permute-start | bytes 1179656 | tf_op jit(solution)/shard_map/ppermute | solution.py:291
  66.5 6.0 %collective-permute-done.11.refs_0_ = bf16[10,32,768]{2,1,0:T(8,128)(2,1)S(1)} collective-permute-done((bf16[10,32,768]{2,1,0:T(8,128)(2,1)S(1)}, bf16[10,32,768]{2,1,0:T(8,128)(2,1)S(1)}, u32[]{:S(2)}, u32[]{:S(2)}) %collective-permute-start.11) | collective-permute-done | bytes 491552 | tf_op jit(solution)/shard_map/ppermute | solution.py:288
  72.4 0.0 collective-permute-done.9.up_received
  72.4 0.9 second.4
  73.4 2.7 %collective-permute-start.14 = (bf16[7,32,768]{2,1,0:T(8,128)(2,1)S(1)}, bf16[7,32,768]{2,1,0:T(8,128)(2,1)S(1)}, u32[]{:S(2)}, u32[]{:S(2)}) collective-permute-start(bf16[7,32,768]{2,1,0:T(8,128)(2,1)S(1)} %get-tuple-element.85), channel_id=1, source_target_pairs={{0,3},{1,0},{2,1},{3,2},{4,7},{5,4},{6,5},{7,6},{8,11},{9,8},{10,9... | collective-permute-start | bytes 1032200 | tf_op jit(solution)/shard_map/ppermute | solution.py:291
  76.0 4.2 %collective-permute-done.12.up_received = bf16[8,32,768]{2,1,0:T(8,128)(2,1)S(1)} collective-permute-done((bf16[8,32,768]{2,1,0:T(8,128)(2,1)S(1)}, bf16[8,32,768]{2,1,0:T(8,128)(2,1)S(1)}, u32[]{:S(2)}, u32[]{:S(2)}) %collective-permute-start.12) | collective-permute-done | bytes 393248 | tf_op jit(solution)/shard_map/ppermute | solution.py:291
  80.2 0.0 collective-permute-done.13.down_received.after
  80.2 0.5 second.5
  80.7 4.5 %collective-permute-done.14.down_arrived = bf16[7,32,768]{2,1,0:T(8,128)(2,1)S(1)} collective-permute-done((bf16[7,32,768]{2,1,0:T(8,128)(2,1)S(1)}, bf16[7,32,768]{2,1,0:T(8,128)(2,1)S(1)}, u32[]{:S(2)}, u32[]{:S(2)}) %collective-permute-start.14) | collective-permute-done | bytes 344096 | tf_op jit(solution)/shard_map/ppermute | solution.py:291
  85.2 0.7 collective-permute-done.15.refs_0_.before
  86.0 0.7 back.4
  86.7 0.9 collective-permute-start.19
  87.6 3.0 %collective-permute-start.16 = (bf16[4,32,768]{2,1,0:T(8,128)(2,1)S(1)}, bf16[4,32,768]{2,1,0:T(8,128)(2,1)S(1)}, u32[]{:S(2)}, u32[]{:S(2)}) collective-permute-start(bf16[4,32,768]{2,1,0:T(8,128)(2,1)S(1)} %get-tuple-element.89), channel_id=1, source_target_pairs={{0,3},{1,0},{2,1},{3,2},{4,7},{5,4},{6,5},{7,6},{8,11},{9,8},{10,9... | collective-permute-start | bytes 589832 | tf_op jit(solution)/shard_map/ppermute | solution.py:291
  90.6 0.0 collective-permute-start.17
  90.6 1.2 %collective-permute-start.18 = (bf16[2,32,768]{2,1,0:T(8,128)(2,1)S(1)}, bf16[2,32,768]{2,1,0:T(8,128)(2,1)S(1)}, u32[]{:S(2)}, u32[]{:S(2)}) collective-permute-start(bf16[2,32,768]{2,1,0:T(8,128)(2,1)S(1)} %get-tuple-element.96), channel_id=1, source_target_pairs={{0,4},{1,5},{2,6},{3,7},{4,0},{5,1},{6,2},{7,3},{8,12},{9,13},{10,... | collective-permute-start | bytes 294920 | tf_op jit(solution)/shard_map/ppermute | solution.py:288
  91.7 2.0 %collective-permute-done.16.down_arrived = bf16[4,32,768]{2,1,0:T(8,128)(2,1)S(1)} collective-permute-done((bf16[4,32,768]{2,1,0:T(8,128)(2,1)S(1)}, bf16[4,32,768]{2,1,0:T(8,128)(2,1)S(1)}, u32[]{:S(2)}, u32[]{:S(2)}) %collective-permute-start.16) | collective-permute-done | bytes 196640 | tf_op jit(solution)/shard_map/ppermute | solution.py:291
  93.7 3.7 %collective-permute-done.17.refs_0_.before = bf16[4,32,768]{2,1,0:T(8,128)(2,1)S(1)} collective-permute-done((bf16[4,32,768]{2,1,0:T(8,128)(2,1)S(1)}, bf16[4,32,768]{2,1,0:T(8,128)(2,1)S(1)}, u32[]{:S(2)}, u32[]{:S(2)}) %collective-permute-start.17) | collective-permute-done | bytes 196640 | tf_op jit(solution)/shard_map/ppermute | solution.py:291
  97.4 0.4 back.5
  97.8 1.3 %collective-permute-start.20 = (bf16[4,32,768]{2,1,0:T(8,128)(2,1)S(1)}, bf16[4,32,768]{2,1,0:T(8,128)(2,1)S(1)}, u32[]{:S(2)}, u32[]{:S(2)}) collective-permute-start(bf16[4,32,768]{2,1,0:T(8,128)(2,1)S(1)} %get-tuple-element.107), channel_id=1, source_target_pairs={{0,4},{1,5},{2,6},{3,7},{4,0},{5,1},{6,2},{7,3},{8,12},{9,13},{10,... | collective-permute-start | bytes 589832 | tf_op jit(solution)/shard_map/ppermute | solution.py:288
  99.1 0.4 keep.3
  99.5 0.0 collective-permute-done.18.other
  99.6 0.1 give.1
  99.6 2.9 %collective-permute-start.21 = (bf16[4,32,768]{2,1,0:T(8,128)(2,1)S(1)}, bf16[4,32,768]{2,1,0:T(8,128)(2,1)S(1)}, u32[]{:S(2)}, u32[]{:S(2)}) collective-permute-start(bf16[4,32,768]{2,1,0:T(8,128)(2,1)S(1)} %get-tuple-element.109), channel_id=1, source_target_pairs={{0,8},{8,16},{16,24},{24,32},{32,40},{40,48},{48,56},{64,72},{72,8... | collective-permute-start | bytes 589832 | tf_op jit(solution)/shard_map/ppermute | solution.py:299
  102.5 0.9 keep.4
  103.4 0.3 keep.5
  103.7 0.0 collective-permute-done.19.sums
  103.7 0.2 read.2
  103.9 0.1 read.3
  104.0 3.2 %collective-permute-done.21.given = bf16[4,32,768]{2,1,0:T(8,128)(2,1)S(1)} collective-permute-done((bf16[4,32,768]{2,1,0:T(8,128)(2,1)S(1)}, bf16[4,32,768]{2,1,0:T(8,128)(2,1)S(1)}, u32[]{:S(2)}, u32[]{:S(2)}) %collective-permute-start.21) | collective-permute-done | bytes 196640 | tf_op jit(solution)/shard_map/ppermute | solution.py:299
  107.2 2.2 %place_blocks.1 = f32[2,2,4,2,32,512]{5,4,3,2,1,0:T(8,128)} custom-call(s32[2]{0:T(128)S(1)} %pad_add_fusion.meta.refs_0_, s32[4,2]{1,0:T(4,128)S(1)} %copy.8.offsets.refs_1_, f32[10,32,512]{2,1,0:T(8,128)S(1)} %get-tuple-element.99.early, f32[7,32,512]{2,1,0:T(8,128)S(1)} %get-tuple-element.95.kept.kept_one, f32[4,32,512]{2,1,0:T(8,128)S(1)} %get-tuple-element.102.kept_two, ...), custom_call_target="tpu_custom_call" | custom-call | tf_op jit(solution)/shard_map/place_blocks/pallas_call | solution.py:269
  (9 shorter events, 0.1 us)
Async XLA Ops:
  0.0 3.0 %copy-start.1 = (s32[4,2]{0,1:T(2,128)S(1)}, s32[4,2]{0,1:T(2,128)}, u32[]{:S(2)}) copy-start(s32[4,2]{0,1:T(2,128)} %param.3) | copy-start | bytes 100
  1.7 26.1 %collective-permute-start = (bf16[2,2,2,256,256]{4,3,2,1,0:T(8,128)(2,1)S(1)}, bf16[2,2,2,256,256]{4,3,2,1,0:T(8,128)(2,1)S(1)}, u32[]{:S(2)}, u32[]{:S(2)}) collective-permute-start(bf16[2,2,2,256,256]{4,3,2,1,0:T(8,128)(2,1)S(1)} %get-tuple-element.111), channel_id=1, source_target_pairs={{0,4},{1,5},{2,6},{3,7},{4,0},{5,1},{6,2},{7,3},{8,12},{9,13},{10,... | collective-permute-start | bytes 3145736 | tf_op jit(solution)/shard_map/ppermute | solution.py:288
  3.2 1.6 %copy-start = (bf16[2,2,2,2,256,256]{5,4,3,2,1,0:T(8,128)(2,1)S(1)}, bf16[2,2,2,2,256,256]{5,4,3,2,1,0:T(8,128)(2,1)}, u32[]{:S(2)}) copy-start(bf16[2,2,2,2,256,256]{5,4,3,2,1,0:T(8,128)(2,1)} %green.1) | copy-start | bytes 6291460
  8.1 25.6 %collective-permute-start.2 = (bf16[20,32,768]{2,1,0:T(8,128)(2,1)S(1)}, bf16[20,32,768]{2,1,0:T(8,128)(2,1)S(1)}, u32[]{:S(2)}, u32[]{:S(2)}) collective-permute-start(bf16[20,32,768]{2,1,0:T(8,128)(2,1)S(1)} %get-tuple-element.60), channel_id=1, source_target_pairs={{0,1},{1,2},{2,3},{3,0},{4,5},{5,6},{6,7},{7,4},{8,9},{9,10},{10,1... | collective-permute-start | bytes 2949128 | tf_op jit(solution)/shard_map/ppermute | solution.py:291
  9.8 24.0 %collective-permute-start.3 = (bf16[20,32,768]{2,1,0:T(8,128)(2,1)S(1)}, bf16[20,32,768]{2,1,0:T(8,128)(2,1)S(1)}, u32[]{:S(2)}, u32[]{:S(2)}) collective-permute-start(bf16[20,32,768]{2,1,0:T(8,128)(2,1)S(1)} %get-tuple-element.61), channel_id=1, source_target_pairs={{0,3},{1,0},{2,1},{3,2},{4,7},{5,4},{6,5},{7,6},{8,11},{9,8},{10,9... | collective-permute-start | bytes 2949128 | tf_op jit(solution)/shard_map/ppermute | solution.py:291
  11.5 16.3 %collective-permute-start.1 = (bf16[2,2,256,256]{3,2,1,0:T(8,128)(2,1)S(1)}, bf16[2,2,256,256]{3,2,1,0:T(8,128)(2,1)S(1)}, u32[]{:S(2)}, u32[]{:S(2)}) collective-permute-start(bf16[2,2,256,256]{3,2,1,0:T(8,128)(2,1)S(1)} %slice_bitcast_fusion.2), channel_id=1, source_target_pairs={{8,0},{16,8},{24,16},{32,24},{40,32},{48,40},{56,48},{72,64},{80,7... | collective-permute-start | bytes 1572872 | tf_op jit(solution)/shard_map/ppermute | solution.py:299
  27.9 14.2 %collective-permute-start.5 = (bf16[2,2,2,256,256]{4,3,2,1,0:T(8,128)(2,1)S(1)}, bf16[2,2,2,256,256]{4,3,2,1,0:T(8,128)(2,1)S(1)}, u32[]{:S(2)}, u32[]{:S(2)}) collective-permute-start(bf16[2,2,2,256,256]{4,3,2,1,0:T(8,128)(2,1)S(1)} %get-tuple-element.66), channel_id=1, source_target_pairs={{64,0},{72,8},{80,16},{88,24},{96,32},{104,40},{112,48},{120,56},{... | collective-permute-start | bytes 3145736 | tf_op jit(solution)/shard_map/ppermute | solution.py:299
  29.9 17.8 %collective-permute-start.4 = (bf16[2,2,256,256]{3,2,1,0:T(8,128)(2,1)S(1)}, bf16[2,2,256,256]{3,2,1,0:T(8,128)(2,1)S(1)}, u32[]{:S(2)}, u32[]{:S(2)}) collective-permute-start(bf16[2,2,256,256]{3,2,1,0:T(8,128)(2,1)S(1)} %get-tuple-element.65), channel_id=1, source_target_pairs={{8,0},{16,8},{24,16},{32,24},{40,32},{48,40},{56,48},{72,64},{80,7... | collective-permute-start | bytes 1572872 | tf_op jit(solution)/shard_map/ppermute | solution.py:299
  31.8 26.5 %collective-permute-start.6 = (bf16[2,2,256,256]{3,2,1,0:T(8,128)(2,1)S(1)}, bf16[2,2,256,256]{3,2,1,0:T(8,128)(2,1)S(1)}, u32[]{:S(2)}, u32[]{:S(2)}) collective-permute-start(bf16[2,2,256,256]{3,2,1,0:T(8,128)(2,1)S(1)} %get-tuple-element.68), channel_id=1, source_target_pairs={{72,0},{80,8},{88,16},{96,24},{104,32},{112,40},{120,48},{136,64},... | collective-permute-start | bytes 1572872 | tf_op jit(solution)/shard_map/ppermute | solution.py:299
  35.1 26.2 %collective-permute-start.7 = (bf16[10,32,768]{2,1,0:T(8,128)(2,1)S(1)}, bf16[10,32,768]{2,1,0:T(8,128)(2,1)S(1)}, u32[]{:S(2)}, u32[]{:S(2)}) collective-permute-start(bf16[10,32,768]{2,1,0:T(8,128)(2,1)S(1)} %get-tuple-element.70), channel_id=1, source_target_pairs={{0,3},{1,0},{2,1},{3,2},{4,7},{5,4},{6,5},{7,6},{8,11},{9,8},{10,9... | collective-permute-start | bytes 1474568 | tf_op jit(solution)/shard_map/ppermute | solution.py:291
  37.2 24.1 %collective-permute-start.8 = (bf16[10,32,768]{2,1,0:T(8,128)(2,1)S(1)}, bf16[10,32,768]{2,1,0:T(8,128)(2,1)S(1)}, u32[]{:S(2)}, u32[]{:S(2)}) collective-permute-start(bf16[10,32,768]{2,1,0:T(8,128)(2,1)S(1)} %get-tuple-element.72), channel_id=1, source_target_pairs={{0,1},{1,2},{2,3},{3,0},{4,5},{5,6},{6,7},{7,4},{8,9},{9,10},{10,1... | collective-permute-start | bytes 1474568 | tf_op jit(solution)/shard_map/ppermute | solution.py:291
  51.9 20.5 %collective-permute-start.9 = (bf16[14,32,768]{2,1,0:T(8,128)(2,1)S(1)}, bf16[14,32,768]{2,1,0:T(8,128)(2,1)S(1)}, u32[]{:S(2)}, u32[]{:S(2)}) collective-permute-start(bf16[14,32,768]{2,1,0:T(8,128)(2,1)S(1)} %get-tuple-element.74), channel_id=1, source_target_pairs={{0,1},{1,2},{2,3},{3,0},{4,5},{5,6},{6,7},{7,4},{8,9},{9,10},{10,1... | collective-permute-start | bytes 2064392 | tf_op jit(solution)/shard_map/ppermute | solution.py:291
  52.7 19.7 %collective-permute-start.10 = (bf16[14,32,768]{2,1,0:T(8,128)(2,1)S(1)}, bf16[14,32,768]{2,1,0:T(8,128)(2,1)S(1)}, u32[]{:S(2)}, u32[]{:S(2)}) collective-permute-start(bf16[14,32,768]{2,1,0:T(8,128)(2,1)S(1)} %get-tuple-element.75), channel_id=1, source_target_pairs={{0,3},{1,0},{2,1},{3,2},{4,7},{5,4},{6,5},{7,6},{8,11},{9,8},{10,9... | collective-permute-start | bytes 2064392 | tf_op jit(solution)/shard_map/ppermute | solution.py:291
  62.3 10.1 %collective-permute-start.11 = (bf16[10,32,768]{2,1,0:T(8,128)(2,1)S(1)}, bf16[10,32,768]{2,1,0:T(8,128)(2,1)S(1)}, u32[]{:S(2)}, u32[]{:S(2)}) collective-permute-start(bf16[10,32,768]{2,1,0:T(8,128)(2,1)S(1)} %get-tuple-element.78), channel_id=1, source_target_pairs={{0,4},{1,5},{2,6},{3,7},{4,0},{5,1},{6,2},{7,3},{8,12},{9,13},{10,... | collective-permute-start | bytes 1474568 | tf_op jit(solution)/shard_map/ppermute | solution.py:288
  63.2 17.0 %collective-permute-start.12 = (bf16[8,32,768]{2,1,0:T(8,128)(2,1)S(1)}, bf16[8,32,768]{2,1,0:T(8,128)(2,1)S(1)}, u32[]{:S(2)}, u32[]{:S(2)}) collective-permute-start(bf16[8,32,768]{2,1,0:T(8,128)(2,1)S(1)} %get-tuple-element.80), channel_id=1, source_target_pairs={{0,1},{1,2},{2,3},{3,0},{4,5},{5,6},{6,7},{7,4},{8,9},{9,10},{10,1... | collective-permute-start | bytes 1179656 | tf_op jit(solution)/shard_map/ppermute | solution.py:291
  64.3 15.9 %collective-permute-start.13 = (bf16[8,32,768]{2,1,0:T(8,128)(2,1)S(1)}, bf16[8,32,768]{2,1,0:T(8,128)(2,1)S(1)}, u32[]{:S(2)}, u32[]{:S(2)}) collective-permute-start(bf16[8,32,768]{2,1,0:T(8,128)(2,1)S(1)} %get-tuple-element.81), channel_id=1, source_target_pairs={{0,3},{1,0},{2,1},{3,2},{4,7},{5,4},{6,5},{7,6},{8,11},{9,8},{10,9... | collective-permute-start | bytes 1179656 | tf_op jit(solution)/shard_map/ppermute | solution.py:291
  73.4 11.9 %collective-permute-start.14 = (bf16[7,32,768]{2,1,0:T(8,128)(2,1)S(1)}, bf16[7,32,768]{2,1,0:T(8,128)(2,1)S(1)}, u32[]{:S(2)}, u32[]{:S(2)}) collective-permute-start(bf16[7,32,768]{2,1,0:T(8,128)(2,1)S(1)} %get-tuple-element.85), channel_id=1, source_target_pairs={{0,3},{1,0},{2,1},{3,2},{4,7},{5,4},{6,5},{7,6},{8,11},{9,8},{10,9... | collective-permute-start | bytes 1032200 | tf_op jit(solution)/shard_map/ppermute | solution.py:291
  76.0 10.0 %collective-permute-start.15 = (bf16[7,32,768]{2,1,0:T(8,128)(2,1)S(1)}, bf16[7,32,768]{2,1,0:T(8,128)(2,1)S(1)}, u32[]{:S(2)}, u32[]{:S(2)}) collective-permute-start(bf16[7,32,768]{2,1,0:T(8,128)(2,1)S(1)} %get-tuple-element.87), channel_id=1, source_target_pairs={{0,1},{1,2},{2,3},{3,0},{4,5},{5,6},{6,7},{7,4},{8,9},{9,10},{10,1... | collective-permute-start | bytes 1032200 | tf_op jit(solution)/shard_map/ppermute | solution.py:291
  86.7 17.0 %collective-permute-start.19 = (bf16[5,32,768]{2,1,0:T(8,128)(2,1)S(1)}, bf16[5,32,768]{2,1,0:T(8,128)(2,1)S(1)}, u32[]{:S(2)}, u32[]{:S(2)}) collective-permute-start(bf16[5,32,768]{2,1,0:T(8,128)(2,1)S(1)} %get-tuple-element.104), channel_id=1, source_target_pairs={{0,4},{1,5},{2,6},{3,7},{4,0},{5,1},{6,2},{7,3},{8,12},{9,13},{10,... | collective-permute-start | bytes 737288 | tf_op jit(solution)/shard_map/ppermute | solution.py:288
  87.6 6.2 %collective-permute-start.16 = (bf16[4,32,768]{2,1,0:T(8,128)(2,1)S(1)}, bf16[4,32,768]{2,1,0:T(8,128)(2,1)S(1)}, u32[]{:S(2)}, u32[]{:S(2)}) collective-permute-start(bf16[4,32,768]{2,1,0:T(8,128)(2,1)S(1)} %get-tuple-element.89), channel_id=1, source_target_pairs={{0,3},{1,0},{2,1},{3,2},{4,7},{5,4},{6,5},{7,6},{8,11},{9,8},{10,9... | collective-permute-start | bytes 589832 | tf_op jit(solution)/shard_map/ppermute | solution.py:291
  90.6 6.9 %collective-permute-start.17 = (bf16[4,32,768]{2,1,0:T(8,128)(2,1)S(1)}, bf16[4,32,768]{2,1,0:T(8,128)(2,1)S(1)}, u32[]{:S(2)}, u32[]{:S(2)}) collective-permute-start(bf16[4,32,768]{2,1,0:T(8,128)(2,1)S(1)} %get-tuple-element.91), channel_id=1, source_target_pairs={{0,1},{1,2},{2,3},{3,0},{4,5},{5,6},{6,7},{7,4},{8,9},{9,10},{10,1... | collective-permute-start | bytes 589832 | tf_op jit(solution)/shard_map/ppermute | solution.py:291
  90.6 9.0 %collective-permute-start.18 = (bf16[2,32,768]{2,1,0:T(8,128)(2,1)S(1)}, bf16[2,32,768]{2,1,0:T(8,128)(2,1)S(1)}, u32[]{:S(2)}, u32[]{:S(2)}) collective-permute-start(bf16[2,32,768]{2,1,0:T(8,128)(2,1)S(1)} %get-tuple-element.96), channel_id=1, source_target_pairs={{0,4},{1,5},{2,6},{3,7},{4,0},{5,1},{6,2},{7,3},{8,12},{9,13},{10,... | collective-permute-start | bytes 294920 | tf_op jit(solution)/shard_map/ppermute | solution.py:288
  97.8 6.0 %collective-permute-start.20 = (bf16[4,32,768]{2,1,0:T(8,128)(2,1)S(1)}, bf16[4,32,768]{2,1,0:T(8,128)(2,1)S(1)}, u32[]{:S(2)}, u32[]{:S(2)}) collective-permute-start(bf16[4,32,768]{2,1,0:T(8,128)(2,1)S(1)} %get-tuple-element.107), channel_id=1, source_target_pairs={{0,4},{1,5},{2,6},{3,7},{4,0},{5,1},{6,2},{7,3},{8,12},{9,13},{10,... | collective-permute-start | bytes 589832 | tf_op jit(solution)/shard_map/ppermute | solution.py:288
  99.6 7.6 %collective-permute-start.21 = (bf16[4,32,768]{2,1,0:T(8,128)(2,1)S(1)}, bf16[4,32,768]{2,1,0:T(8,128)(2,1)S(1)}, u32[]{:S(2)}, u32[]{:S(2)}) collective-permute-start(bf16[4,32,768]{2,1,0:T(8,128)(2,1)S(1)} %get-tuple-element.109), channel_id=1, source_target_pairs={{0,8},{8,16},{16,24},{24,32},{32,40},{40,48},{48,56},{64,72},{72,8... | collective-permute-start | bytes 589832 | tf_op jit(solution)/shard_map/ppermute | solution.py:299
